TPU v7x, 256 devices: a whole 4x4x8 slice. The times are simulated.
256 devices in a mesh: dp: 32 (over y, z), expert: 8 (over x, core).
Axes of the slice: x: 4, y: 4, z: 8, core: 2. Of those that a mesh axis runs over, the one named last changes fastest.
Arguments:
- tokens: bfloat16 [1024, 7168], P(('dp', 'expert')), may hold values from -6 to 6
- grad_out: bfloat16 [1024, 7168], P(('dp', 'expert')), may hold values from -6 to 6
- expert_ids: int32 [1024, 2], P(('dp', 'expert')), may hold values from 0 to 7, all different within a row; in each aligned block of 4 rows (0 to 3, 4 to 7, ...) at most 2 rows name the same one
- gate_values: float32 [1024, 2], P(('dp', 'expert')), may hold values from 0.1 to 1
- gate_master: float32 [8, 2048, 7168], P('expert', 'dp'), as said below
- gate_scale: float32 [8, 2048, 224], P('expert', 'dp'), as said below
- up_master: float32 [8, 2048, 7168], P('expert', 'dp'), as said below
- up_scale: float32 [8, 2048, 224], P('expert', 'dp'), as said below
- down_master: float32 [8, 2048, 7168], P('expert', 'dp'), as said below
- down_scale: float32 [8, 2048, 224], P('expert', 'dp'), as said below
Outputs:
- grad_tokens: bfloat16 [1024, 7168], P(('dp', 'expert'))
- grad_gate_master: float32 [8, 2048, 7168], P('expert', 'dp')
- grad_up_master: float32 [8, 2048, 7168], P('expert', 'dp')
- grad_down_master: float32 [8, 2048, 7168], P('expert', 'dp')
Inputs may be any that keep to these rules, and one draw needn't show every extreme that they name: `expert_ids`: each token names two different experts; among the 4 tokens of one device (an aligned block of rows) no expert is named more than 2 times, a bound that some block reaches. gate_master divided by its group's gate_scale lies within 0.35 of an integer from -9 to 8 in every entry. `gate_scale`: positive scales. up_master divided by its group's up_scale lies within 0.35 of an integer from -9 to 8 in every entry. `up_scale`: positive scales. down_master divided by its group's down_scale lies within 0.35 of an integer from -9 to 8 in every entry. `down_scale`: positive scales.
All inputs are finite; a program needn't handle non-finite values.
Results may differ from a plain program's by a relative error of at most 0.022.
Values may be sent and summed in bfloat16 or wider, within the bound.
No kernel may reach another device: no remote copies, remote signals or barrier semaphores. Data moves between devices by JAX's collectives and lax.ppermute only.
A program may use at most 128 MiB of HBM per device.

v0:
```python
import jax
import jax.numpy as jnp
from jax import lax
from jax.sharding import PartitionSpec as P


def dequantize(master, scales):
    groups = scales.shape[-1]
    scaled = master.reshape(master.shape[0], groups, master.shape[1] // groups) / scales[:, :, None]
    levels = jnp.clip(jnp.floor(scaled + 0.5), -8.0, 7.0)
    weight = (levels * scales[:, :, None]).reshape(master.shape).astype(jnp.bfloat16)
    passed = (
        jnp.where((scaled > -8.5) & (scaled < 7.5), 1.0, 0.0)
        .astype(jnp.float32)
        .reshape(master.shape)
    )
    return (weight, passed)


def rows_backward(rows_x, rows_dz, gate_w, up_w, down_w):
    gate_pre = jnp.dot(rows_x, gate_w.T, preferred_element_type=jnp.float32)
    up_pre = jnp.dot(rows_x, up_w.T, preferred_element_type=jnp.float32)
    sig_gate = jax.nn.sigmoid(gate_pre)
    silu_gate = gate_pre * sig_gate
    hidden = (silu_gate * up_pre).astype(jnp.bfloat16)
    delta_hidden = jnp.dot(rows_dz, down_w.T, preferred_element_type=jnp.float32)
    delta_up = (delta_hidden * silu_gate).astype(jnp.bfloat16)
    delta_gate = (delta_hidden * up_pre * sig_gate * (1.0 + gate_pre * (1.0 - sig_gate))).astype(
        jnp.bfloat16
    )
    grad_gate = jnp.dot(delta_gate.T, rows_x, preferred_element_type=jnp.float32)
    grad_up = jnp.dot(delta_up.T, rows_x, preferred_element_type=jnp.float32)
    grad_down = jnp.dot(hidden.T, rows_dz, preferred_element_type=jnp.float32)
    return (delta_gate, delta_up, grad_gate, grad_up, grad_down)


def per_device(
    tokens,
    grad_out,
    expert_ids,
    gate_values,
    gate_master,
    gate_scale,
    up_master,
    up_scale,
    down_master,
    down_scale,
):
    experts_here = lax.axis_size("expert")
    tok_count = tokens.shape[0]
    capacity = tok_count // 2
    width = tokens.shape[1]
    flat_ids = expert_ids.reshape(-1)
    onehot = (flat_ids[:, None] == jnp.arange(experts_here, dtype=jnp.int32)[None, :]).astype(
        jnp.int32
    )
    earlier = jnp.cumsum(onehot, axis=0) - onehot
    position = jnp.sum(earlier * onehot, axis=1)
    slot_index = flat_ids * capacity + position
    placing = (
        slot_index[None, :] == jnp.arange(experts_here * capacity, dtype=jnp.int32)[:, None]
    ).astype(jnp.bfloat16)
    token_rows = jnp.repeat(tokens, 2, axis=0)
    scaled_grad = (
        gate_values.reshape(-1)[:, None] * jnp.repeat(grad_out, 2, axis=0).astype(jnp.float32)
    ).astype(jnp.bfloat16)
    send_x = (
        jnp.dot(placing, token_rows, preferred_element_type=jnp.float32)
        .astype(jnp.bfloat16)
        .reshape(experts_here, capacity, width)
    )
    send_dz = (
        jnp.dot(placing, scaled_grad, preferred_element_type=jnp.float32)
        .astype(jnp.bfloat16)
        .reshape(experts_here, capacity, width)
    )
    recv_x, recv_dz = (
        lax.all_to_all(send_x, "expert", split_axis=0, concat_axis=0, tiled=True),
        lax.all_to_all(send_dz, "expert", split_axis=0, concat_axis=0, tiled=True),
    )
    local_x = recv_x.reshape(-1, width)
    local_dz = recv_dz.reshape(-1, width)
    gate_w, gate_keep = dequantize(gate_master[0], gate_scale[0])
    up_w, up_keep = dequantize(up_master[0], up_scale[0])
    down_w, down_keep = dequantize(down_master[0], down_scale[0])
    all_x, all_dz = (
        lax.all_gather(local_x, "dp", axis=0, tiled=True),
        lax.all_gather(local_dz, "dp", axis=0, tiled=True),
    )
    delta_gate, delta_up, grad_gate, grad_up, grad_down = rows_backward(
        all_x, all_dz, gate_w, up_w, down_w
    )
    partial_value = jnp.dot(delta_gate, gate_w, preferred_element_type=jnp.float32) + jnp.dot(
        delta_up, up_w, preferred_element_type=jnp.float32
    )
    grad_rows = lax.psum_scatter(
        partial_value.astype(jnp.bfloat16), "dp", scatter_dimension=0, tiled=True
    )
    returned = lax.all_to_all(
        grad_rows.reshape(experts_here, capacity, width),
        "expert",
        split_axis=0,
        concat_axis=0,
        tiled=True,
    )
    per_assign = jnp.dot(placing.T, returned.reshape(-1, width), preferred_element_type=jnp.float32)
    grad_tokens = jnp.sum(per_assign.reshape(tok_count, 2, width), axis=1).astype(jnp.bfloat16)
    return (
        grad_tokens,
        (grad_gate * gate_keep)[None],
        (grad_up * up_keep)[None],
        (grad_down * down_keep)[None],
    )


def solution(mesh):
    return jax.shard_map(
        per_device,
        mesh=mesh,
        in_specs=(
            P(("dp", "expert"), None),
            P(("dp", "expert"), None),
            P(("dp", "expert"), None),
            P(("dp", "expert"), None),
            P("expert", "dp", None),
            P("expert", "dp", None),
            P("expert", "dp", None),
            P("expert", "dp", None),
            P("expert", "dp", None),
            P("expert", "dp", None),
        ),
        out_specs=(
            P(("dp", "expert"), None),
            P("expert", "dp", None),
            P("expert", "dp", None),
            P("expert", "dp", None),
        ),
        check_vma=False,
    )
```

profile of v0, /device:TPU:2, one launch (start us, length us, event | category | flops | bytes accessed | tf_op | source)
XLA Modules:
  0.0 467.6 jit_solution(14260764418641085862)
XLA Ops:
  9.6 10.4 %all_to_all.15 = bf16[8,2,7168]{2,1,0:T(2,128)(2,1)S(1)} all-to-all(bf16[8,2,7168]{2,1,0:T(2,128)(2,1)S(1)} %reshape.91), channel_id=1, replica_groups=mesh['dp'=32,'expert'=8] {'expert'}, dimensions={0} | all-to-all | bytes 458752 | tf_op jit(solution)/shard_map/all_to_all | solution.py:78
  21.7 9.6 %all_to_all.16 = bf16[8,2,7168]{2,1,0:T(2,128)(2,1)S(1)} all-to-all(bf16[8,2,7168]{2,1,0:T(2,128)(2,1)S(1)} %reshape.88), channel_id=1, replica_groups=mesh['dp'=32,'expert'=8] {'expert'}, dimensions={0} | all-to-all | bytes 458752 | tf_op jit(solution)/shard_map/all_to_all | solution.py:79
  32.4 2.0 div.46
  34.5 3.6 copy.36
  38.1 2.0 div.50
  40.1 3.5 copy.39
  43.6 2.0 div.54
  45.7 2.8 copy.42
  48.5 2.7 multiply_convert_fusion.1
  51.2 1.4 multiply_convert_fusion
  52.6 63.7 %all-gather.5.cloned.1.call-done = bf16[512,7168]{1,0:T(8,128)(2,1)} async-done(((bf16[16,7168]{1,0:T(8,128)(2,1)}), bf16[512,7168]{1,0:T(8,128)(2,1)}) %all-gather.5.cloned.1.call-update) | async-done | bytes 7340048 | tf_op jit(solution)/shard_map/all_gather | solution.py:87
  116.3 5.6 %fusion.20 = f32[512,64]{0,1:T(8,128)S(1)} fusion(bf16[512,7168]{1,0:T(8,128)(2,1)} %all-gather.5.cloned.1.call-done, bf16[64,7168]{1,0:T(8,128)(2,1)S(1)} %multiply_convert_fusion.1), kind=kOutput, calls=%fused_computation.42 | convolution fusion | flops 469762048 | bytes 8388608 | tf_op jit(solution)/shard_map/dot_general | solution.py:22
  121.9 2.3 fusion.21
  124.2 85.1 %all-gather.3.cloned.1.call-done = bf16[512,7168]{1,0:T(8,128)(2,1)} async-done(((bf16[16,7168]{1,0:T(8,128)(2,1)}), bf16[512,7168]{1,0:T(8,128)(2,1)}) %all-gather.3.cloned.1.call-update) | async-done | bytes 7340048 | tf_op jit(solution)/shard_map/all_gather | solution.py:88
  209.3 6.6 %multiply_convert_fusion.6 = (bf16[512,64]{0,1:T(8,128)(2,1)S(1)}, bf16[512,64]{0,1:T(8,128)(2,1)S(1)}) fusion(f32[512,64]{0,1:T(8,128)S(1)} %fusion.21, f32[512,64]{0,1:T(8,128)S(1)} %fusion.20, bf16[512,7168]{1,0:T(8,128)(2,1)} %all-gather.3.cloned.1.call-done, f32[64,7168]{1,0:T(8,128)} %copy.36, f32[1,64,7168]{2,1,0:T(8,128)} %param.18), kind=kOutput, calls=%fused_computation.22 | convolution fusion | flops 472940544 | bytes 11403264 | tf_op jit(solution)/shard_map/dot_general | solution.py:26
  215.9 2.1 fusion.22
  218.0 5.0 %add_convert_fusion = bf16[512,7168]{1,0:T(8,128)(2,1)} fusion(f32[512,7168]{1,0:T(8,128)S(1)} %fusion.22, bf16[512,64]{0,1:T(8,128)(2,1)S(1)} %get-tuple-element.4, bf16[64,7168]{1,0:T(8,128)(2,1)S(1)} %multiply_convert_fusion.1), kind=kOutput, calls=%fused_computation | convolution fusion | flops 477102080 | bytes 23003136 | tf_op jit(solution)/shard_map/dot_general | solution.py:93
  223.2 7.1 %fusion.1 = f32[1,64,7168]{2,1,0:T(8,128)} fusion(bf16[512,64]{0,1:T(8,128)(2,1)S(1)} %get-tuple-element.4, bf16[512,7168]{1,0:T(8,128)(2,1)} %all-gather.5.cloned.1.call-done, f32[64,7168]{1,0:T(8,128)} %copy.39, f32[1,64,7168]{2,1,0:T(8,128)} %param.16), kind=kOutput, calls=%fused_computation.4 | convolution fusion | flops 472514560 | bytes 12910592 | tf_op jit(solution)/shard_map/dot_general | solution.py:32
  230.3 6.1 %fusion = f32[1,64,7168]{2,1,0:T(8,128)} fusion(bf16[512,7168]{1,0:T(8,128)(2,1)} %all-gather.3.cloned.1.call-done, f32[64,7168]{1,0:T(8,128)S(1)} %copy-done.4, f32[1,64,7168]{2,1,0:T(8,128)S(1)} %copy-done.10, f32[512,64]{0,1:T(8,128)S(1)} %fusion.20, f32[512,64]{0,1:T(8,128)S(1)} %fusion.21), kind=kOutput, calls=%fused_computation.2 | convolution fusion | flops 472711168 | bytes 13107200 | tf_op jit(solution)/shard_map/dot_general | solution.py:33
  236.4 210.8 %reduce-scatter.2.cloned.1.call-done = bf16[16,7168]{1,0:T(8,128)(2,1)} async-done(((bf16[512,7168]{1,0:T(8,128)(2,1)}), bf16[16,7168]{1,0:T(8,128)(2,1)}) %reduce-scatter.2.cloned.1.call-update) | async-done | bytes 229392 | tf_op jit(solution)/shard_map/reduce_scatter | solution.py:96
  447.2 1.7 reshape.93
  448.9 4.8 %all-to-all-start.2 = ((bf16[8,2,7168]{2,1,0:T(2,128)(2,1)}), bf16[8,2,7168]{2,1,0:T(2,128)(2,1)S(1)}, u32[]{:S(2)}, u32[]{:S(2)}) async-start(bf16[8,2,7168]{2,1,0:T(2,128)(2,1)} %reshape.93), calls=%async_computation.3 | async-start | bytes 458752 | tf_op jit(solution)/shard_map/all_to_all | solution.py:99
  453.7 6.4 %fusion.2 = f32[1,64,7168]{2,1,0:T(8,128)} fusion(bf16[512,64]{0,1:T(8,128)(2,1)S(1)} %get-tuple-element.5, bf16[512,7168]{1,0:T(8,128)(2,1)} %all-gather.5.cloned.1.call-done, f32[64,7168]{1,0:T(8,128)S(1)} %copy.42, f32[1,64,7168]{2,1,0:T(8,128)} %param.14), kind=kOutput, calls=%fused_computation.6 | convolution fusion | flops 472514560 | bytes 12910592 | tf_op jit(solution)/shard_map/dot_general | solution.py:31
  460.2 0.9 convolution_reduce_fusion
  (54 shorter events, 5.4 us)
Async XLA Ops:
  7.2 13.7 %copy-start.9 = (f32[4,2]{0,1:T(2,128)S(1)}, f32[4,2]{0,1:T(2,128)}, u32[]{:S(2)}) copy-start(f32[4,2]{0,1:T(2,128)} %param.13) | copy-start | bytes 100
  7.2 13.9 %copy-start.8 = (bf16[4,7168]{1,0:T(4,128)(2,1)S(1)}, bf16[4,7168]{1,0:T(4,128)(2,1)}, u32[]{:S(2)}) copy-start(bf16[4,7168]{1,0:T(4,128)(2,1)} %param.11) | copy-start | bytes 172036
  7.2 109.1 %all-gather.5.cloned.1.call-start = ((), (), s32[]{:S(2)}) async-start(), calls=%async_computation.5 | async-start | bytes 7569408 | tf_op jit(solution)/shard_map/all_gather | solution.py:87
  20.0 12.1 %copy-start.5 = (f32[1,64,224]{2,1,0:T(8,128)S(1)}, f32[1,64,224]{2,1,0:T(8,128)}, u32[]{:S(2)}) copy-start(f32[1,64,224]{2,1,0:T(8,128)} %param.15) | copy-start | bytes 172036
  20.0 12.2 %copy-start.6 = (f32[1,64,224]{2,1,0:T(8,128)S(1)}, f32[1,64,224]{2,1,0:T(8,128)}, u32[]{:S(2)}) copy-start(f32[1,64,224]{2,1,0:T(8,128)} %param.17) | copy-start | bytes 172036
  20.0 12.3 %copy-start.7 = (f32[1,64,224]{2,1,0:T(8,128)S(1)}, f32[1,64,224]{2,1,0:T(8,128)}, u32[]{:S(2)}) copy-start(f32[1,64,224]{2,1,0:T(8,128)} %param.19) | copy-start | bytes 172036
  20.8 188.5 %all-gather.3.cloned.1.call-start = ((), (), s32[]{:S(2)}) async-start(), calls=%async_computation.4 | async-start | bytes 7569408 | tf_op jit(solution)/shard_map/all_gather | solution.py:88
  32.0 415.2 %reduce-scatter.2.cloned.1.call-start = ((), (), s32[]{:S(2)}) async-start(), calls=%async_computation.6 | async-start | bytes 7569408 | tf_op jit(solution)/shard_map/reduce_scatter | solution.py:96
  48.5 2.7 copy-start.3
  116.3 5.6 %copy-start = (bf16[512,7168]{1,0:T(8,128)(2,1)S(1)}, bf16[512,7168]{1,0:T(8,128)(2,1)}, u32[]{:S(2)}) copy-start(bf16[512,7168]{1,0:T(8,128)(2,1)} %all-gather.5.cloned.1.call-done) | copy-start | bytes 22020100
  116.3 5.6 %copy-start.1 = (bf16[64,7168]{1,0:T(8,128)(2,1)S(1)}, bf16[64,7168]{1,0:T(8,128)(2,1)}, u32[]{:S(2)}) copy-start(bf16[64,7168]{1,0:T(8,128)(2,1)} %multiply_convert_fusion) | copy-start | bytes 2752516
  209.3 6.6 %copy-start.2 = (bf16[64,7168]{1,0:T(8,128)(2,1)S(1)}, bf16[64,7168]{1,0:T(8,128)(2,1)}, u32[]{:S(2)}) copy-start(bf16[64,7168]{1,0:T(8,128)(2,1)} %multiply_convert_fusion) | copy-start | bytes 2752516
  223.2 7.1 %copy-start.4 = (f32[64,7168]{1,0:T(8,128)S(1)}, f32[64,7168]{1,0:T(8,128)}, u32[]{:S(2)}) copy-start(f32[64,7168]{1,0:T(8,128)} %copy.36) | copy-start | bytes 5505028
  223.2 7.1 %copy-start.10 = (f32[1,64,7168]{2,1,0:T(8,128)S(1)}, f32[1,64,7168]{2,1,0:T(8,128)}, u32[]{:S(2)}) copy-start(f32[1,64,7168]{2,1,0:T(8,128)} %param.18) | copy-start | bytes 5505028
  448.9 11.2 %all-to-all-start.2 = ((bf16[8,2,7168]{2,1,0:T(2,128)(2,1)}), bf16[8,2,7168]{2,1,0:T(2,128)(2,1)S(1)}, u32[]{:S(2)}, u32[]{:S(2)}) async-start(bf16[8,2,7168]{2,1,0:T(2,128)(2,1)} %reshape.93), calls=%async_computation.3 | async-start | bytes 458752 | tf_op jit(solution)/shard_map/all_to_all | solution.py:99
Sparse Core Ops, SparseCore 0:
  20.9 95.2 all-gather.4
  118.9 90.3 all-gather.2
  223.2 224.0 reduce-scatter.1
where the time goes:
time: 469 us; the launch traced here: 468 us
  waiting for transfers between devices  360 us (77%)
  matrix products  42.5 us (9%)
  local copies, waits for them, and re-layouts  22.2 us (5%)
  blocking collectives  20 us (4%)
  between operations  13.9 us (3%)
  starting transfers between devices  4.93 us (1%)
    reduce_scatter x1, waiting for transfers between devices, per_device(): lax.psum_scatter(partial_value.astype(jnp.bfloat16), 'dp', scatter_dimens...  211 us
    all_gather x1, waiting for transfers between devices, per_device(): lax.all_gather(local_dz, 'dp', axis=0, tiled=True)  85.1 us
    all_gather x1, waiting for transfers between devices, per_device(): lax.all_gather(local_x, 'dp', axis=0, tiled=True)  63.7 us
    div x9, local copies, waits for them, and re-layouts, dequantize(): master.reshape(master.shape[0], groups, master.shape[1] // groups)  16.3 us
    all_to_all x1, blocking collectives, per_device(): lax.all_to_all(send_x, 'expert', split_axis=0, concat_axis=0, tiled=True)  10.4 us
    all_to_all x1, blocking collectives, per_device(): lax.all_to_all(send_dz, 'expert', split_axis=0, concat_axis=0, tiled=True)  9.59 us
  transfers between devices with their start and end apart: 4, of which 3 were waited for; matrix products, arithmetic and copies ran while one was open for 11% of the time, Pallas kernels for 0%

commit v1 on v0

v1 whole, which is shorter than its diff:
```python
import jax
import jax.numpy as jnp
from jax import lax
from jax.sharding import PartitionSpec as P

NX = 4
X_GROUPS = [[0, 2, 4, 6], [1, 3, 5, 7]]
CORE_SWAP = [(i, i ^ 1) for i in range(8)]
BF = jnp.bfloat16
F32 = jnp.float32


def dequantize(master, scales):
    groups = scales.shape[-1]
    scaled = master.reshape(master.shape[0], groups, master.shape[1] // groups) / scales[:, :, None]
    levels = jnp.clip(jnp.floor(scaled + 0.5), -8.0, 7.0)
    weight = (levels * scales[:, :, None]).reshape(master.shape).astype(BF)
    passed = ((scaled > -8.5) & (scaled < 7.5)).reshape(master.shape)
    return (weight, passed)


def across_x(a):
    return lax.all_to_all(a, "expert", 0, 0, axis_index_groups=X_GROUPS, tiled=True)


def to_slices(a):
    return a.reshape(a.shape[0], NX, -1).transpose(1, 0, 2)


def from_slices(a):
    return a.transpose(1, 0, 2).reshape(a.shape[1], -1)


def nt(a, b):
    return lax.dot_general(a, b, (((1,), (1,)), ((), ())), preferred_element_type=F32)


def tn(a, b):
    return lax.dot_general(a, b, (((0,), (0,)), ((), ())), preferred_element_type=F32)


def per_device(
    tokens,
    grad_out,
    expert_ids,
    gate_values,
    gate_master,
    gate_scale,
    up_master,
    up_scale,
    down_master,
    down_scale,
):
    experts = lax.axis_size("expert")
    expert = lax.axis_index("expert")
    n_dp = lax.axis_size("dp")
    toks, width = tokens.shape
    hid = gate_master.shape[1]
    part = width // NX
    factor = jnp.sum(
        jnp.where(
            expert_ids[:, :, None] == jnp.arange(experts, dtype=jnp.int32), gate_values[:, :, None], 0.0
        ),
        axis=1,
    )
    f_hi = lax.reduce_precision(factor, 8, 7)
    f_mid = lax.reduce_precision(factor - f_hi, 8, 7)
    f_lo = factor - f_hi - f_mid
    f_cols = jnp.concatenate([f_hi, f_mid, f_lo], axis=1).astype(BF)
    f_cols = jnp.pad(f_cols, ((0, 0), (0, 128 - f_cols.shape[1])))
    payload = jnp.concatenate(
        [to_slices(tokens), to_slices(grad_out), jnp.broadcast_to(f_cols, (NX,) + f_cols.shape)], axis=2
    )
    mine = across_x(payload).reshape(NX * toks, -1)
    own = lax.all_gather(mine, "dp", axis=0, tiled=True)
    other = lax.ppermute(own, "expert", CORE_SWAP)
    halves = (own, other)
    half = own.shape[0]

    gate_w, gate_keep = dequantize(gate_master[0], gate_scale[0])
    up_w, up_keep = dequantize(up_master[0], up_scale[0])
    down_w, down_keep = dequantize(down_master[0], down_scale[0])
    w_all = across_x(to_slices(jnp.concatenate([gate_w, up_w, down_w], axis=0)))
    w_gu = w_all[:, : 2 * hid].reshape(NX * 2 * hid, part)
    w_d = w_all[:, 2 * hid :].reshape(NX * hid, part)

    pre_gu = jnp.concatenate([nt(w_gu, h[:, :part]) for h in halves], axis=1)
    pre_d = jnp.concatenate([nt(w_d, h[:, part : 2 * part]) for h in halves], axis=1)
    pre = jnp.concatenate(
        [pre_gu.reshape(NX, 2 * hid, 2 * half), pre_d.reshape(NX, hid, 2 * half)], axis=1
    ).astype(BF)
    pre = jnp.sum(across_x(pre).astype(F32), axis=0)
    picks = jnp.arange(128, dtype=jnp.int32)
    picks = ((picks % experts == expert) & (picks < 3 * experts)).astype(BF)
    weight = jnp.concatenate([nt(picks[None, :], h[:, 2 * part :]) for h in halves], axis=1)

    gate_pre, up_pre = pre[:hid], pre[hid : 2 * hid]
    delta_hidden = jnp.where(weight > 0.0, pre[2 * hid :] * weight, 0.0)
    sig_gate = jax.nn.sigmoid(gate_pre)
    silu_gate = gate_pre * sig_gate
    hidden = jnp.where(weight > 0.0, silu_gate * up_pre * weight, 0.0)
    delta_up = delta_hidden * silu_gate
    delta_gate = delta_hidden * up_pre * sig_gate * (1.0 + gate_pre * (1.0 - sig_gate))
    delta = jnp.concatenate([delta_gate, delta_up, hidden], axis=0).astype(BF)
    delta = lax.all_gather(delta, "expert", axis=0, axis_index_groups=X_GROUPS)
    d_gu = delta[:, : 2 * hid].reshape(NX * 2 * hid, 2 * half)
    d_h = delta[:, 2 * hid :].reshape(NX * hid, 2 * half)

    theirs = lax.ppermute(tn(d_gu[:, half:], w_gu).astype(BF), "expert", CORE_SWAP)
    grad_x = (tn(d_gu[:, :half], w_gu) + theirs.astype(F32)).astype(BF)
    grad_x = lax.all_to_all(grad_x.reshape(n_dp, NX * toks, part), "dp", 0, 0, tiled=True)
    grad_x = jnp.sum(grad_x.astype(F32), axis=0).astype(BF)
    grad_tokens = from_slices(across_x(grad_x.reshape(NX, toks, part)))

    g_gu = sum(
        jnp.dot(d_gu[:, i * half : (i + 1) * half], h[:, :part], preferred_element_type=F32)
        for i, h in enumerate(halves)
    )
    g_d = sum(
        jnp.dot(d_h[:, i * half : (i + 1) * half], h[:, part : 2 * part], preferred_element_type=F32)
        for i, h in enumerate(halves)
    )
    g_all = jnp.concatenate([g_gu.reshape(NX, 2 * hid, part), g_d.reshape(NX, hid, part)], axis=1)
    g_all = from_slices(across_x(g_all.astype(BF))).astype(F32)
    return (
        grad_tokens,
        jnp.where(gate_keep, g_all[:hid], 0.0)[None],
        jnp.where(up_keep, g_all[hid : 2 * hid], 0.0)[None],
        jnp.where(down_keep, g_all[2 * hid :], 0.0)[None],
    )


def solution(mesh):
    rows = P(("dp", "expert"), None)
    weights = P("expert", "dp", None)
    return jax.shard_map(
        per_device,
        mesh=mesh,
        in_specs=(rows,) * 4 + (weights,) * 6,
        out_specs=(rows,) + (weights,) * 3,
        check_vma=False,
    )
```

time: 469 us -> 372 us (0.79)
  waiting for transfers between devices: 360 us -> 176 us
  local copies, waits for them, and re-layouts: 22.2 us -> 54.4 us
  other arithmetic: 4.37 us -> 34.7 us
  blocking collectives: 20 us -> 44.5 us
  matrix products: 42.5 us -> 22.3 us
  starting transfers between devices: 4.93 us -> 24.9 us
    reduce_scatter x1 -> x0, waiting for transfers between devices: 211 us -> none  [per_device(): lax.psum_scatter(partial_value.astype(jnp.bfloat16), 'dp', scatter_dimens...]
    all_to_all x1 -> x4, waiting for transfers between devices: 0.01 us -> 84.8 us  [the longest x3 43.1 us: across_x(): lax.all_to_all(a, 'expert', 0, 0, axis_index_groups=X_GROUPS, tiled=True)]
    all_gather x2, waiting for transfers between devices: 149 us -> 91.3 us  [the longest x1 67.1 us: per_device(): own = lax.all_gather(mine, 'dp', axis=0, tiled=True)]
    unnamed x24 -> x44, local copies, waits for them, and re-layouts: 0.9 us -> 29 us
    all_to_all x2, blocking collectives: 20 us -> 44.5 us  [across_x(): lax.all_to_all(a, 'expert', 0, 0, axis_index_groups=X_GROUPS, tiled=True)]
    dot_general x11 -> x12, matrix products: 42.5 us -> 22.3 us  [the longest x6 8.71 us: nt(): lax.dot_general(a, b, (((1,), (1,)), ((), ())), preferred_element_type=F32)]
    all_to_all x1 -> x4, starting transfers between devices: 4.81 us -> 24.9 us  [the longest x3 14.9 us: across_x(): lax.all_to_all(a, 'expert', 0, 0, axis_index_groups=X_GROUPS, tiled=True)]
    slice x0 -> x9, local copies, waits for them, and re-layouts: none -> 17.2 us  [the longest x2 7.34 us: per_device(): g_all[2 * hid:]]
  transfers between devices with their start and end apart: 4 -> 8, of which waited for: 3 -> 5; matrix products, arithmetic and copies ran while one was open for 11% -> 23% of each run, Pallas kernels for 0% -> 0%
where the time goes in v1:
time: 372 us; the launch traced here: 371 us
  waiting for transfers between devices  176 us (47%)
  local copies, waits for them, and re-layouts  54.4 us (15%)
  blocking collectives  44.5 us (12%)
  other arithmetic  34.7 us (9%)
  starting transfers between devices  24.9 us (7%)
  matrix products  22.3 us (6%)
  between operations  14.4 us (4%)
    all_gather x1, waiting for transfers between devices, per_device(): own = lax.all_gather(mine, 'dp', axis=0, tiled=True)  67.1 us
    all_to_all x2, blocking collectives, across_x(): lax.all_to_all(a, 'expert', 0, 0, axis_index_groups=X_GROUPS, tiled=True)  44.5 us
    all_to_all x3, waiting for transfers between devices, across_x(): lax.all_to_all(a, 'expert', 0, 0, axis_index_groups=X_GROUPS, tiled=True)  43.1 us
    all_to_all x1, waiting for transfers between devices, per_device(): lax.all_to_all(grad_x.reshape(n_dp, NX * toks, part), 'dp', 0, 0, tiled=T...  41.7 us
    unnamed x44, local copies, waits for them, and re-layouts  29 us
    all_gather x1, waiting for transfers between devices, per_device(): delta = lax.all_gather(delta, 'expert', axis=0, axis_index_groups=X_GROUPS)  24.1 us
    all_to_all x3, starting transfers between devices, across_x(): lax.all_to_all(a, 'expert', 0, 0, axis_index_groups=X_GROUPS, tiled=True)  14.9 us
    all_to_all x1, starting transfers between devices, per_device(): lax.all_to_all(grad_x.reshape(n_dp, NX * toks, part), 'dp', 0, 0, tiled=T...  9.97 us
  transfers between devices with their start and end apart: 8, of which 5 were waited for; matrix products, arithmetic and copies ran while one was open for 23% of the time, Pallas kernels for 0%

profile of v1, /device:TPU:2, one launch (start us, length us, event | category | flops | bytes accessed | tf_op | source)
XLA Modules:
  0.0 371.3 jit_solution(11115530982347535969)
XLA Ops:
  9.1 9.1 %all_to_all.30 = bf16[4,4,3712]{2,1,0:T(4,128)(2,1)S(1)} all-to-all(bf16[4,4,3712]{2,1,0:T(4,128)(2,1)S(1)} %pad_maximum_fusion.5), channel_id=1, replica_groups={{0,2,4,6},{1,3,5,7},{8,10,12,14},{9,11,13,15},{16,18,20,22},{17,19,21,2..., dimensions={0} | all-to-all | bytes 237568 | tf_op jit(solution)/shard_map/all_to_all | solution.py:23
  18.9 3.6 copy.71
  25.2 3.6 copy.69
  35.2 67.1 %all-gather.3.cloned.1.call-done = bf16[512,3712]{1,0:T(8,128)(2,1)} async-done(((bf16[16,3712]{1,0:T(8,128)(2,1)}), bf16[512,3712]{1,0:T(8,128)(2,1)}) %all-gather.3.cloned.1.call-update) | async-done | bytes 3801104 | tf_op jit(solution)/shard_map/all_gather | solution.py:75
  108.9 4.4 %copy.73 = bf16[4,192,1792]{2,1,0:T(8,128)(2,1)S(1)} copy(bf16[4,192,1792]{1,2,0:T(8,128)(2,1)} %maximum_bitcast_fusion) | data formatting | bytes 5505024 | tf_op jit(solution)/shard_map/transpose | solution.py:27
  113.3 35.4 %all_to_all.31 = bf16[4,192,1792]{2,1,0:T(8,128)(2,1)S(1)} all-to-all(bf16[4,192,1792]{2,1,0:T(8,128)(2,1)S(1)} %copy.73), channel_id=1, replica_groups={{0,2,4,6},{1,3,5,7},{8,10,12,14},{9,11,13,15},{16,18,20,22},{17,19,21,2..., dimensions={0} | all-to-all | bytes 5505024 | tf_op jit(solution)/shard_map/all_to_all | solution.py:23
  160.1 5.0 %all-to-all-start.2 = ((bf16[4,192,1024]{2,1,0:T(8,128)(2,1)}), bf16[4,192,1024]{2,1,0:T(8,128)(2,1)S(1)}, u32[]{:S(2)}, u32[]{:S(2)}) async-start(bf16[4,192,1024]{2,1,0:T(8,128)(2,1)} %pad_maximum_fusion.1), calls=%async_computation.2 | async-start | bytes 3145728 | tf_op jit(solution)/shard_map/all_to_all | solution.py:23
  167.2 14.8 %all-to-all-done.2 = bf16[4,192,1024]{2,1,0:T(8,128)(2,1)S(1)} async-done(((bf16[4,192,1024]{2,1,0:T(8,128)(2,1)}), bf16[4,192,1024]{2,1,0:T(8,128)(2,1)S(1)}, u32[]{:S(2)}, u32[]{:S(2)}) %all-to-all-start.2) | async-done | bytes 1572896 | tf_op jit(solution)/shard_map/all_to_all | solution.py:23
  184.7 24.1 %all-gather.5.cloned.1.call-done = bf16[4,192,1024]{2,1,0:T(8,128)(2,1)} async-done(((bf16[1,192,1024]{2,1,0:T(8,128)(2,1)}), bf16[4,192,1024]{2,1,0:T(8,128)(2,1)}) %all-gather.5.cloned.1.call-update) | async-done | bytes 1572880 | tf_op jit(solution)/shard_map/all_gather | solution.py:105
  222.1 5.2 %all-to-all-start.5 = ((bf16[4,192,1792]{2,1,0:T(8,128)(2,1)}), bf16[4,192,1792]{2,1,0:T(8,128)(2,1)S(1)}, u32[]{:S(2)}, u32[]{:S(2)}) async-start(bf16[4,192,1792]{2,1,0:T(8,128)(2,1)} %pad_maximum_fusion), calls=%async_computation.5 | async-start | bytes 5505024 | tf_op jit(solution)/shard_map/all_to_all | solution.py:23
  227.3 4.6 %add_convert_fusion.1 = bf16[512,1792]{1,0:T(8,128)(2,1)} fusion(bf16[512,1792]{1,0:T(8,128)(2,1)} %collective-permute-done.1, bf16[512,1792]{1,0:T(8,128)(2,1)} %bitcast.144, bf16[512,1024]{1,0:T(8,128)(2,1)} %bitcast.136), kind=kOutput, calls=%fused_computation.24 | convolution fusion | flops 942276608 | bytes 6029312 | tf_op jit(solution)/shard_map/dot_general | solution.py:39
  231.9 28.3 %all-to-all-done.5 = bf16[4,192,1792]{2,1,0:T(8,128)(2,1)S(1)} async-done(((bf16[4,192,1792]{2,1,0:T(8,128)(2,1)}), bf16[4,192,1792]{2,1,0:T(8,128)(2,1)S(1)}, u32[]{:S(2)}, u32[]{:S(2)}) %all-to-all-start.5) | async-done | bytes 2752544 | tf_op jit(solution)/shard_map/all_to_all | solution.py:23
  260.1 10.0 %all-to-all-start.3 = ((bf16[32,16,1792]{2,1,0:T(8,128)(2,1)}), bf16[32,16,1792]{2,1,0:T(8,128)(2,1)}, u32[]{:S(2)}, u32[]{:S(2)}) async-start(bf16[32,16,1792]{2,1,0:T(8,128)(2,1)} %bitcast.146), calls=%async_computation.3 | async-start | bytes 3670016 | tf_op jit(solution)/shard_map/all_to_all | solution.py:111
  273.0 41.7 %all-to-all-done.3 = bf16[32,16,1792]{2,1,0:T(8,128)(2,1)} async-done(((bf16[32,16,1792]{2,1,0:T(8,128)(2,1)}), bf16[32,16,1792]{2,1,0:T(8,128)(2,1)}, u32[]{:S(2)}, u32[]{:S(2)}) %all-to-all-start.3) | async-done | bytes 1835040 | tf_op jit(solution)/shard_map/all_to_all | solution.py:111
  317.1 4.7 %all-to-all-start.4 = ((bf16[4,4,1792]{2,1,0:T(4,128)(2,1)}), bf16[4,4,1792]{2,1,0:T(4,128)(2,1)S(1)}, u32[]{:S(2)}, u32[]{:S(2)}) async-start(bf16[4,4,1792]{2,1,0:T(4,128)(2,1)} %reshape.179), calls=%async_computation.4 | async-start | bytes 114688 | tf_op jit(solution)/shard_map/all_to_all | solution.py:23
  321.8 4.9 %fusion.72 = (f32[64,4,1792]{2,0,1:T(8,128)S(1)}, f32[64,4,1792]{2,0,1:T(8,128)}, f32[64,4,1792]{2,0,1:T(8,128)}) fusion(f32[192,4,1792]{2,0,1:T(8,128)} %convert_bitcast_fusion), kind=kLoop, calls=%fused_computation.103 | loop fusion | bytes 11010048 | tf_op jit(solution)/shard_map/slice | solution.py:129
  326.7 3.5 copy.78
  330.2 5.6 %bitcast_select_fusion.2 = f32[64,7168]{0,1:T(8,128)} fusion(f32[64,4,1792]{0,2,1:T(8,128)} %copy.78, f32[1,64,7168]{1,2,0:T(8,128)} %copy.67, f32[64,224]{0,1:T(8,128)S(1)} %copy-done.13), kind=kLoop, calls=%fused_computation.21 | loop fusion | flops 2293760 | bytes 5562368 | tf_op jit(solution)/shard_map/jit(_where)/select_n | solution.py:127
  335.8 3.5 copy.83
  339.3 3.5 copy.80
  342.9 5.7 %bitcast_select_fusion.1 = f32[64,7168]{0,1:T(8,128)} fusion(f32[64,4,1792]{0,2,1:T(8,128)} %copy.80, f32[1,64,7168]{1,2,0:T(8,128)} %copy.69, f32[64,224]{0,1:T(8,128)S(1)} %copy-done.11), kind=kLoop, calls=%fused_computation.19 | loop fusion | flops 2293760 | bytes 5562368 | tf_op jit(solution)/shard_map/jit(_where)/select_n | solution.py:128
  348.6 3.5 copy.84
  354.6 5.7 %bitcast_select_fusion = f32[64,7168]{0,1:T(8,128)} fusion(f32[64,4,1792]{0,2,1:T(8,128)} %copy.82, f32[1,64,7168]{1,2,0:T(8,128)} %copy.71, f32[64,224]{0,1:T(8,128)S(1)} %copy.72), kind=kLoop, calls=%fused_computation.17 | loop fusion | flops 2293760 | bytes 5562368 | tf_op jit(solution)/shard_map/jit(_where)/select_n | solution.py:129
  360.3 3.5 copy.85
  (94 shorter events, 55.6 us)
Async XLA Ops:
  7.2 15.4 %copy-start.14 = (f32[1,64,224]{2,1,0:T(8,128)S(1)}, f32[1,64,224]{2,1,0:T(8,128)}, u32[]{:S(2)}) copy-start(f32[1,64,224]{2,1,0:T(8,128)} %param.19) | copy-start | bytes 172036
  7.2 15.5 %copy-start.9 = (f32[1,64,7168]{2,1,0:T(8,128)S(1)}, f32[1,64,7168]{2,1,0:T(8,128)}, u32[]{:S(2)}) copy-start(f32[1,64,7168]{2,1,0:T(8,128)} %param.14) | copy-start | bytes 5505028
  7.2 95.1 %all-gather.3.cloned.1.call-start = ((), (), s32[]{:S(2)}) async-start(), calls=%async_computation.6 | async-start | bytes 3919872 | tf_op jit(solution)/shard_map/all_gather | solution.py:75
  25.2 3.6 copy-start.15
  25.2 3.8 %copy-start.16 = (f32[1,64,224]{2,1,0:T(8,128)S(1)}, f32[1,64,224]{2,1,0:T(8,128)}, u32[]{:S(2)}) copy-start(f32[1,64,224]{2,1,0:T(8,128)} %param.17) | copy-start | bytes 172036
  28.9 0.7 copy-start.12
  29.0 2.1 copy-start.1
  29.0 3.2 copy-start.2
  102.3 2.0 copy-start
  102.3 51.0 %collective-permute-start = (bf16[512,3712]{1,0:T(8,128)(2,1)}, bf16[512,3712]{1,0:T(8,128)(2,1)}, u32[]{:S(2)}, u32[]{:S(2)}) collective-permute-start(bf16[512,3712]{1,0:T(8,128)(2,1)} %all-gather.3.cloned.1.call-done), channel_id=1, source_target_pairs={{0,1},{1,0},{2,3},{3,2},{4,5},{5,4},{6,7},{7,6},{8,9},{9,8},{10,11... | collective-permute-start | bytes 11403272 | tf_op jit(solution)/shard_map/ppermute | solution.py:76
  104.3 1.5 copy-start.3
  148.7 2.7 copy-start.5
  148.9 4.5 %copy-start.7 = (bf16[4,128,1792]{2,1,0:T(8,128)(2,1)}, bf16[4,128,1792]{2,1,0:T(8,128)(2,1)S(1)}, u32[]{:S(2)}) copy-start(bf16[4,128,1792]{2,1,0:T(8,128)(2,1)S(1)} %slice.100) | copy-start | bytes 5505028
  160.1 21.9 %all-to-all-start.2 = ((bf16[4,192,1024]{2,1,0:T(8,128)(2,1)}), bf16[4,192,1024]{2,1,0:T(8,128)(2,1)S(1)}, u32[]{:S(2)}, u32[]{:S(2)}) async-start(bf16[4,192,1024]{2,1,0:T(8,128)(2,1)} %pad_maximum_fusion.1), calls=%async_computation.2 | async-start | bytes 3145728 | tf_op jit(solution)/shard_map/all_to_all | solution.py:23
  165.1 43.7 %all-gather.5.cloned.1.call-start = ((), (), s32[]{:S(2)}) async-start(), calls=%async_computation.7 | async-start | bytes 1966080 | tf_op jit(solution)/shard_map/all_gather | solution.py:105
  183.0 27.3 %copy-start.8 = (bf16[4,128,1792]{2,1,0:T(8,128)(2,1)S(1)}, bf16[4,128,1792]{2,1,0:T(8,128)(2,1)}, u32[]{:S(2)}) copy-start(bf16[4,128,1792]{2,1,0:T(8,128)(2,1)} %copy-done.7) | copy-start | bytes 5505028
  208.8 4.9 %copy-start.6 = (bf16[512,3712]{1,0:T(8,128)(2,1)S(1)}, bf16[512,3712]{1,0:T(8,128)(2,1)}, u32[]{:S(2)}) copy-start(bf16[512,3712]{1,0:T(8,128)(2,1)} %all-gather.3.cloned.1.call-done) | copy-start | bytes 11403268
  210.2 7.5 %copy-start.4 = (bf16[4,128,1024]{2,1,0:T(8,128)(2,1)}, bf16[4,128,1024]{2,1,0:T(8,128)(2,1)S(1)}, u32[]{:S(2)}) copy-start(bf16[4,128,1024]{2,1,0:T(8,128)(2,1)S(1)} %slice.109) | copy-start | bytes 3145732
  212.7 14.6 %collective-permute-start.1 = (bf16[512,1792]{1,0:T(8,128)(2,1)}, bf16[512,1792]{1,0:T(8,128)(2,1)}, u32[]{:S(2)}, u32[]{:S(2)}) collective-permute-start(bf16[512,1792]{1,0:T(8,128)(2,1)} %convolution_convert_fusion), channel_id=1, source_target_pairs={{0,1},{1,0},{2,3},{3,2},{4,5},{5,4},{6,7},{7,6},{8,9},{9,8},{10,11... | collective-permute-start | bytes 5505032 | tf_op jit(solution)/shard_map/ppermute | solution.py:109
  222.1 38.1 %all-to-all-start.5 = ((bf16[4,192,1792]{2,1,0:T(8,128)(2,1)}), bf16[4,192,1792]{2,1,0:T(8,128)(2,1)S(1)}, u32[]{:S(2)}, u32[]{:S(2)}) async-start(bf16[4,192,1792]{2,1,0:T(8,128)(2,1)} %pad_maximum_fusion), calls=%async_computation.5 | async-start | bytes 5505024 | tf_op jit(solution)/shard_map/all_to_all | solution.py:23
  260.1 54.5 %all-to-all-start.3 = ((bf16[32,16,1792]{2,1,0:T(8,128)(2,1)}), bf16[32,16,1792]{2,1,0:T(8,128)(2,1)}, u32[]{:S(2)}, u32[]{:S(2)}) async-start(bf16[32,16,1792]{2,1,0:T(8,128)(2,1)} %bitcast.146), calls=%async_computation.3 | async-start | bytes 3670016 | tf_op jit(solution)/shard_map/all_to_all | solution.py:111
  317.1 46.7 %all-to-all-start.4 = ((bf16[4,4,1792]{2,1,0:T(4,128)(2,1)}), bf16[4,4,1792]{2,1,0:T(4,128)(2,1)S(1)}, u32[]{:S(2)}, u32[]{:S(2)}) async-start(bf16[4,4,1792]{2,1,0:T(4,128)(2,1)} %reshape.179), calls=%async_computation.4 | async-start | bytes 114688 | tf_op jit(solution)/shard_map/all_to_all | solution.py:23
  326.7 3.5 copy-start.13
  339.3 3.5 copy-start.11
  (1 other events, 0.6 us)
Sparse Core Ops, SparseCore 0:
  19.1 83.1 all-gather.2
  184.8 23.9 all-gather.4

commit v2 on v1

v2 whole, which is shorter than its diff:
```python
import jax
import jax.numpy as jnp
from jax import lax
from jax.experimental import pallas as pl
from jax.experimental.pallas import tpu as pltpu
from jax.sharding import PartitionSpec as P

NX = 4
GROUP = 32
X_GROUPS = [[0, 2, 4, 6], [1, 3, 5, 7]]
CORE_SWAP = [(i, i ^ 1) for i in range(8)]
BF = jnp.bfloat16
F32 = jnp.float32
VMEM_LIMIT = 48 * 1024 * 1024


def shift_x(a, by):
    if by % NX == 0:
        return a
    return lax.ppermute(a, "expert", [(i, ((i // 2 + by) % NX) * 2 + i % 2) for i in range(2 * NX)])


def across_x(a):
    return lax.all_to_all(a, "expert", 0, 0, axis_index_groups=X_GROUPS, tiled=True)


def to_slices(a):
    return a.reshape(a.shape[0], NX, -1).transpose(1, 0, 2)


def from_slices(a):
    return a.transpose(1, 0, 2).reshape(a.shape[1], -1)


def nt(a, b):
    return lax.dot_general(a, b, (((1,), (1,)), ((), ())), preferred_element_type=F32)


def tn(a, b):
    return lax.dot_general(a, b, (((0,), (0,)), ((), ())), preferred_element_type=F32)


def mm(a, b):
    return jnp.dot(a, b, preferred_element_type=F32)


def three_terms(a):
    hi = a.astype(BF)
    rest = a - hi.astype(F32)
    mid = rest.astype(BF)
    return hi, mid, (rest - mid.astype(F32)).astype(BF)


def dequantize_kernel(x_ref, gm, um, dm, gs, us, ds, w0, w1, w2, w3, keep):
    hid, groups = gs.shape[1:]
    part = w0.shape[1]
    scales = three_terms(jnp.concatenate([gs[0], us[0], ds[0]], axis=0))
    group = lax.broadcasted_iota(jnp.int32, (groups, part), 0)
    lane_group = lax.broadcasted_iota(jnp.int32, (groups, part), 1) // GROUP
    for s, w in enumerate((w0, w1, w2, w3)):
        block = lax.rem(x_ref[0] + s, NX)
        col = pl.multiple_of(block * part, 128)
        spread = jnp.where(group == lane_group + block * (part // GROUP), 1.0, 0.0).astype(BF)
        scale = mm(scales[0], spread) + mm(scales[1], spread) + mm(scales[2], spread)
        for p, master in enumerate((gm, um, dm)):
            rows = slice(p * hid, (p + 1) * hid)
            unit = scale[rows]
            ratio = master[0, :, pl.ds(col, part)] / unit
            levels = jnp.clip(jnp.floor(ratio + 0.5), -8.0, 7.0)
            w[rows] = (levels * unit).astype(BF)
            keep[s, rows] = jnp.where((ratio > -8.5) & (ratio < 7.5), 1.0, 0.0).astype(BF)


def finish_kernel(x_ref, r0, r1, r2, r3, keep, og, ou, od):
    hid = og.shape[1]
    part = r0.shape[1]
    for s, r in enumerate((r0, r1, r2, r3)):
        col = pl.multiple_of(lax.rem(x_ref[0] + s, NX) * part, 128)
        for p, out in enumerate((og, ou, od)):
            rows = slice(p * hid, (p + 1) * hid)
            out[0, :, pl.ds(col, part)] = jnp.where(
                keep[s, rows].astype(F32) > 0.0, r[rows].astype(F32), 0.0
            )


def local_call(kernel, n_in, out_shape, cost):
    vmem = pl.BlockSpec(memory_space=pltpu.VMEM)
    return pl.pallas_call(
        kernel,
        out_shape=out_shape,
        in_specs=[pl.BlockSpec(memory_space=pltpu.SMEM)] + [vmem] * n_in,
        out_specs=[vmem] * len(out_shape),
        compiler_params=pltpu.CompilerParams(vmem_limit_bytes=VMEM_LIMIT),
        cost_estimate=pl.CostEstimate(flops=cost[0], bytes_accessed=cost[1], transcendentals=0),
    )


def per_device(
    tokens,
    grad_out,
    expert_ids,
    gate_values,
    gate_master,
    gate_scale,
    up_master,
    up_scale,
    down_master,
    down_scale,
):
    experts = lax.axis_size("expert")
    expert = lax.axis_index("expert")
    n_dp = lax.axis_size("dp")
    toks, width = tokens.shape
    hid = gate_master.shape[1]
    part = width // NX
    cap = toks // 2
    x_index = (expert // 2).reshape(1)

    named = expert_ids[:, :, None] == jnp.arange(experts, dtype=jnp.int32)
    factor = jnp.sum(jnp.where(named, gate_values[:, :, None], 0.0), axis=1)
    member = jnp.any(named, axis=1)
    rank = jnp.cumsum(member.astype(jnp.int32), axis=0) - 1
    f_hi = lax.reduce_precision(factor, 8, 7)
    f_mid = lax.reduce_precision(factor - f_hi, 8, 7)
    cols = [f_hi, f_mid, factor - f_hi - f_mid]
    cols += [jnp.where(member & (rank == slot), 1.0, 0.0) for slot in range(cap)]
    cols = jnp.concatenate(cols, axis=1).astype(BF)
    cols = jnp.pad(cols, ((0, 0), (0, 128 - cols.shape[1])))
    payload = jnp.concatenate(
        [to_slices(tokens), to_slices(grad_out), jnp.broadcast_to(cols, (NX,) + cols.shape)], axis=2
    )
    mine = across_x(payload).reshape(NX * toks, -1)
    own = lax.all_gather(mine, "dp", axis=0, tiled=True)
    other = lax.ppermute(own, "expert", CORE_SWAP)
    halves = (own, other)
    half = own.shape[0]
    blocks = half // toks

    sliced = jax.ShapeDtypeStruct((3 * hid, part), BF)
    *w_mine, keep = local_call(
        dequantize_kernel,
        6,
        [sliced] * NX + [jax.ShapeDtypeStruct((NX, 3 * hid, part), BF)],
        (30 * 3 * hid * width, 8 * 3 * hid * width),
    )(x_index, gate_master, up_master, down_master, gate_scale, up_scale, down_scale)
    w = [shift_x(a, s) for s, a in enumerate(w_mine)]
    w_gu = jnp.concatenate([a[: 2 * hid] for a in w], axis=0)
    w_d = jnp.concatenate([a[2 * hid :] for a in w], axis=0)

    pick = jnp.arange(128, dtype=jnp.int32)[:, None]
    owner = (jnp.arange(NX, dtype=jnp.int32)[None, :] * (experts - 2) + expert) % experts
    same_block = (
        jnp.arange(half, dtype=jnp.int32)[:, None] // toks == jnp.arange(blocks, dtype=jnp.int32)[None, :]
    )
    place = []
    for h in halves:
        slots = [
            mm(h[:, 2 * part :], (pick == owner + (3 + slot) * experts).astype(BF)) for slot in range(cap)
        ]
        place.append(
            [
                jnp.concatenate(
                    [jnp.where(same_block & (col[:, s : s + 1] > 0.5), 1.0, 0.0).astype(BF) for col in slots],
                    axis=1,
                )
                for s in range(NX)
            ]
        )
    pick_own = (pick % experts == expert) & (pick < 3 * experts)
    weight = jnp.concatenate(
        [
            jnp.sum(mm(h[:, 2 * part :], pick_own.astype(BF)) * place[i][0].astype(F32), axis=0)[None]
            for i, h in enumerate(halves)
        ],
        axis=1,
    )

    pre_gu = [nt(w_gu, h[:, :part]).astype(BF) for h in halves]
    pre_d = [nt(w_d, h[:, part : 2 * part]).astype(BF) for h in halves]
    pre = []
    for s in range(NX):
        packed = [
            mm(
                jnp.concatenate(
                    [pre_gu[i][s * 2 * hid : (s + 1) * 2 * hid], pre_d[i][s * hid : (s + 1) * hid]], axis=0
                ),
                place[i][s],
            )
            for i in range(2)
        ]
        pre.append(shift_x(jnp.concatenate(packed, axis=1).astype(BF), -s))
    pre = sum(a.astype(F32) for a in pre)

    gate_pre, up_pre = pre[:hid], pre[hid : 2 * hid]
    delta_hidden = jnp.where(weight > 0.0, pre[2 * hid :] * weight, 0.0)
    sig_gate = jax.nn.sigmoid(gate_pre)
    silu_gate = gate_pre * sig_gate
    hidden = jnp.where(weight > 0.0, silu_gate * up_pre * weight, 0.0)
    delta_up = delta_hidden * silu_gate
    delta_gate = delta_hidden * up_pre * sig_gate * (1.0 + gate_pre * (1.0 - sig_gate))
    delta = jnp.concatenate([delta_gate, delta_up, hidden], axis=0).astype(BF)
    delta = [shift_x(delta, s) for s in range(NX)]
    spread = [
        [
            nt(d[:, i * cap * blocks : (i + 1) * cap * blocks], place[i][s]).astype(BF)
            for s, d in enumerate(delta)
        ]
        for i in range(2)
    ]
    d_gu = [jnp.concatenate([d[: 2 * hid] for d in spread[i]], axis=0) for i in range(2)]
    d_h = [jnp.concatenate([d[2 * hid :] for d in spread[i]], axis=0) for i in range(2)]

    theirs = lax.ppermute(tn(d_gu[1], w_gu).astype(BF), "expert", CORE_SWAP)
    grad_x = (tn(d_gu[0], w_gu) + theirs.astype(F32)).astype(BF)
    grad_x = lax.all_to_all(grad_x.reshape(n_dp, NX * toks, part), "dp", 0, 0, tiled=True)
    grad_x = jnp.sum(grad_x.astype(F32), axis=0).astype(BF)
    grad_tokens = from_slices(across_x(grad_x.reshape(NX, toks, part)))

    g_gu = sum(mm(d_gu[i], h[:, :part]) for i, h in enumerate(halves)).astype(BF)
    g_d = sum(mm(d_h[i], h[:, part : 2 * part]) for i, h in enumerate(halves)).astype(BF)
    g_all = [
        shift_x(
            jnp.concatenate(
                [g_gu[s * 2 * hid : (s + 1) * 2 * hid], g_d[s * hid : (s + 1) * hid]], axis=0
            ),
            -s,
        )
        for s in range(NX)
    ]
    grads = local_call(
        finish_kernel,
        NX + 1,
        [jax.ShapeDtypeStruct((1, hid, width), F32)] * 3,
        (3 * 3 * hid * width, 8 * 3 * hid * width),
    )(x_index, *g_all, keep)
    return (grad_tokens, *grads)


def solution(mesh):
    rows = P(("dp", "expert"), None)
    weights = P("expert", "dp", None)
    return jax.shard_map(
        per_device,
        mesh=mesh,
        in_specs=(rows,) * 4 + (weights,) * 6,
        out_specs=(rows,) + (weights,) * 3,
        check_vma=False,
    )
```

time: 372 us -> 268 us (0.72)
  local copies, waits for them, and re-layouts: 54.4 us -> 8.17 us
  blocking collectives: 44.5 us -> 9.1 us
  other arithmetic: 34.7 us -> 10.6 us
  waiting for transfers between devices: 176 us -> 152 us
  Pallas kernels: 0 us -> 12 us
  starting transfers between devices: 24.9 us -> 33.1 us
  matrix products: 22.3 us -> 27.1 us
    ppermute x1 -> x13, waiting for transfers between devices: 0.01 us -> 44.2 us  [the longest x12 41.6 us: shift_x(): lax.ppermute(a, 'expert', [(i, (i // 2 + by) % NX * 2 + i % 2) for i in r...]
    all_to_all x3 -> x1, waiting for transfers between devices: 43.1 us -> 0.01 us  [across_x(): lax.all_to_all(a, 'expert', 0, 0, axis_index_groups=X_GROUPS, tiled=True)]
    all_to_all x2 -> x1, blocking collectives: 44.5 us -> 9.1 us  [across_x(): lax.all_to_all(a, 'expert', 0, 0, axis_index_groups=X_GROUPS, tiled=True)]
    unnamed x44 -> x29, local copies, waits for them, and re-layouts: 29 us -> 4.68 us
    all_gather x1 -> x0, waiting for transfers between devices: 24.1 us -> none  [per_device(): delta = lax.all_gather(delta, 'expert', axis=0, axis_index_groups=X_GROUPS)]
    ppermute x1 -> x13, starting transfers between devices: 0.01 us -> 20.9 us  [the longest x12 20.8 us: shift_x(): lax.ppermute(a, 'expert', [(i, (i // 2 + by) % NX * 2 + i % 2) for i in r...]
    select_n x3 -> x1, other arithmetic: 17.1 us -> 0.01 us  [per_device(): jnp.arange(half, dtype=jnp.int32)[:, None] // toks]
    all_to_all x1, waiting for transfers between devices: 41.7 us -> 24.8 us  [per_device(): lax.all_to_all(grad_x.reshape(n_dp, NX * toks, part), 'dp', 0, 0, tiled=T...]
  transfers between devices with their start and end apart: 8 -> 17, of which waited for: 5 -> 11; matrix products, arithmetic and copies ran while one was open for 23% -> 9% of each run, Pallas kernels for 0% -> 4%
where the time goes in v2:
time: 268 us; the launch traced here: 267 us
  waiting for transfers between devices  152 us (57%)
  starting transfers between devices  33.1 us (12%)
  matrix products  27.1 us (10%)
  between operations  14.8 us (6%)
  Pallas kernels  12 us (4%)
  other arithmetic  10.6 us (4%)
  blocking collectives  9.1 us (3%)
  local copies, waits for them, and re-layouts  8.17 us (3%)
    all_gather x1, waiting for transfers between devices, per_device(): own = lax.all_gather(mine, 'dp', axis=0, tiled=True)  83.4 us
    ppermute x12, waiting for transfers between devices, shift_x(): lax.ppermute(a, 'expert', [(i, (i // 2 + by) % NX * 2 + i % 2) for i in r...  41.6 us
    all_to_all x1, waiting for transfers between devices, per_device(): lax.all_to_all(grad_x.reshape(n_dp, NX * toks, part), 'dp', 0, 0, tiled=T...  24.8 us
    ppermute x12, starting transfers between devices, shift_x(): lax.ppermute(a, 'expert', [(i, (i // 2 + by) % NX * 2 + i % 2) for i in r...  20.8 us
    dot_general x18, matrix products, mm(): return jnp.dot(a, b, preferred_element_type=F32)  15 us
    all_to_all x1, blocking collectives, across_x(): lax.all_to_all(a, 'expert', 0, 0, axis_index_groups=X_GROUPS, tiled=True)  9.1 us
    dot_general x12, matrix products, nt(): lax.dot_general(a, b, (((1,), (1,)), ((), ())), preferred_element_type=F32)  8.6 us
    pallas_call x1, Pallas kernels, per_device(): local_call(dequantize_kernel, 6, [sliced] * NX + [jax.ShapeDtypeStruct((N...  7.58 us
  transfers between devices with their start and end apart: 17, of which 11 were waited for; matrix products, arithmetic and copies ran while one was open for 9% of the time, Pallas kernels for 4%

profile of v2, /device:TPU:2, one launch (start us, length us, event | category | flops | bytes accessed | tf_op | source)
XLA Modules:
  0.0 267.2 jit_solution(6772543478141023080)
XLA Ops:
  9.8 9.1 %all_to_all.15 = bf16[4,4,3712]{2,1,0:T(4,128)(2,1)S(1)} all-to-all(bf16[4,4,3712]{2,1,0:T(4,128)(2,1)S(1)} %pad_maximum_fusion.34), channel_id=1, replica_groups={{0,2,4,6},{1,3,5,7},{8,10,12,14},{9,11,13,15},{16,18,20,22},{17,19,21,2..., dimensions={0} | all-to-all | bytes 237568 | tf_op jit(solution)/shard_map/all_to_all | solution.py:24
  19.6 83.4 %all-gather.2.cloned.1.call-done = bf16[512,3712]{1,0:T(8,128)(2,1)} async-done(((bf16[16,3712]{1,0:T(8,128)(2,1)}), bf16[512,3712]{1,0:T(8,128)(2,1)}) %all-gather.2.cloned.1.call-update) | async-done | bytes 3801104 | tf_op jit(solution)/shard_map/all_gather | solution.py:133
  107.0 7.6 %shard_map.129 = (bf16[192,1792]{1,0:T(8,128)(2,1)S(1)}, bf16[192,1792]{1,0:T(8,128)(2,1)S(1)}, bf16[192,1792]{1,0:T(8,128)(2,1)S(1)}, bf16[192,1792]{1,0:T(8,128)(2,1)S(1)}, bf16[4,192,1792]{2,1,0:T(8,128)(2,1)}) custom-call(s32[1]{0:T(128)} %bitcast.8.x_ref, f32[1,64,7168]{2,1,0:T(8,128)S(1)} %copy-done.1, f32[1,64,7168]{2,1,0:T(8,128)} %um.1, ...), custom_call_target="tpu_custom_call" | custom-call | flops 41287680 | bytes 11010048 | tf_op jit(solution)/shard_map/pallas_call | solution.py:140
  119.4 13.4 %collective-permute-done.1 = bf16[192,1792]{1,0:T(8,128)(2,1)S(1)} collective-permute-done((bf16[192,1792]{1,0:T(8,128)(2,1)S(1)}, bf16[192,1792]{1,0:T(8,128)(2,1)S(1)}, u32[]{:S(2)}, u32[]{:S(2)}) %collective-permute-start.1) | collective-permute-done | bytes 688160 | tf_op jit(solution)/shard_map/ppermute | solution.py:20
  132.9 3.0 %collective-permute-done.2 = bf16[192,1792]{1,0:T(8,128)(2,1)S(1)} collective-permute-done((bf16[192,1792]{1,0:T(8,128)(2,1)S(1)}, bf16[192,1792]{1,0:T(8,128)(2,1)S(1)}, u32[]{:S(2)}, u32[]{:S(2)}) %collective-permute-start.2) | collective-permute-done | bytes 688160 | tf_op jit(solution)/shard_map/ppermute | solution.py:20
  135.9 13.3 %collective-permute-done.3 = bf16[192,1792]{1,0:T(8,128)(2,1)S(1)} collective-permute-done((bf16[192,1792]{1,0:T(8,128)(2,1)S(1)}, bf16[192,1792]{1,0:T(8,128)(2,1)S(1)}, u32[]{:S(2)}, u32[]{:S(2)}) %collective-permute-start.3) | collective-permute-done | bytes 688160 | tf_op jit(solution)/shard_map/ppermute | solution.py:20
  154.1 2.2 fusion.24
  156.3 2.6 fusion.18
  162.3 2.2 collective-permute-start.5
  168.7 3.6 %collective-permute-done.5 = bf16[192,512]{1,0:T(8,128)(2,1)S(1)} collective-permute-done((bf16[192,512]{1,0:T(8,128)(2,1)S(1)}, bf16[192,512]{1,0:T(8,128)(2,1)S(1)}, u32[]{:S(2)}, u32[]{:S(2)}) %collective-permute-start.5) | collective-permute-done | bytes 196640 | tf_op jit(solution)/shard_map/ppermute | solution.py:20
  174.3 3.1 %collective-permute-start.9 = (bf16[192,512]{1,0:T(8,128)(2,1)S(1)}, bf16[192,512]{1,0:T(8,128)(2,1)S(1)}, u32[]{:S(2)}, u32[]{:S(2)}) collective-permute-start(bf16[192,512]{1,0:T(8,128)(2,1)S(1)} %pad_maximum_fusion.19), channel_id=1, source_target_pairs={{0,6},{1,7},{2,0},{3,1},{4,2},{5,3},{6,4},{7,5},{8,14},{9,15},{10,... | collective-permute-start | bytes 589832 | tf_op jit(solution)/shard_map/ppermute | solution.py:20
  179.7 2.9 %collective-permute-done.9 = bf16[192,512]{1,0:T(8,128)(2,1)S(1)} collective-permute-done((bf16[192,512]{1,0:T(8,128)(2,1)S(1)}, bf16[192,512]{1,0:T(8,128)(2,1)S(1)}, u32[]{:S(2)}, u32[]{:S(2)}) %collective-permute-start.9) | collective-permute-done | bytes 196640 | tf_op jit(solution)/shard_map/ppermute | solution.py:20
  183.0 3.0 %collective-permute-done.8 = bf16[192,512]{1,0:T(8,128)(2,1)S(1)} collective-permute-done((bf16[192,512]{1,0:T(8,128)(2,1)S(1)}, bf16[192,512]{1,0:T(8,128)(2,1)S(1)}, u32[]{:S(2)}, u32[]{:S(2)}) %collective-permute-start.8) | collective-permute-done | bytes 196640 | tf_op jit(solution)/shard_map/ppermute | solution.py:20
  189.5 2.6 collective-permute-done.10
  192.1 2.4 add_convert_fusion.1
  194.5 5.7 %all-to-all-start.1 = ((bf16[32,16,1792]{2,1,0:T(8,128)(2,1)}), bf16[32,16,1792]{2,1,0:T(8,128)(2,1)}, u32[]{:S(2)}, u32[]{:S(2)}) async-start(bf16[32,16,1792]{2,1,0:T(8,128)(2,1)} %bitcast.12), calls=%async_computation.1 | async-start | bytes 3670016 | tf_op jit(solution)/shard_map/all_to_all | solution.py:215
  200.3 2.2 fusion.7
  204.7 2.6 fusion.11
  207.3 2.6 add_convert_fusion
  212.5 3.2 %collective-permute-start.11 = (bf16[192,1792]{1,0:T(8,128)(2,1)}, bf16[192,1792]{1,0:T(8,128)(2,1)S(1)}, u32[]{:S(2)}, u32[]{:S(2)}) collective-permute-start(bf16[192,1792]{1,0:T(8,128)(2,1)} %pad_maximum_fusion.3), channel_id=1, source_target_pairs={{0,6},{1,7},{2,0},{3,1},{4,2},{5,3},{6,4},{7,5},{8,14},{9,15},{10,... | collective-permute-start | bytes 2064392 | tf_op jit(solution)/shard_map/ppermute | solution.py:20
  217.7 2.6 collective-permute-start.13
  220.4 24.8 %all-to-all-done.1 = bf16[32,16,1792]{2,1,0:T(8,128)(2,1)} async-done(((bf16[32,16,1792]{2,1,0:T(8,128)(2,1)}), bf16[32,16,1792]{2,1,0:T(8,128)(2,1)}, u32[]{:S(2)}, u32[]{:S(2)}) %all-to-all-start.1) | async-done | bytes 1835040 | tf_op jit(solution)/shard_map/all_to_all | solution.py:215
  247.6 6.5 %all-to-all-start.2 = ((bf16[4,4,1792]{2,1,0:T(4,128)(2,1)}), bf16[4,4,1792]{2,1,0:T(4,128)(2,1)S(1)}, u32[]{:S(2)}, u32[]{:S(2)}) async-start(bf16[4,4,1792]{2,1,0:T(4,128)(2,1)} %reshape.143), calls=%async_computation.2 | async-start | bytes 114688 | tf_op jit(solution)/shard_map/all_to_all | solution.py:24
  255.3 4.4 %shard_map.130 = (f32[1,64,7168]{2,1,0:T(8,128)}, f32[1,64,7168]{2,1,0:T(8,128)}, f32[1,64,7168]{2,1,0:T(8,128)}) custom-call(s32[1]{0:T(128)} %bitcast.8.x_ref, bf16[192,1792]{1,0:T(8,128)(2,1)S(1)} %pad_maximum_fusion.2.r0, bf16[192,1792]{1,0:T(8,128)(2,1)S(1)} %collective-permute-done.11.r1, bf16[192,1792]{1,0:T(8,128)(2,1)} %collective-permute-done.12.r2, ...), custom_call_target="tpu_custom_call" | custom-call | flops 4128768 | bytes 11010048 | tf_op jit(solution)/shard_map/pallas_call | solution.py:230
  (146 shorter events, 43.3 us)
Async XLA Ops:
  7.2 95.8 %all-gather.2.cloned.1.call-start = ((), (), s32[]{:S(2)}) async-start(), calls=%async_computation.3 | async-start | bytes 3919872 | tf_op jit(solution)/shard_map/all_gather | solution.py:133
  103.0 48.8 %collective-permute-start = (bf16[512,3712]{1,0:T(8,128)(2,1)}, bf16[512,3712]{1,0:T(8,128)(2,1)}, u32[]{:S(2)}, u32[]{:S(2)}) collective-permute-start(bf16[512,3712]{1,0:T(8,128)(2,1)} %all-gather.2.cloned.1.call-done), channel_id=1, source_target_pairs={{0,1},{1,0},{2,3},{3,2},{4,5},{5,4},{6,7},{7,6},{8,9},{9,8},{10,11... | collective-permute-start | bytes 11403272 | tf_op jit(solution)/shard_map/ppermute | solution.py:134
  114.6 18.2 %collective-permute-start.1 = (bf16[192,1792]{1,0:T(8,128)(2,1)S(1)}, bf16[192,1792]{1,0:T(8,128)(2,1)S(1)}, u32[]{:S(2)}, u32[]{:S(2)}) collective-permute-start(bf16[192,1792]{1,0:T(8,128)(2,1)S(1)} %get-tuple-element.13), channel_id=1, source_target_pairs={{0,2},{1,3},{2,4},{3,5},{4,6},{5,7},{6,0},{7,1},{8,10},{9,11},{10,... | collective-permute-start | bytes 2064392 | tf_op jit(solution)/shard_map/ppermute | solution.py:20
  116.1 19.8 %collective-permute-start.2 = (bf16[192,1792]{1,0:T(8,128)(2,1)S(1)}, bf16[192,1792]{1,0:T(8,128)(2,1)S(1)}, u32[]{:S(2)}, u32[]{:S(2)}) collective-permute-start(bf16[192,1792]{1,0:T(8,128)(2,1)S(1)} %get-tuple-element.14), channel_id=1, source_target_pairs={{0,4},{1,5},{2,6},{3,7},{4,0},{5,1},{6,2},{7,3},{8,12},{9,13},{10,... | collective-permute-start | bytes 2064392 | tf_op jit(solution)/shard_map/ppermute | solution.py:20
  117.2 32.0 %collective-permute-start.3 = (bf16[192,1792]{1,0:T(8,128)(2,1)S(1)}, bf16[192,1792]{1,0:T(8,128)(2,1)S(1)}, u32[]{:S(2)}, u32[]{:S(2)}) collective-permute-start(bf16[192,1792]{1,0:T(8,128)(2,1)S(1)} %get-tuple-element.15), channel_id=1, source_target_pairs={{0,6},{1,7},{2,0},{3,1},{4,2},{5,3},{6,4},{7,5},{8,14},{9,15},{10,... | collective-permute-start | bytes 2064392 | tf_op jit(solution)/shard_map/ppermute | solution.py:20
  132.8 16.5 %copy-start.13 = (bf16[512,3712]{1,0:T(8,128)(2,1)S(1)}, bf16[512,3712]{1,0:T(8,128)(2,1)}, u32[]{:S(2)}) copy-start(bf16[512,3712]{1,0:T(8,128)(2,1)} %all-gather.2.cloned.1.call-done) | copy-start | bytes 11403268
  161.1 7.6 %collective-permute-start.4 = (bf16[192,512]{1,0:T(8,128)(2,1)S(1)}, bf16[192,512]{1,0:T(8,128)(2,1)S(1)}, u32[]{:S(2)}, u32[]{:S(2)}) collective-permute-start(bf16[192,512]{1,0:T(8,128)(2,1)S(1)} %pad_maximum_fusion.16), channel_id=1, source_target_pairs={{0,6},{1,7},{2,0},{3,1},{4,2},{5,3},{6,4},{7,5},{8,14},{9,15},{10,... | collective-permute-start | bytes 589832 | tf_op jit(solution)/shard_map/ppermute | solution.py:20
  162.3 9.9 %collective-permute-start.5 = (bf16[192,512]{1,0:T(8,128)(2,1)S(1)}, bf16[192,512]{1,0:T(8,128)(2,1)S(1)}, u32[]{:S(2)}, u32[]{:S(2)}) collective-permute-start(bf16[192,512]{1,0:T(8,128)(2,1)S(1)} %pad_maximum_fusion.17), channel_id=1, source_target_pairs={{0,4},{1,5},{2,6},{3,7},{4,0},{5,1},{6,2},{7,3},{8,12},{9,13},{10,... | collective-permute-start | bytes 589832 | tf_op jit(solution)/shard_map/ppermute | solution.py:20
  165.0 9.0 %collective-permute-start.6 = (bf16[192,512]{1,0:T(8,128)(2,1)S(1)}, bf16[192,512]{1,0:T(8,128)(2,1)S(1)}, u32[]{:S(2)}, u32[]{:S(2)}) collective-permute-start(bf16[192,512]{1,0:T(8,128)(2,1)S(1)} %pad_maximum_fusion.18), channel_id=1, source_target_pairs={{0,2},{1,3},{2,4},{3,5},{4,6},{5,7},{6,0},{7,1},{8,10},{9,11},{10,... | collective-permute-start | bytes 589832 | tf_op jit(solution)/shard_map/ppermute | solution.py:20
  174.3 8.4 %collective-permute-start.9 = (bf16[192,512]{1,0:T(8,128)(2,1)S(1)}, bf16[192,512]{1,0:T(8,128)(2,1)S(1)}, u32[]{:S(2)}, u32[]{:S(2)}) collective-permute-start(bf16[192,512]{1,0:T(8,128)(2,1)S(1)} %pad_maximum_fusion.19), channel_id=1, source_target_pairs={{0,6},{1,7},{2,0},{3,1},{4,2},{5,3},{6,4},{7,5},{8,14},{9,15},{10,... | collective-permute-start | bytes 589832 | tf_op jit(solution)/shard_map/ppermute | solution.py:20
  177.4 8.6 %collective-permute-start.8 = (bf16[192,512]{1,0:T(8,128)(2,1)S(1)}, bf16[192,512]{1,0:T(8,128)(2,1)S(1)}, u32[]{:S(2)}, u32[]{:S(2)}) collective-permute-start(bf16[192,512]{1,0:T(8,128)(2,1)S(1)} %pad_maximum_fusion.19), channel_id=1, source_target_pairs={{0,4},{1,5},{2,6},{3,7},{4,0},{5,1},{6,2},{7,3},{8,12},{9,13},{10,... | collective-permute-start | bytes 589832 | tf_op jit(solution)/shard_map/ppermute | solution.py:20
  177.4 9.4 %collective-permute-start.7 = (bf16[192,512]{1,0:T(8,128)(2,1)S(1)}, bf16[192,512]{1,0:T(8,128)(2,1)S(1)}, u32[]{:S(2)}, u32[]{:S(2)}) collective-permute-start(bf16[192,512]{1,0:T(8,128)(2,1)S(1)} %pad_maximum_fusion.19), channel_id=1, source_target_pairs={{0,2},{1,3},{2,4},{3,5},{4,6},{5,7},{6,0},{7,1},{8,10},{9,11},{10,... | collective-permute-start | bytes 589832 | tf_op jit(solution)/shard_map/ppermute | solution.py:20
  179.7 8.9 %copy-start.5 = (bf16[192,512]{1,0:T(8,128)(2,1)}, bf16[192,512]{1,0:T(8,128)(2,1)S(1)}, u32[]{:S(2)}) copy-start(bf16[192,512]{1,0:T(8,128)(2,1)S(1)} %convolution_convert_fusion.4) | copy-start | bytes 589828
  182.9 6.0 %copy-start.6 = (bf16[192,512]{1,0:T(8,128)(2,1)}, bf16[192,512]{1,0:T(8,128)(2,1)S(1)}, u32[]{:S(2)}) copy-start(bf16[192,512]{1,0:T(8,128)(2,1)S(1)} %convolution_convert_fusion.1) | copy-start | bytes 589828
  188.2 3.9 %collective-permute-start.10 = (bf16[512,1792]{1,0:T(8,128)(2,1)S(1)}, bf16[512,1792]{1,0:T(8,128)(2,1)S(1)}, u32[]{:S(2)}, u32[]{:S(2)}) collective-permute-start(bf16[512,1792]{1,0:T(8,128)(2,1)S(1)} %convolution_convert_fusion), channel_id=1, source_target_pairs={{0,1},{1,0},{2,3},{3,2},{4,5},{5,4},{6,7},{7,6},{8,9},{9,8},{10,11... | collective-permute-start | bytes 5505032 | tf_op jit(solution)/shard_map/ppermute | solution.py:213
  194.5 5.7 %slice-start.4 = ((bf16[192,512]{1,0:T(8,128)(2,1)}), bf16[64,512]{1,0:T(8,128)(2,1)S(1)}, s32[]{:S(2)}) async-start(bf16[192,512]{1,0:T(8,128)(2,1)} %copy-done.9), calls=%async_computation.8 | async-start | bytes 131072 | tf_op jit(solution)/shard_map/slice | solution.py:211
  194.5 5.7 %slice-start.5 = ((bf16[192,512]{1,0:T(8,128)(2,1)}), bf16[64,512]{1,0:T(8,128)(2,1)S(1)}, s32[]{:S(2)}) async-start(bf16[192,512]{1,0:T(8,128)(2,1)} %copy-done.10), calls=%async_computation.9 | async-start | bytes 131072 | tf_op jit(solution)/shard_map/slice | solution.py:211
  194.5 5.7 %slice-start.6 = ((bf16[192,512]{1,0:T(8,128)(2,1)}), bf16[64,512]{1,0:T(8,128)(2,1)S(1)}, s32[]{:S(2)}) async-start(bf16[192,512]{1,0:T(8,128)(2,1)} %copy-done.11), calls=%async_computation.10 | async-start | bytes 131072 | tf_op jit(solution)/shard_map/slice | solution.py:211
  194.5 50.7 %all-to-all-start.1 = ((bf16[32,16,1792]{2,1,0:T(8,128)(2,1)}), bf16[32,16,1792]{2,1,0:T(8,128)(2,1)}, u32[]{:S(2)}, u32[]{:S(2)}) async-start(bf16[32,16,1792]{2,1,0:T(8,128)(2,1)} %bitcast.12), calls=%async_computation.1 | async-start | bytes 3670016 | tf_op jit(solution)/shard_map/all_to_all | solution.py:215
  212.5 42.8 %collective-permute-start.11 = (bf16[192,1792]{1,0:T(8,128)(2,1)}, bf16[192,1792]{1,0:T(8,128)(2,1)S(1)}, u32[]{:S(2)}, u32[]{:S(2)}) collective-permute-start(bf16[192,1792]{1,0:T(8,128)(2,1)} %pad_maximum_fusion.3), channel_id=1, source_target_pairs={{0,6},{1,7},{2,0},{3,1},{4,2},{5,3},{6,4},{7,5},{8,14},{9,15},{10,... | collective-permute-start | bytes 2064392 | tf_op jit(solution)/shard_map/ppermute | solution.py:20
  216.6 38.7 %collective-permute-start.12 = (bf16[192,1792]{1,0:T(8,128)(2,1)}, bf16[192,1792]{1,0:T(8,128)(2,1)}, u32[]{:S(2)}, u32[]{:S(2)}) collective-permute-start(bf16[192,1792]{1,0:T(8,128)(2,1)} %pad_maximum_fusion.4), channel_id=1, source_target_pairs={{0,4},{1,5},{2,6},{3,7},{4,0},{5,1},{6,2},{7,3},{8,12},{9,13},{10,... | collective-permute-start | bytes 2064392 | tf_op jit(solution)/shard_map/ppermute | solution.py:20
  217.7 37.5 %copy-start = (bf16[4,192,1792]{2,1,0:T(8,128)(2,1)S(1)}, bf16[4,192,1792]{2,1,0:T(8,128)(2,1)}, u32[]{:S(2)}) copy-start(bf16[4,192,1792]{2,1,0:T(8,128)(2,1)} %get-tuple-element.16.keep) | copy-start | bytes 8257540
  217.7 37.5 %collective-permute-start.13 = (bf16[192,1792]{1,0:T(8,128)(2,1)}, bf16[192,1792]{1,0:T(8,128)(2,1)}, u32[]{:S(2)}, u32[]{:S(2)}) collective-permute-start(bf16[192,1792]{1,0:T(8,128)(2,1)} %pad_maximum_fusion.5), channel_id=1, source_target_pairs={{0,2},{1,3},{2,4},{3,5},{4,6},{5,7},{6,0},{7,1},{8,10},{9,11},{10,... | collective-permute-start | bytes 2064392 | tf_op jit(solution)/shard_map/ppermute | solution.py:20
  247.6 12.2 %all-to-all-start.2 = ((bf16[4,4,1792]{2,1,0:T(4,128)(2,1)}), bf16[4,4,1792]{2,1,0:T(4,128)(2,1)S(1)}, u32[]{:S(2)}, u32[]{:S(2)}) async-start(bf16[4,4,1792]{2,1,0:T(4,128)(2,1)} %reshape.143), calls=%async_computation.2 | async-start | bytes 114688 | tf_op jit(solution)/shard_map/all_to_all | solution.py:24
  (15 other events, 41.0 us)
Sparse Core Ops, SparseCore 0:
  19.8 83.1 all-gather.1

commit v3 on v2

v3 whole, which is shorter than its diff:
```python
import jax
import jax.numpy as jnp
from jax import lax
from jax.experimental import pallas as pl
from jax.experimental.pallas import tpu as pltpu
from jax.sharding import PartitionSpec as P

NX, NY, NZ = 4, 4, 8
GROUP = 32
X_GROUPS = [[0, 2, 4, 6], [1, 3, 5, 7]]
CORE_SWAP = [(i, i ^ 1) for i in range(8)]
BF = jnp.bfloat16
F32 = jnp.float32
VMEM_LIMIT = 60 * 1024 * 1024


def shift_x(a, by):
    if by % NX == 0:
        return a
    return lax.ppermute(a, "expert", [(i, ((i // 2 + by) % NX) * 2 + i % 2) for i in range(2 * NX)])


def shift_y(a, by):
    if by == 0:
        return a
    return lax.ppermute(a, "dp", [(i, ((i // NZ + by) % NY) * NZ + i % NZ) for i in range(NY * NZ)])


def shift_z(a, by):
    if by == 0:
        return a
    return lax.ppermute(a, "dp", [(i, (i // NZ) * NZ + (i % NZ + by) % NZ) for i in range(NY * NZ)])


def gather_y(a):
    return jnp.concatenate([a] + [shift_y(a, -k) for k in range(1, NY)], axis=0)


def gather_z(a, early, late):
    after, before = [a], [a]
    for step in range(NZ // 2 - 1):
        if step == 2:
            (after[-1], before[-1]), early = lax.optimization_barrier(((after[-1], before[-1]), early))
        after.append(shift_z(after[-1], -1))
        before.append(shift_z(before[-1], 1))
    last, late = lax.optimization_barrier(((after[-1], before[-1]), late))
    cut = a.shape[0] // 2
    far = jnp.concatenate([shift_z(last[0][:cut], -1), shift_z(last[1][cut:], 1)], axis=0)
    return jnp.concatenate(after + [far] + before[:0:-1], axis=0), early, late


def in_order(a, z, y):
    a = lax.dynamic_slice_in_dim(jnp.concatenate([a, a], axis=0), NZ - z, NZ, 0)
    a = lax.dynamic_slice_in_dim(jnp.concatenate([a, a], axis=1), NY - y, NY, 1)
    return a.transpose(1, 0, 2, 3)


def placing(at, slots):
    return jnp.concatenate([jnp.where(at & (c > 0.5), 1.0, 0.0).astype(BF) for c in slots], axis=1)


def total(terms):
    return jnp.sum(terms.astype(F32), axis=0).astype(BF)


def across_x(a):
    return lax.all_to_all(a, "expert", 0, 0, axis_index_groups=X_GROUPS, tiled=True)


def to_slices(a):
    return a.reshape(a.shape[0], NX, -1).transpose(1, 0, 2)


def from_slices(a):
    return a.transpose(1, 0, 2).reshape(a.shape[1], -1)


def nt(a, b):
    return lax.dot_general(a, b, (((1,), (1,)), ((), ())), preferred_element_type=F32)


def tn(a, b):
    return lax.dot_general(a, b, (((0,), (0,)), ((), ())), preferred_element_type=F32)


def mm(a, b):
    return jnp.dot(a, b, preferred_element_type=F32)


def three_terms(a):
    hi = a.astype(BF)
    rest = a - hi.astype(F32)
    mid = rest.astype(BF)
    return hi, mid, (rest - mid.astype(F32)).astype(BF)


def dequantize_kernel(gm, um, dm, gs, us, ds, w, keep):
    hid, groups = gs.shape[1:]
    part = w.shape[2]
    scales = three_terms(jnp.concatenate([gs[0], us[0], ds[0]], axis=0))
    group = lax.broadcasted_iota(jnp.int32, (groups, part), 0)
    lane_group = lax.broadcasted_iota(jnp.int32, (groups, part), 1) // GROUP
    spread = jnp.where(group == lane_group + pl.program_id(0) * (part // GROUP), 1.0, 0.0).astype(BF)
    scale = mm(scales[0], spread) + mm(scales[1], spread) + mm(scales[2], spread)
    for p, master in enumerate((gm, um, dm)):
        rows = slice(p * hid, (p + 1) * hid)
        unit = scale[rows]
        ratio = master[0] / unit
        levels = jnp.clip(jnp.floor(ratio + 0.5), -8.0, 7.0)
        w[0, rows] = (levels * unit).astype(BF)
        keep[0, rows] = jnp.where((ratio > -8.5) & (ratio < 7.5), 1.0, 0.0).astype(BF)


def dequantize(masters, scales):
    _, hid, width = masters[0].shape
    part = width // NX
    out = pl.BlockSpec((1, 3 * hid, part), lambda i: (i, 0, 0))
    return pl.pallas_call(
        dequantize_kernel,
        grid=(NX,),
        out_shape=[jax.ShapeDtypeStruct((NX, 3 * hid, part), BF)] * 2,
        in_specs=[pl.BlockSpec((1, hid, part), lambda i: (0, 0, i))] * 3
        + [pl.BlockSpec(scales[0].shape, lambda i: (0, 0, 0))] * 3,
        out_specs=[out] * 2,
        compiler_params=pltpu.CompilerParams(vmem_limit_bytes=VMEM_LIMIT),
        cost_estimate=pl.CostEstimate(
            flops=30 * 3 * hid * width, bytes_accessed=8 * 3 * hid * width, transcendentals=0
        ),
    )(*masters, *scales)


def finish_kernel(x_ref, r0, r1, r2, r3, keep, og, ou, od):
    hid = og.shape[1]
    part = r0.shape[1]
    for s, r in enumerate((r0, r1, r2, r3)):
        block = lax.rem(x_ref[0] + s, NX)
        col = pl.multiple_of(block * part, 128)
        for p, out in enumerate((og, ou, od)):
            rows = slice(p * hid, (p + 1) * hid)
            out[0, :, pl.ds(col, part)] = jnp.where(
                keep[block, rows].astype(F32) > 0.0, r[rows].astype(F32), 0.0
            )


def local_call(kernel, n_in, out_shape, cost):
    vmem = pl.BlockSpec(memory_space=pltpu.VMEM)
    return pl.pallas_call(
        kernel,
        out_shape=out_shape,
        in_specs=[pl.BlockSpec(memory_space=pltpu.SMEM)] + [vmem] * n_in,
        out_specs=[vmem] * len(out_shape),
        compiler_params=pltpu.CompilerParams(vmem_limit_bytes=VMEM_LIMIT),
        cost_estimate=pl.CostEstimate(flops=cost[0], bytes_accessed=cost[1], transcendentals=0),
    )


def per_device(
    tokens,
    grad_out,
    expert_ids,
    gate_values,
    gate_master,
    gate_scale,
    up_master,
    up_scale,
    down_master,
    down_scale,
):
    experts = lax.axis_size("expert")
    expert = lax.axis_index("expert")
    toks, width = tokens.shape
    hid = gate_master.shape[1]
    part = width // NX
    cap = toks // 2
    x_index = (expert // 2).reshape(1)

    named = expert_ids[:, :, None] == jnp.arange(experts, dtype=jnp.int32)
    factor = jnp.sum(jnp.where(named, gate_values[:, :, None], 0.0), axis=1)
    member = jnp.any(named, axis=1)
    rank = jnp.cumsum(member.astype(jnp.int32), axis=0) - 1
    f_hi = lax.reduce_precision(factor, 8, 7)
    f_mid = lax.reduce_precision(factor - f_hi, 8, 7)
    cols = [f_hi, f_mid, factor - f_hi - f_mid]
    cols += [jnp.where(member & (rank == slot), 1.0, 0.0) for slot in range(cap)]
    cols = jnp.concatenate(cols, axis=1).astype(BF)
    cols = jnp.pad(cols, ((0, 0), (0, 128 - cols.shape[1])))
    payload = jnp.concatenate(
        [to_slices(tokens), jnp.broadcast_to(cols, (NX,) + cols.shape), to_slices(grad_out)], axis=2
    )
    mine = across_x(payload).reshape(NX * toks, -1)
    w_mine, keep = dequantize(
        (gate_master, up_master, down_master), (gate_scale, up_scale, down_scale)
    )
    w_mine = [
        lax.dynamic_index_in_dim(w_mine, (expert // 2 + s) % NX, 0, keepdims=False) for s in range(NX)
    ]
    own, w_mine = lax.optimization_barrier((gather_y(mine), w_mine))
    w = [shift_x(a, s) if s != 2 else a for s, a in enumerate(w_mine)]
    w = lax.optimization_barrier(w)
    own, (w[1], w[3]), w[2] = gather_z(own, (w[1], w[3]), shift_x(w[2], 2))
    halves = (own, lax.ppermute(own, "expert", CORE_SWAP))
    x_rows = [h[:, :part] for h in halves]
    g_rows = [h[:, part + 128 :] for h in halves]
    tables = [h[:, part : part + 128] for h in halves]
    half = own.shape[0]
    blocks = half // toks
    w_gu = jnp.concatenate([a[: 2 * hid] for a in w], axis=0)
    w_d = jnp.concatenate([a[2 * hid :] for a in w], axis=0)

    pick = jnp.arange(128, dtype=jnp.int32)[:, None]
    owner = (jnp.arange(NX, dtype=jnp.int32)[None, :] * (experts - 2) + expert) % experts
    pick_own = ((pick % experts == expert) & (pick < 3 * experts)).astype(BF)
    unit = NX * toks
    token = jnp.arange(half, dtype=jnp.int32)[:, None]
    block = jnp.arange(blocks, dtype=jnp.int32)[None, :]
    y, z = lax.axis_index("dp") // NZ, lax.axis_index("dp") % NZ
    t_y, t_z = token // (NZ * unit), token // unit % NZ
    from_here = ((t_z + NZ - z) % NZ) * NY + (t_y + NY - y) % NY
    at = token // toks == block
    at_in_order = from_here * NX + token % unit // toks == block
    place, place_in_order, weight = [], [], []
    for table in tables:
        slots = [mm(table, (pick == owner + (3 + slot) * experts).astype(BF)) for slot in range(cap)]
        place.append([placing(at, [c[:, s : s + 1] for c in slots]) for s in range(NX)])
        slots = [in_order(a.reshape(NZ, NY, unit, NX), z, y).reshape(half, NX) for a in slots]
        place_in_order.append([placing(at_in_order, [c[:, s : s + 1] for c in slots]) for s in range(NX)])
        weight.append(jnp.sum(mm(table, pick_own) * place[-1][0].astype(F32), axis=0)[None])
    weight = jnp.concatenate(weight, axis=1)

    pre_gu = [nt(w_gu, h).astype(BF) for h in x_rows]
    pre_d = [nt(w_d, h).astype(BF) for h in g_rows]
    pre = []
    for s in range(NX):
        packed = [
            jnp.concatenate(
                [
                    mm(pre_gu[i][s * 2 * hid : (s + 1) * 2 * hid], place[i][s]),
                    mm(pre_d[i][s * hid : (s + 1) * hid], place[i][s]),
                ],
                axis=0,
            )
            for i in range(2)
        ]
        pre.append(shift_x(jnp.concatenate(packed, axis=1).astype(BF), -s))
    pre = sum(a.astype(F32) for a in pre)

    gate_pre, up_pre = pre[:hid], pre[hid : 2 * hid]
    delta_hidden = jnp.where(weight > 0.0, pre[2 * hid :] * weight, 0.0)
    sig_gate = jax.nn.sigmoid(gate_pre)
    silu_gate = gate_pre * sig_gate
    hidden = jnp.where(weight > 0.0, silu_gate * up_pre * weight, 0.0)
    delta_up = delta_hidden * silu_gate
    delta_gate = delta_hidden * up_pre * sig_gate * (1.0 + gate_pre * (1.0 - sig_gate))
    delta = jnp.concatenate([delta_gate, delta_up, hidden], axis=0).astype(BF)
    delta = [shift_x(delta, s) for s in range(NX)]
    d_gu, d_h, d_in_order = [], [], []
    for i in range(2):
        packed = [d[:, i * cap * blocks : (i + 1) * cap * blocks] for d in delta]
        d_in_order.append(
            jnp.concatenate([nt(d[: 2 * hid], place_in_order[i][s]) for s, d in enumerate(packed)], axis=0).astype(BF)
        )
        tokens_d = [nt(d, place[i][s]).astype(BF) for s, d in enumerate(packed)]
        d_gu.append(jnp.concatenate([d[: 2 * hid] for d in tokens_d], axis=0))
        d_h.append(jnp.concatenate([d[2 * hid :] for d in tokens_d], axis=0))

    theirs = lax.ppermute(tn(d_in_order[1], w_gu).astype(BF), "expert", CORE_SWAP)
    grad_x = (tn(d_in_order[0], w_gu) + theirs.astype(F32)).astype(BF)
    grad_x = lax.all_to_all(grad_x.reshape(NY * NZ, unit, part), "dp", 0, 0, tiled=True)
    grad_tokens = from_slices(across_x(total(grad_x).reshape(NX, toks, part)))

    g_gu = sum(mm(d_gu[i], h) for i, h in enumerate(x_rows)).astype(BF)
    g_d = sum(mm(d_h[i], h) for i, h in enumerate(g_rows)).astype(BF)
    g_all = [
        shift_x(
            jnp.concatenate(
                [g_gu[s * 2 * hid : (s + 1) * 2 * hid], g_d[s * hid : (s + 1) * hid]], axis=0
            ),
            -s,
        )
        for s in range(NX)
    ]
    grads = local_call(
        finish_kernel,
        NX + 1,
        [jax.ShapeDtypeStruct((1, hid, width), F32)] * 3,
        (3 * 3 * hid * width, 8 * 3 * hid * width),
    )(x_index, *g_all, keep)
    return (grad_tokens, *grads)


def solution(mesh):
    rows = P(("dp", "expert"), None)
    weights = P("expert", "dp", None)
    return jax.shard_map(
        per_device,
        mesh=mesh,
        in_specs=(rows,) * 4 + (weights,) * 6,
        out_specs=(rows,) + (weights,) * 3,
        check_vma=False,
    )
```

time: 268 us -> 206 us (0.77)
  waiting for transfers between devices: 152 us -> 69.7 us
  starting transfers between devices: 33.1 us -> 54.9 us
  matrix products: 27.1 us -> 40.2 us
  between operations: 14.8 us -> 2.04 us
  blocking collectives: 9.1 us -> 0 us
  local copies, waits for them, and re-layouts: 8.17 us -> 13.4 us
    all_gather x1 -> x0, waiting for transfers between devices: 83.4 us -> none  [per_device(): own = lax.all_gather(mine, 'dp', axis=0, tiled=True)]
    ppermute x12, waiting for transfers between devices: 41.6 us -> 18.9 us  [shift_x(): lax.ppermute(a, 'expert', [(i, (i // 2 + by) % NX * 2 + i % 2) for i in r...]
    ppermute x2 -> x13, waiting for transfers between devices: 2.59 us -> 22.5 us  [the longest x8 18.9 us: shift_z(): lax.ppermute(a, 'dp', [(i, i // NZ * NZ + (i % NZ + by) % NZ) for i in ra...]
    ppermute x2 -> x13, starting transfers between devices: 0.1 us -> 19.1 us  [the longest x8 13.9 us: shift_z(): lax.ppermute(a, 'dp', [(i, i // NZ * NZ + (i % NZ + by) % NZ) for i in ra...]
    all_to_all x1 -> x0, blocking collectives: 9.1 us -> none  [across_x(): lax.all_to_all(a, 'expert', 0, 0, axis_index_groups=X_GROUPS, tiled=True)]
    dot_general x12 -> x20, matrix products: 8.6 us -> 15.7 us  [nt(): lax.dot_general(a, b, (((1,), (1,)), ((), ())), preferred_element_type=F32)]
    dot_general x18 -> x26, matrix products: 15 us -> 20.9 us  [mm(): return jnp.dot(a, b, preferred_element_type=F32)]
    all_to_all x1 -> x2, starting transfers between devices: 6.49 us -> 11.2 us  [across_x(): lax.all_to_all(a, 'expert', 0, 0, axis_index_groups=X_GROUPS, tiled=True)]
  transfers between devices with their start and end apart: 17 -> 28, of which waited for: 11 -> 20; matrix products, arithmetic and copies ran while one was open for 9% -> 20% of each run, Pallas kernels for 4% -> 7%
where the time goes in v3:
time: 206 us; the launch traced here: 205 us
  waiting for transfers between devices  69.7 us (34%)
  starting transfers between devices  54.9 us (27%)
  matrix products  40.2 us (20%)
  Pallas kernels  13.6 us (7%)
  local copies, waits for them, and re-layouts  13.4 us (7%)
  other arithmetic  10.7 us (5%)
    all_to_all x1, waiting for transfers between devices, per_device(): lax.all_to_all(grad_x.reshape(NY * NZ, unit, part), 'dp', 0, 0, tiled=True)  28.3 us
    dot_general x26, matrix products, mm(): return jnp.dot(a, b, preferred_element_type=F32)  20.9 us
    ppermute x8, waiting for transfers between devices, shift_z(): lax.ppermute(a, 'dp', [(i, i // NZ * NZ + (i % NZ + by) % NZ) for i in ra...  18.9 us
    ppermute x12, waiting for transfers between devices, shift_x(): lax.ppermute(a, 'expert', [(i, (i // 2 + by) % NX * 2 + i % 2) for i in r...  18.9 us
    ppermute x12, starting transfers between devices, shift_x(): lax.ppermute(a, 'expert', [(i, (i // 2 + by) % NX * 2 + i % 2) for i in r...  18.2 us
    dot_general x20, matrix products, nt(): lax.dot_general(a, b, (((1,), (1,)), ((), ())), preferred_element_type=F32)  15.7 us
    ppermute x8, starting transfers between devices, shift_z(): lax.ppermute(a, 'dp', [(i, i // NZ * NZ + (i % NZ + by) % NZ) for i in ra...  13.9 us
    all_to_all x2, starting transfers between devices, across_x(): lax.all_to_all(a, 'expert', 0, 0, axis_index_groups=X_GROUPS, tiled=True)  11.2 us
  transfers between devices with their start and end apart: 28, of which 20 were waited for; matrix products, arithmetic and copies ran while one was open for 20% of the time, Pallas kernels for 7%

profile of v3, /device:TPU:2, one launch (start us, length us, event | category | flops | bytes accessed | tf_op | source)
XLA Modules:
  0.0 204.5 jit_solution(10757197229163034000)
XLA Ops:
  3.9 5.6 %all-to-all-start = ((bf16[4,4,3712]{2,1,0:T(4,128)(2,1)}), bf16[4,4,3712]{2,1,0:T(4,128)(2,1)S(1)}, u32[]{:S(2)}, u32[]{:S(2)}) async-start(bf16[4,4,3712]{2,1,0:T(4,128)(2,1)} %pad_maximum_fusion.18), calls=%async_computation | async-start | bytes 237568 | tf_op jit(solution)/shard_map/all_to_all | solution.py:67
  9.4 7.9 %shard_map.129 = (bf16[4,192,1792]{2,1,0:T(8,128)(2,1)}, bf16[4,192,1792]{2,1,0:T(8,128)(2,1)}) custom-call(f32[1,64,7168]{2,1,0:T(8,128)} %gm.1, f32[1,64,7168]{2,1,0:T(8,128)} %um.1, f32[1,64,7168]{2,1,0:T(8,128)} %dm.1, f32[1,64,224]{2,1,0:T(8,128)} %gs.1, f32[1,64,224]{2,1,0:T(8,128)} %us.1, f32[1,64,224]{2,1,0:T(8,128)} %ds.1), custom_call_target="tpu_custom_call" | custom-call | flops 41287680 | bytes 11010048 | tf_op jit(solution)/shard_map/pallas_call | solution.py:118
  18.3 2.9 %collective-permute-start.1 = (bf16[16,3712]{1,0:T(8,128)(2,1)S(1)}, bf16[16,3712]{1,0:T(8,128)(2,1)S(1)}, u32[]{:S(2)}, u32[]{:S(2)}) collective-permute-start(bf16[16,3712]{1,0:T(8,128)(2,1)S(1)} %reshape.341), channel_id=1, source_target_pairs={{0,128},{8,136},{16,144},{24,152},{32,160},{40,168},{48,176},{56,1... | collective-permute-start | bytes 356360 | tf_op jit(solution)/shard_map/ppermute | solution.py:26
  26.4 5.8 %collective-permute-start.3 = (bf16[64,3712]{1,0:T(8,128)(2,1)S(1)}, bf16[64,3712]{1,0:T(8,128)(2,1)S(1)}, u32[]{:S(2)}, u32[]{:S(2)}) collective-permute-start(bf16[64,3712]{1,0:T(8,128)(2,1)S(1)} %pad_maximum_fusion.6), channel_id=1, source_target_pairs={{0,56},{8,0},{16,8},{24,16},{32,24},{40,32},{48,40},{56,48},{64,12... | collective-permute-start | bytes 1425416 | tf_op jit(solution)/shard_map/ppermute | solution.py:32
  34.2 7.2 %collective-permute-done.3 = bf16[64,3712]{1,0:T(8,128)(2,1)S(1)} collective-permute-done((bf16[64,3712]{1,0:T(8,128)(2,1)S(1)}, bf16[64,3712]{1,0:T(8,128)(2,1)S(1)}, u32[]{:S(2)}, u32[]{:S(2)}) %collective-permute-start.3) | collective-permute-done | bytes 475168 | tf_op jit(solution)/shard_map/ppermute | solution.py:32
  41.3 3.7 %collective-permute-start.4 = (bf16[64,3712]{1,0:T(8,128)(2,1)S(1)}, bf16[64,3712]{1,0:T(8,128)(2,1)S(1)}, u32[]{:S(2)}, u32[]{:S(2)}) collective-permute-start(bf16[64,3712]{1,0:T(8,128)(2,1)S(1)} %collective-permute-done.3), channel_id=1, source_target_pairs={{0,56},{8,0},{16,8},{24,16},{32,24},{40,32},{48,40},{56,48},{64,12... | collective-permute-start | bytes 1425416 | tf_op jit(solution)/shard_map/ppermute | solution.py:32
  53.3 3.4 %collective-permute-done.6 = bf16[64,3712]{1,0:T(8,128)(2,1)S(1)} collective-permute-done((bf16[64,3712]{1,0:T(8,128)(2,1)S(1)}, bf16[64,3712]{1,0:T(8,128)(2,1)S(1)}, u32[]{:S(2)}, u32[]{:S(2)}) %collective-permute-start.6) | collective-permute-done | bytes 475168 | tf_op jit(solution)/shard_map/ppermute | solution.py:32
  60.4 5.2 %collective-permute-done.11 = bf16[192,1792]{1,0:T(8,128)(2,1)S(1)} collective-permute-done((bf16[192,1792]{1,0:T(8,128)(2,1)S(1)}, bf16[192,1792]{1,0:T(8,128)(2,1)S(1)}, u32[]{:S(2)}, u32[]{:S(2)}) %collective-permute-start.11) | collective-permute-done | bytes 688160 | tf_op jit(solution)/shard_map/ppermute | solution.py:20
  71.0 3.0 %collective-permute-done.12 = bf16[32,3712]{1,0:T(8,128)(2,1)S(1)} collective-permute-done((bf16[32,3712]{1,0:T(8,128)(2,1)S(1)}, bf16[32,3712]{1,0:T(8,128)(2,1)S(1)}, u32[]{:S(2)}, u32[]{:S(2)}) %collective-permute-start.12) | collective-permute-done | bytes 237600 | tf_op jit(solution)/shard_map/ppermute | solution.py:32
  85.0 3.0 %fusion.21 = bf16[256,512]{1,0:T(8,128)(2,1)} fusion(bf16[512,3712]{1,0:T(8,128)(2,1)} %constant_dynamic-update-slice_fusion, bf16[64,1792]{1,0:T(8,128)(2,1)S(1)} %copy-done.9, bf16[64,1792]{1,0:T(8,128)(2,1)S(1)} %slice.347, bf16[64,1792]{1,0:T(8,128)(2,1)} %slice.346, bf16[64,1792]{1,0:T(8,128)(2,1)S(1)} %slice.345), kind=kOutput, calls=%fused_computation.22 | convolution fusion | flops 473563136 | bytes 3014656 | tf_op jit(solution)/shard_map/dot_general | solution.py:79
  88.1 3.5 %fusion.15 = bf16[512,512]{1,0:T(8,128)(2,1)} fusion(bf16[512,3712]{1,0:T(8,128)(2,1)} %constant_dynamic-update-slice_fusion, bf16[128,1792]{1,0:T(8,128)(2,1)S(1)} %slice.342, bf16[128,1792]{1,0:T(8,128)(2,1)S(1)} %slice.341, bf16[128,1792]{1,0:T(8,128)(2,1)S(1)} %slice.340, bf16[128,1792]{1,0:T(8,128)(2,1)S(1)} %slice.339), kind=kOutput, calls=%fused_computation.20 | convolution fusion | flops 947126272 | bytes 4194304 | tf_op jit(solution)/shard_map/dot_general | solution.py:79
  95.8 2.7 %fusion.24 = bf16[256,512]{1,0:T(8,128)(2,1)S(1)} fusion(bf16[512,3712]{1,0:T(8,128)(2,1)} %collective-permute-done.14, bf16[64,1792]{1,0:T(8,128)(2,1)S(1)} %copy-done.10, bf16[64,1792]{1,0:T(8,128)(2,1)} %copy-done.12, bf16[64,1792]{1,0:T(8,128)(2,1)S(1)} %copy-done.11, bf16[64,1792]{1,0:T(8,128)(2,1)S(1)} %slice.345), kind=kOutput, calls=%fused_computation.23 | convolution fusion | flops 473563136 | bytes 3014656 | tf_op jit(solution)/shard_map/dot_general | solution.py:79
  98.8 2.7 %fusion.18 = bf16[512,512]{1,0:T(8,128)(2,1)S(1)} fusion(bf16[512,3712]{1,0:T(8,128)(2,1)} %collective-permute-done.14, bf16[128,1792]{1,0:T(8,128)(2,1)S(1)} %copy-done.5, bf16[128,1792]{1,0:T(8,128)(2,1)S(1)} %copy-done.7, bf16[128,1792]{1,0:T(8,128)(2,1)S(1)} %slice.340, bf16[128,1792]{1,0:T(8,128)(2,1)S(1)} %slice.339), kind=kOutput, calls=%fused_computation.21 | convolution fusion | flops 947126272 | bytes 4194304 | tf_op jit(solution)/shard_map/dot_general | solution.py:79
  115.3 3.2 %collective-permute-done.15 = bf16[192,512]{1,0:T(8,128)(2,1)S(1)} collective-permute-done((bf16[192,512]{1,0:T(8,128)(2,1)S(1)}, bf16[192,512]{1,0:T(8,128)(2,1)S(1)}, u32[]{:S(2)}, u32[]{:S(2)}) %collective-permute-start.15) | collective-permute-done | bytes 196640 | tf_op jit(solution)/shard_map/ppermute | solution.py:20
  124.1 2.4 %collective-permute-done.20 = bf16[192,512]{1,0:T(8,128)(2,1)S(1)} collective-permute-done((bf16[192,512]{1,0:T(8,128)(2,1)S(1)}, bf16[192,512]{1,0:T(8,128)(2,1)S(1)}, u32[]{:S(2)}, u32[]{:S(2)}) %collective-permute-start.20) | collective-permute-done | bytes 196640 | tf_op jit(solution)/shard_map/ppermute | solution.py:20
  127.0 2.8 %collective-permute-done.19 = bf16[192,512]{1,0:T(8,128)(2,1)S(1)} collective-permute-done((bf16[192,512]{1,0:T(8,128)(2,1)S(1)}, bf16[192,512]{1,0:T(8,128)(2,1)S(1)}, u32[]{:S(2)}, u32[]{:S(2)}) %collective-permute-start.19) | collective-permute-done | bytes 196640 | tf_op jit(solution)/shard_map/ppermute | solution.py:20
  136.7 2.4 %add_convert_fusion.1 = bf16[512,1792]{1,0:T(8,128)(2,1)} fusion(bf16[512,1792]{1,0:T(8,128)(2,1)S(1)} %collective-permute-done.21, bf16[128,512]{1,0:T(8,128)(2,1)S(1)} %convolution_convert_fusion.13, bf16[128,512]{1,0:T(8,128)(2,1)S(1)} %convolution_convert_fusion.14, bf16[128,512]{1,0:T(8,128)(2,1)S(1)} %convolution_convert_fusion.15, ...), kind=kOutput, calls=%fused_computation.1 | convolution fusion | flops 951713792 | bytes 6029312 | tf_op jit(solution)/shard_map/dot_general | solution.py:83
  139.3 6.4 %all-to-all-start.1 = ((bf16[32,16,1792]{2,1,0:T(8,128)(2,1)}), bf16[32,16,1792]{2,1,0:T(8,128)(2,1)S(1)}, u32[]{:S(2)}, u32[]{:S(2)}) async-start(bf16[32,16,1792]{2,1,0:T(8,128)(2,1)} %bitcast.62), calls=%async_computation.1 | async-start | bytes 3670016 | tf_op jit(solution)/shard_map/all_to_all | solution.py:268
  150.3 2.7 %fusion.5 = f32[512,1792]{1,0:T(8,128)S(1)} fusion(bf16[512,3712]{1,0:T(8,128)(2,1)} %collective-permute-done.14, bf16[128,512]{1,0:T(8,128)(2,1)S(1)} %slice-done.11, bf16[128,512]{1,0:T(8,128)(2,1)S(1)} %slice-done.13, bf16[128,512]{1,0:T(8,128)(2,1)S(1)} %slice-done.15, bf16[128,512]{1,0:T(8,128)(2,1)S(1)} %slice-done.9), kind=kOutput, calls=%fused_computation.10 | convolution fusion | flops 941621248 | bytes 6029312 | tf_op jit(solution)/shard_map/dot_general | solution.py:87
  153.0 2.6 %add_convert_fusion = bf16[512,1792]{1,0:T(8,128)(2,1)S(1)} fusion(f32[512,1792]{1,0:T(8,128)S(1)} %fusion.5, bf16[512,3712]{1,0:T(8,128)(2,1)} %constant_dynamic-update-slice_fusion, bf16[128,512]{1,0:T(8,128)(2,1)S(1)} %slice-done.3, bf16[128,512]{1,0:T(8,128)(2,1)S(1)} %slice-done.5, bf16[128,512]{1,0:T(8,128)(2,1)S(1)} %slice-done.7, ...), kind=kOutput, calls=%fused_computation | convolution fusion | flops 943456256 | bytes 7864320 | tf_op jit(solution)/shard_map/dot_general | solution.py:87
  155.9 2.5 %collective-permute-start.22 = (bf16[192,1792]{1,0:T(8,128)(2,1)S(1)}, bf16[192,1792]{1,0:T(8,128)(2,1)}, u32[]{:S(2)}, u32[]{:S(2)}) collective-permute-start(bf16[192,1792]{1,0:T(8,128)(2,1)S(1)} %pad_maximum_fusion.3), channel_id=1, source_target_pairs={{0,6},{1,7},{2,0},{3,1},{4,2},{5,3},{6,4},{7,5},{8,14},{9,15},{10,... | collective-permute-start | bytes 2064392 | tf_op jit(solution)/shard_map/ppermute | solution.py:20
  162.4 28.3 %all-to-all-done.1 = bf16[32,16,1792]{2,1,0:T(8,128)(2,1)S(1)} async-done(((bf16[32,16,1792]{2,1,0:T(8,128)(2,1)}), bf16[32,16,1792]{2,1,0:T(8,128)(2,1)S(1)}, u32[]{:S(2)}, u32[]{:S(2)}) %all-to-all-start.1) | async-done | bytes 1835040 | tf_op jit(solution)/shard_map/all_to_all | solution.py:268
  191.6 5.6 %all-to-all-start.2 = ((bf16[4,4,1792]{2,1,0:T(4,128)(2,1)}), bf16[4,4,1792]{2,1,0:T(4,128)(2,1)S(1)}, u32[]{:S(2)}, u32[]{:S(2)}) async-start(bf16[4,4,1792]{2,1,0:T(4,128)(2,1)} %reshape.351), calls=%async_computation.2 | async-start | bytes 114688 | tf_op jit(solution)/shard_map/all_to_all | solution.py:67
  198.2 5.8 %shard_map.130 = (f32[1,64,7168]{2,1,0:T(8,128)}, f32[1,64,7168]{2,1,0:T(8,128)}, f32[1,64,7168]{2,1,0:T(8,128)}) custom-call(s32[1]{0:T(128)} %bitcast.22.x_ref, bf16[192,1792]{1,0:T(8,128)(2,1)} %pad_maximum_fusion.2.r0, bf16[192,1792]{1,0:T(8,128)(2,1)} %collective-permute-done.22.r1, bf16[192,1792]{1,0:T(8,128)(2,1)} %collective-permute-done.23.r2, ...), custom_call_target="tpu_custom_call" | custom-call | flops 4128768 | bytes 11010048 | tf_op jit(solution)/shard_map/pallas_call | solution.py:282
  (282 shorter events, 81.3 us)
Async XLA Ops:
  3.9 13.4 %all-to-all-start = ((bf16[4,4,3712]{2,1,0:T(4,128)(2,1)}), bf16[4,4,3712]{2,1,0:T(4,128)(2,1)S(1)}, u32[]{:S(2)}, u32[]{:S(2)}) async-start(bf16[4,4,3712]{2,1,0:T(4,128)(2,1)} %pad_maximum_fusion.18), calls=%async_computation | async-start | bytes 237568 | tf_op jit(solution)/shard_map/all_to_all | solution.py:67
  18.3 7.8 %collective-permute-start.1 = (bf16[16,3712]{1,0:T(8,128)(2,1)S(1)}, bf16[16,3712]{1,0:T(8,128)(2,1)S(1)}, u32[]{:S(2)}, u32[]{:S(2)}) collective-permute-start(bf16[16,3712]{1,0:T(8,128)(2,1)S(1)} %reshape.341), channel_id=1, source_target_pairs={{0,128},{8,136},{16,144},{24,152},{32,160},{40,168},{48,176},{56,1... | collective-permute-start | bytes 356360 | tf_op jit(solution)/shard_map/ppermute | solution.py:26
  26.4 15.0 %collective-permute-start.3 = (bf16[64,3712]{1,0:T(8,128)(2,1)S(1)}, bf16[64,3712]{1,0:T(8,128)(2,1)S(1)}, u32[]{:S(2)}, u32[]{:S(2)}) collective-permute-start(bf16[64,3712]{1,0:T(8,128)(2,1)S(1)} %pad_maximum_fusion.6), channel_id=1, source_target_pairs={{0,56},{8,0},{16,8},{24,16},{32,24},{40,32},{48,40},{56,48},{64,12... | collective-permute-start | bytes 1425416 | tf_op jit(solution)/shard_map/ppermute | solution.py:32
  32.1 12.9 %collective-permute-start.5 = (bf16[64,3712]{1,0:T(8,128)(2,1)S(1)}, bf16[64,3712]{1,0:T(8,128)(2,1)S(1)}, u32[]{:S(2)}, u32[]{:S(2)}) collective-permute-start(bf16[64,3712]{1,0:T(8,128)(2,1)S(1)} %pad_maximum_fusion.6), channel_id=1, source_target_pairs={{0,8},{8,16},{16,24},{24,32},{32,40},{40,48},{48,56},{56,0},{64,72... | collective-permute-start | bytes 1425416 | tf_op jit(solution)/shard_map/ppermute | solution.py:32
  32.1 16.0 %collective-permute-start.7 = (bf16[192,1792]{1,0:T(8,128)(2,1)S(1)}, bf16[192,1792]{1,0:T(8,128)(2,1)S(1)}, u32[]{:S(2)}, u32[]{:S(2)}) collective-permute-start(bf16[192,1792]{1,0:T(8,128)(2,1)S(1)} %get-tuple-element.28), channel_id=1, source_target_pairs={{0,2},{1,3},{2,4},{3,5},{4,6},{5,7},{6,0},{7,1},{8,10},{9,11},{10,... | collective-permute-start | bytes 2064392 | tf_op jit(solution)/shard_map/ppermute | solution.py:20
  33.6 15.7 %collective-permute-start.8 = (bf16[192,1792]{1,0:T(8,128)(2,1)S(1)}, bf16[192,1792]{1,0:T(8,128)(2,1)S(1)}, u32[]{:S(2)}, u32[]{:S(2)}) collective-permute-start(bf16[192,1792]{1,0:T(8,128)(2,1)S(1)} %get-tuple-element.30), channel_id=1, source_target_pairs={{0,6},{1,7},{2,0},{3,1},{4,2},{5,3},{6,4},{7,5},{8,14},{9,15},{10,... | collective-permute-start | bytes 2064392 | tf_op jit(solution)/shard_map/ppermute | solution.py:20
  41.3 12.0 %collective-permute-start.4 = (bf16[64,3712]{1,0:T(8,128)(2,1)S(1)}, bf16[64,3712]{1,0:T(8,128)(2,1)S(1)}, u32[]{:S(2)}, u32[]{:S(2)}) collective-permute-start(bf16[64,3712]{1,0:T(8,128)(2,1)S(1)} %collective-permute-done.3), channel_id=1, source_target_pairs={{0,56},{8,0},{16,8},{24,16},{32,24},{40,32},{48,40},{56,48},{64,12... | collective-permute-start | bytes 1425416 | tf_op jit(solution)/shard_map/ppermute | solution.py:32
  45.0 11.7 %collective-permute-start.6 = (bf16[64,3712]{1,0:T(8,128)(2,1)S(1)}, bf16[64,3712]{1,0:T(8,128)(2,1)S(1)}, u32[]{:S(2)}, u32[]{:S(2)}) collective-permute-start(bf16[64,3712]{1,0:T(8,128)(2,1)S(1)} %collective-permute-done.5), channel_id=1, source_target_pairs={{0,8},{8,16},{16,24},{24,32},{32,40},{40,48},{48,56},{56,0},{64,72... | collective-permute-start | bytes 1425416 | tf_op jit(solution)/shard_map/ppermute | solution.py:32
  49.3 16.3 %collective-permute-start.11 = (bf16[192,1792]{1,0:T(8,128)(2,1)S(1)}, bf16[192,1792]{1,0:T(8,128)(2,1)S(1)}, u32[]{:S(2)}, u32[]{:S(2)}) collective-permute-start(bf16[192,1792]{1,0:T(8,128)(2,1)S(1)} %get-tuple-element.35), channel_id=1, source_target_pairs={{0,4},{1,5},{2,6},{3,7},{4,0},{5,1},{6,2},{7,3},{8,12},{9,13},{10,... | collective-permute-start | bytes 2064392 | tf_op jit(solution)/shard_map/ppermute | solution.py:20
  56.7 9.6 %collective-permute-start.9 = (bf16[64,3712]{1,0:T(8,128)(2,1)S(1)}, bf16[64,3712]{1,0:T(8,128)(2,1)S(1)}, u32[]{:S(2)}, u32[]{:S(2)}) collective-permute-start(bf16[64,3712]{1,0:T(8,128)(2,1)S(1)} %collective-permute-done.4), channel_id=1, source_target_pairs={{0,56},{8,0},{16,8},{24,16},{32,24},{40,32},{48,40},{56,48},{64,12... | collective-permute-start | bytes 1425416 | tf_op jit(solution)/shard_map/ppermute | solution.py:32
  57.0 10.8 %collective-permute-start.10 = (bf16[64,3712]{1,0:T(8,128)(2,1)S(1)}, bf16[64,3712]{1,0:T(8,128)(2,1)S(1)}, u32[]{:S(2)}, u32[]{:S(2)}) collective-permute-start(bf16[64,3712]{1,0:T(8,128)(2,1)S(1)} %collective-permute-done.6), channel_id=1, source_target_pairs={{0,8},{8,16},{16,24},{24,32},{32,40},{40,48},{48,56},{56,0},{64,72... | collective-permute-start | bytes 1425416 | tf_op jit(solution)/shard_map/ppermute | solution.py:32
  68.4 7.6 %collective-permute-start.13 = (bf16[32,3712]{1,0:T(8,128)(2,1)S(1)}, bf16[32,3712]{1,0:T(8,128)(2,1)S(1)}, u32[]{:S(2)}, u32[]{:S(2)}) collective-permute-start(bf16[32,3712]{1,0:T(8,128)(2,1)S(1)} %slice.332), channel_id=1, source_target_pairs={{0,8},{8,16},{16,24},{24,32},{32,40},{40,48},{48,56},{56,0},{64,72... | collective-permute-start | bytes 712712 | tf_op jit(solution)/shard_map/ppermute | solution.py:32
  79.1 12.5 %collective-permute-start.14 = (bf16[512,3712]{1,0:T(8,128)(2,1)}, bf16[512,3712]{1,0:T(8,128)(2,1)}, u32[]{:S(2)}, u32[]{:S(2)}) collective-permute-start(bf16[512,3712]{1,0:T(8,128)(2,1)} %constant_dynamic-update-slice_fusion), channel_id=1, source_target_pairs={{0,1},{1,0},{2,3},{3,2},{4,5},{5,4},{6,7},{7,6},{8,9},{9,8},{10,11... | collective-permute-start | bytes 11403272 | tf_op jit(solution)/shard_map/ppermute | solution.py:201
  104.6 10.2 %collective-permute-start.17 = (bf16[192,512]{1,0:T(8,128)(2,1)S(1)}, bf16[192,512]{1,0:T(8,128)(2,1)S(1)}, u32[]{:S(2)}, u32[]{:S(2)}) collective-permute-start(bf16[192,512]{1,0:T(8,128)(2,1)S(1)} %maximum_maximum_fusion.2), channel_id=1, source_target_pairs={{0,2},{1,3},{2,4},{3,5},{4,6},{5,7},{6,0},{7,1},{8,10},{9,11},{10,... | collective-permute-start | bytes 589832 | tf_op jit(solution)/shard_map/ppermute | solution.py:20
  105.9 9.4 %collective-permute-start.16 = (bf16[192,512]{1,0:T(8,128)(2,1)S(1)}, bf16[192,512]{1,0:T(8,128)(2,1)S(1)}, u32[]{:S(2)}, u32[]{:S(2)}) collective-permute-start(bf16[192,512]{1,0:T(8,128)(2,1)S(1)} %maximum_maximum_fusion.1), channel_id=1, source_target_pairs={{0,4},{1,5},{2,6},{3,7},{4,0},{5,1},{6,2},{7,3},{8,12},{9,13},{10,... | collective-permute-start | bytes 589832 | tf_op jit(solution)/shard_map/ppermute | solution.py:20
  107.4 11.0 %collective-permute-start.15 = (bf16[192,512]{1,0:T(8,128)(2,1)S(1)}, bf16[192,512]{1,0:T(8,128)(2,1)S(1)}, u32[]{:S(2)}, u32[]{:S(2)}) collective-permute-start(bf16[192,512]{1,0:T(8,128)(2,1)S(1)} %maximum_maximum_fusion), channel_id=1, source_target_pairs={{0,6},{1,7},{2,0},{3,1},{4,2},{5,3},{6,4},{7,5},{8,14},{9,15},{10,... | collective-permute-start | bytes 589832 | tf_op jit(solution)/shard_map/ppermute | solution.py:20
  118.7 7.7 %collective-permute-start.20 = (bf16[192,512]{1,0:T(8,128)(2,1)S(1)}, bf16[192,512]{1,0:T(8,128)(2,1)S(1)}, u32[]{:S(2)}, u32[]{:S(2)}) collective-permute-start(bf16[192,512]{1,0:T(8,128)(2,1)S(1)} %pad_maximum_fusion.15), channel_id=1, source_target_pairs={{0,6},{1,7},{2,0},{3,1},{4,2},{5,3},{6,4},{7,5},{8,14},{9,15},{10,... | collective-permute-start | bytes 589832 | tf_op jit(solution)/shard_map/ppermute | solution.py:20
  119.2 10.6 %collective-permute-start.19 = (bf16[192,512]{1,0:T(8,128)(2,1)S(1)}, bf16[192,512]{1,0:T(8,128)(2,1)S(1)}, u32[]{:S(2)}, u32[]{:S(2)}) collective-permute-start(bf16[192,512]{1,0:T(8,128)(2,1)S(1)} %pad_maximum_fusion.15), channel_id=1, source_target_pairs={{0,4},{1,5},{2,6},{3,7},{4,0},{5,1},{6,2},{7,3},{8,12},{9,13},{10,... | collective-permute-start | bytes 589832 | tf_op jit(solution)/shard_map/ppermute | solution.py:20
  121.1 10.2 %collective-permute-start.18 = (bf16[192,512]{1,0:T(8,128)(2,1)S(1)}, bf16[192,512]{1,0:T(8,128)(2,1)S(1)}, u32[]{:S(2)}, u32[]{:S(2)}) collective-permute-start(bf16[192,512]{1,0:T(8,128)(2,1)S(1)} %pad_maximum_fusion.15), channel_id=1, source_target_pairs={{0,2},{1,3},{2,4},{3,5},{4,6},{5,7},{6,0},{7,1},{8,10},{9,11},{10,... | collective-permute-start | bytes 589832 | tf_op jit(solution)/shard_map/ppermute | solution.py:20
  139.3 51.4 %all-to-all-start.1 = ((bf16[32,16,1792]{2,1,0:T(8,128)(2,1)}), bf16[32,16,1792]{2,1,0:T(8,128)(2,1)S(1)}, u32[]{:S(2)}, u32[]{:S(2)}) async-start(bf16[32,16,1792]{2,1,0:T(8,128)(2,1)} %bitcast.62), calls=%async_computation.1 | async-start | bytes 3670016 | tf_op jit(solution)/shard_map/all_to_all | solution.py:268
  155.9 42.2 %collective-permute-start.22 = (bf16[192,1792]{1,0:T(8,128)(2,1)S(1)}, bf16[192,1792]{1,0:T(8,128)(2,1)}, u32[]{:S(2)}, u32[]{:S(2)}) collective-permute-start(bf16[192,1792]{1,0:T(8,128)(2,1)S(1)} %pad_maximum_fusion.3), channel_id=1, source_target_pairs={{0,6},{1,7},{2,0},{3,1},{4,2},{5,3},{6,4},{7,5},{8,14},{9,15},{10,... | collective-permute-start | bytes 2064392 | tf_op jit(solution)/shard_map/ppermute | solution.py:20
  159.3 38.9 %collective-permute-start.23 = (bf16[192,1792]{1,0:T(8,128)(2,1)}, bf16[192,1792]{1,0:T(8,128)(2,1)}, u32[]{:S(2)}, u32[]{:S(2)}) collective-permute-start(bf16[192,1792]{1,0:T(8,128)(2,1)} %pad_maximum_fusion.4), channel_id=1, source_target_pairs={{0,4},{1,5},{2,6},{3,7},{4,0},{5,1},{6,2},{7,3},{8,12},{9,13},{10,... | collective-permute-start | bytes 2064392 | tf_op jit(solution)/shard_map/ppermute | solution.py:20
  160.7 37.5 %collective-permute-start.24 = (bf16[192,1792]{1,0:T(8,128)(2,1)}, bf16[192,1792]{1,0:T(8,128)(2,1)}, u32[]{:S(2)}, u32[]{:S(2)}) collective-permute-start(bf16[192,1792]{1,0:T(8,128)(2,1)} %pad_maximum_fusion.5), channel_id=1, source_target_pairs={{0,2},{1,3},{2,4},{3,5},{4,6},{5,7},{6,0},{7,1},{8,10},{9,11},{10,... | collective-permute-start | bytes 2064392 | tf_op jit(solution)/shard_map/ppermute | solution.py:20
  191.6 12.3 %all-to-all-start.2 = ((bf16[4,4,1792]{2,1,0:T(4,128)(2,1)}), bf16[4,4,1792]{2,1,0:T(4,128)(2,1)S(1)}, u32[]{:S(2)}, u32[]{:S(2)}) async-start(bf16[4,4,1792]{2,1,0:T(4,128)(2,1)} %reshape.351), calls=%async_computation.2 | async-start | bytes 114688 | tf_op jit(solution)/shard_map/all_to_all | solution.py:67
  (63 other events, 347.6 us)

commit v4 on v3

v4 whole, which is shorter than its diff:
```python
import functools

import jax
import jax.numpy as jnp
from jax import lax
from jax.experimental import pallas as pl
from jax.experimental.pallas import tpu as pltpu
from jax.sharding import PartitionSpec as P

NX, NY, NZ = 4, 4, 8
GROUP = 32
X_GROUPS = [[0, 2, 4, 6], [1, 3, 5, 7]]
Z_GROUPS = [[y * NZ + z for z in range(NZ)] for y in range(NY)]
Z_ORDER = ((0, 1, 7, 2), (6, 3, 5, 4))
CORE_SWAP = [(i, i ^ 1) for i in range(8)]
BF = jnp.bfloat16
F32 = jnp.float32
VMEM_LIMIT = 60 * 1024 * 1024
KERNEL_VMEM = 24 * 1024 * 1024


def shift_x(a, by):
    if by % NX == 0:
        return a
    return lax.ppermute(a, "expert", [(i, ((i // 2 + by) % NX) * 2 + i % 2) for i in range(2 * NX)])


def shift_y(a, by):
    if by == 0:
        return a
    return lax.ppermute(a, "dp", [(i, ((i // NZ + by) % NY) * NZ + i % NZ) for i in range(NY * NZ)])


def shift_z(a, by):
    if by == 0:
        return a
    return lax.ppermute(a, "dp", [(i, (i // NZ) * NZ + (i % NZ + by) % NZ) for i in range(NY * NZ)])


def gather_y(a):
    return jnp.concatenate([a] + [shift_y(a, -k) for k in range(1, NY)], axis=0)


def gather_z(a, early, late, work):
    after, before = [a], [a]
    for step in range(NZ // 2 - 1):
        if step == 2:
            (after[-1], before[-1]), early = lax.optimization_barrier(((after[-1], before[-1]), early))
        after.append(shift_z(after[-1], -1))
        before.append(shift_z(before[-1], 1))
    last, late = lax.optimization_barrier(((after[-1], before[-1]), late))
    cut = a.shape[0] // 2
    far = (shift_z(last[0][:cut], -1), shift_z(last[1][cut:], 1))
    first = after[:3] + before[1:2]
    first = jnp.concatenate([first[0], first[1], first[3], first[2]], axis=0)
    first = (first, lax.ppermute(first, "expert", CORE_SWAP))
    partial, ws = work(first, early, late)
    far, mine = lax.optimization_barrier((far, partial[0]))
    done = ([mine, partial[1]], ws)
    second = jnp.concatenate([before[2], last[0], last[1], *far], axis=0)
    return first, done, (second, lax.ppermute(second, "expert", CORE_SWAP))


def by_y_and_z(a, z):
    flat = Z_ORDER[0] + Z_ORDER[1]
    a = a.reshape(NZ, NY, -1, a.shape[-1])
    a = jnp.concatenate([a[flat.index(k)][None] for k in range(NZ)] * 2, axis=0)
    a = lax.dynamic_slice_in_dim(a, NZ - z, NZ, 0)
    return a.transpose(1, 0, 2, 3).reshape(-1, a.shape[-1])


def total(terms):
    return sum(a.astype(F32) for a in terms).astype(BF)


def exchange(a, groups):
    return lax.all_to_all(a, "dp", 0, 0, axis_index_groups=groups, tiled=True)


def across_x(a):
    return lax.all_to_all(a, "expert", 0, 0, axis_index_groups=X_GROUPS, tiled=True)


def to_slices(a):
    return a.reshape(a.shape[0], NX, -1).transpose(1, 0, 2)


def from_slices(a):
    return a.transpose(1, 0, 2).reshape(a.shape[1], -1)


def nt(a, b):
    return lax.dot_general(a, b, (((1,), (1,)), ((), ())), preferred_element_type=F32)


def tn(a, b):
    return lax.dot_general(a, b, (((0,), (0,)), ((), ())), preferred_element_type=F32)


def mm(a, b):
    return jnp.dot(a, b, preferred_element_type=F32)


def three_terms(a):
    hi = a.astype(BF)
    rest = a - hi.astype(F32)
    mid = rest.astype(BF)
    return hi, mid, (rest - mid.astype(F32)).astype(BF)


def dequantize_kernel(x_ref, gm, um, dm, gs, us, ds, w0, w1, w2, w3, keep):
    step = pl.program_id(0)
    hid, groups = gs.shape[1:]
    part = w0.shape[1]
    scales = three_terms(jnp.concatenate([gs[0], us[0], ds[0]], axis=0))
    group = lax.broadcasted_iota(jnp.int32, (groups, part), 0)
    lane_group = lax.broadcasted_iota(jnp.int32, (groups, part), 1) // GROUP
    first = lax.rem(x_ref[0] + step, NX) * (part // GROUP)
    spread = jnp.where(group == lane_group + first, 1.0, 0.0).astype(BF)
    scale = mm(scales[0], spread) + mm(scales[1], spread) + mm(scales[2], spread)
    for p, master in enumerate((gm, um, dm)):
        rows = slice(p * hid, (p + 1) * hid)
        unit = scale[rows]
        ratio = master[0] / unit
        levels = jnp.clip(jnp.floor(ratio + 0.5), -8.0, 7.0)
        weight = (levels * unit).astype(BF)
        for s, w in enumerate((w0, w1, w2, w3)):

            @pl.when(step == s)
            def _(w=w, weight=weight, rows=rows):
                w[rows] = weight

        keep[0, rows] = jnp.where((ratio > -8.5) & (ratio < 7.5), 1.0, 0.0).astype(BF)


def dequantize(x_index, masters, scales):
    _, hid, width = masters[0].shape
    part = width // NX
    grid = pltpu.PrefetchScalarGridSpec(
        num_scalar_prefetch=1,
        grid=(NX,),
        in_specs=[pl.BlockSpec((1, hid, part), lambda i, x: (0, 0, lax.rem(x[0] + i, NX)))] * 3
        + [pl.BlockSpec(scales[0].shape, lambda i, x: (0, 0, 0))] * 3,
        out_specs=[pl.BlockSpec((3 * hid, part), lambda i, x: (0, 0))] * NX
        + [pl.BlockSpec((1, 3 * hid, part), lambda i, x: (i, 0, 0))],
    )
    return pl.pallas_call(
        dequantize_kernel,
        grid_spec=grid,
        out_shape=[jax.ShapeDtypeStruct((3 * hid, part), BF)] * NX
        + [jax.ShapeDtypeStruct((NX, 3 * hid, part), BF)],
        compiler_params=pltpu.CompilerParams(vmem_limit_bytes=VMEM_LIMIT),
        cost_estimate=pl.CostEstimate(
            flops=30 * 3 * hid * width, bytes_accessed=8 * 3 * hid * width, transcendentals=0
        ),
    )(x_index, *masters, *scales)


def finish_kernel(x_ref, r0, r1, r2, r3, keep, og, ou, od):
    hid = og.shape[1]
    part = r0.shape[1]
    for s, r in enumerate((r0, r1, r2, r3)):
        col = pl.multiple_of(lax.rem(x_ref[0] + s, NX) * part, 128)
        for p, out in enumerate((og, ou, od)):
            rows = slice(p * hid, (p + 1) * hid)
            out[0, :, pl.ds(col, part)] = jnp.where(
                keep[s, rows].astype(F32) > 0.0, r[rows].astype(F32), 0.0
            )


def slot_of(found, blocks, toks, s):
    block = lax.broadcasted_iota(jnp.int32, (found.shape[0], 1), 0) // toks
    second = jnp.where(found[:, 2 * s + 1 : 2 * s + 2] > 0.5, block + blocks, -1)
    return jnp.where(found[:, 2 * s : 2 * s + 1] > 0.5, block, second)


def places(slot, slots):
    column = lax.broadcasted_iota(jnp.int32, (slot.shape[0], slots), 1)
    return jnp.where(column == slot, 1.0, 0.0)


def forward_kernel(toks, rows, pick, w0, w1, w2, w3, p0, p1, p2, p3, weight, slot):
    ws, outs = (w0, w1, w2, w3), (p0, p1, p2, p3)
    part, n, slots = w0.shape[1], rows.shape[0], weight.shape[1]
    gu = 2 * w0.shape[0] // 3
    found = mm(rows[:, 2 * part :], pick[...])
    x, g = rows[:, :part], rows[:, part : 2 * part]
    pre_gu = nt(jnp.concatenate([w[:gu] for w in ws], axis=0), x).astype(BF)
    pre_d = nt(jnp.concatenate([w[gu:] for w in ws], axis=0), g).astype(BF)
    slot[...] = jnp.full(slot.shape, -1, jnp.int32)
    for s, out in enumerate(outs):
        where = slot_of(found, n // toks, toks, s)
        slot[:, s : s + 1] = where
        place = places(where, slots)
        if s == 0:
            weight[...] = jnp.sum(place * found[:, 8:9], axis=0, keepdims=True)
        place = place.astype(BF)
        out[:gu] = mm(pre_gu[s * gu : (s + 1) * gu], place).astype(BF)
        out[gu:] = mm(pre_d[s * gu // 2 : (s + 1) * gu // 2], place).astype(BF)


def weight_grad_kernel(
    s0, s1, s2, s3, x0, x1, x2, x3, g0, g1, g2, g3, d0, d1, d2, d3, o0, o1, o2, o3, d_gu, d_h
):
    ds, outs = (d0, d1, d2, d3), (o0, o1, o2, o3)
    gu = 2 * o0.shape[0] // 3
    slots = d0.shape[1] // 4

    @pl.when(pl.program_id(0) == 0)
    def _():
        for i, slot in enumerate((s0, s1, s2, s3)):
            for s, d in enumerate(ds):
                spread = nt(
                    d[:, i * slots : (i + 1) * slots], places(slot[:, s : s + 1], slots).astype(BF)
                ).astype(BF)
                at = slice(i * spread.shape[1], (i + 1) * spread.shape[1])
                d_gu[s * gu : (s + 1) * gu, at] = spread[:gu]
                d_h[s * gu // 2 : (s + 1) * gu // 2, at] = spread[gu:]

    x = jnp.concatenate([x0[...], x1[...], x2[...], x3[...]], axis=0)
    g = jnp.concatenate([g0[...], g1[...], g2[...], g3[...]], axis=0)
    g_gu = mm(d_gu[...], x).astype(BF)
    g_h = mm(d_h[...], g).astype(BF)
    for s, out in enumerate(outs):
        out[:gu] = g_gu[s * gu : (s + 1) * gu]
        out[gu:] = g_h[s * gu // 2 : (s + 1) * gu // 2]


def weight_grads(slots, groups, delta, part):
    n, rows = groups[0].shape[0], delta[0].shape[0]
    wide = 256 if part % 256 == 0 else part
    first, second = part // wide, 2 * rows // 3
    whole = lambda a: pl.BlockSpec(a.shape, lambda i: (0, 0))
    return pl.pallas_call(
        weight_grad_kernel,
        grid=(first,),
        out_shape=[jax.ShapeDtypeStruct((rows, part), BF)] * NX,
        in_specs=[whole(a) for a in slots]
        + [pl.BlockSpec((n, wide), lambda i: (0, i))] * 4
        + [pl.BlockSpec((n, wide), lambda i: (0, first + i))] * 4
        + [whole(a) for a in delta],
        out_specs=[pl.BlockSpec((rows, wide), lambda i: (0, i))] * NX,
        scratch_shapes=[pltpu.VMEM((NX * second, 4 * n), BF), pltpu.VMEM((NX * second // 2, 4 * n), BF)],
        compiler_params=pltpu.CompilerParams(vmem_limit_bytes=VMEM_LIMIT),
        cost_estimate=pl.CostEstimate(
            flops=2 * rows * NX * part * 4 * n,
            bytes_accessed=2 * (8 * n * part + 2 * NX * rows * part),
            transcendentals=0,
        ),
    )(*slots, *groups, *groups, *delta)


def input_grad(half, slot, ds, ws):
    gu = 2 * ws[0].shape[0] // 3
    slots = ds[0].shape[1] // 2
    spread = jnp.concatenate(
        [
            nt(places(slot[:, s : s + 1], slots).astype(BF), d[:gu, half * slots : (half + 1) * slots])
            for s, d in enumerate(ds)
        ],
        axis=1,
    ).astype(BF)
    return mm(spread, jnp.concatenate([w[:gu] for w in ws], axis=0))


def theirs_kernel(slot, d0, d1, d2, d3, w0, w1, w2, w3, out):
    out[...] = input_grad(1, slot, (d0, d1, d2, d3), (w0, w1, w2, w3)).astype(BF)


def ours_kernel(slot, d0, d1, d2, d3, w0, w1, w2, w3, theirs, l0, l1, l2, l3, right):
    grad = input_grad(0, slot, (d0, d1, d2, d3), (w0, w1, w2, w3))
    grad = (grad + theirs[...].astype(F32)).astype(BF)
    cut = l0.shape[1]
    unit = grad.shape[0] // (NY * NZ)
    for y, left in enumerate((l0, l1, l2, l3)):
        left[...] = grad[y * NZ * unit : (y + 1) * NZ * unit, :cut]
        for z in range(NZ):
            row = (y * NZ + z) * unit
            right[z, y * unit : (y + 1) * unit] = grad[row : row + unit, cut:]


def local_call(kernel, out_shape, cost, scalars=0, limit=KERNEL_VMEM):
    vmem = pl.BlockSpec(memory_space=pltpu.VMEM)
    smem = pl.BlockSpec(memory_space=pltpu.SMEM)

    def call(*args):
        return pl.pallas_call(
            kernel,
            out_shape=out_shape,
            in_specs=[smem] * scalars + [vmem] * (len(args) - scalars),
            out_specs=[vmem] * len(out_shape),
            compiler_params=pltpu.CompilerParams(vmem_limit_bytes=limit),
            cost_estimate=pl.CostEstimate(flops=cost[0], bytes_accessed=cost[1], transcendentals=0),
        )(*args)

    return call


def per_device(
    tokens,
    grad_out,
    expert_ids,
    gate_values,
    gate_master,
    gate_scale,
    up_master,
    up_scale,
    down_master,
    down_scale,
):
    experts = lax.axis_size("expert")
    expert = lax.axis_index("expert")
    toks, width = tokens.shape
    hid = gate_master.shape[1]
    part = width // NX
    cap = toks // 2
    x_index = (expert // 2).reshape(1)

    named = expert_ids[:, :, None] == jnp.arange(experts, dtype=jnp.int32)
    factor = jnp.sum(jnp.where(named, gate_values[:, :, None], 0.0), axis=1)
    member = jnp.any(named, axis=1)
    rank = jnp.cumsum(member.astype(jnp.int32), axis=0) - 1
    f_hi = lax.reduce_precision(factor, 8, 7)
    f_mid = lax.reduce_precision(factor - f_hi, 8, 7)
    cols = [f_hi, f_mid, factor - f_hi - f_mid]
    cols += [jnp.where(member & (rank == slot), 1.0, 0.0) for slot in range(cap)]
    cols = jnp.concatenate(cols, axis=1).astype(BF)
    cols = jnp.pad(cols, ((0, 0), (0, 128 - cols.shape[1])))
    payload = jnp.concatenate(
        [to_slices(tokens), to_slices(grad_out), jnp.broadcast_to(cols, (NX,) + cols.shape)], axis=2
    )
    mine = across_x(payload).reshape(NX * toks, -1)
    *w_mine, keep = dequantize(
        x_index, (gate_master, up_master, down_master), (gate_scale, up_scale, down_scale)
    )
    own, w_mine = lax.optimization_barrier((gather_y(mine), w_mine))
    w = [shift_x(a, s) if s != 2 else a for s, a in enumerate(w_mine)]
    w = lax.optimization_barrier(w)
    n = NY * NZ * NX * toks // 2
    slots = n // toks * cap

    row = jnp.arange(128, dtype=jnp.int32)[:, None]
    col = jnp.arange(128, dtype=jnp.int32)[None, :]
    owner = (col // cap * (experts - 2) + expert) % experts
    pick = (col < cap * NX) & (row == owner + (3 + col % cap) * experts)
    pick |= (col == cap * NX) & (row % experts == expert) & (row < 3 * experts)
    pick = pick.astype(BF)
    row_bytes = 2 * n * mine.shape[1]
    w_bytes = 2 * 3 * hid * width
    forward = local_call(
        functools.partial(forward_kernel, toks),
        [jax.ShapeDtypeStruct((3 * hid, slots), BF)] * NX
        + [jax.ShapeDtypeStruct((1, slots), F32), jax.ShapeDtypeStruct((n, 128), jnp.int32)],
        (2 * 3 * hid * width * n, row_bytes + w_bytes),
    )

    def work(rows, early, late):
        ws = (w[0], early[0], late, early[1])
        return [forward(a, pick, *ws) for a in rows], ws

    first, (partial, w), second = gather_z(own, (w[1], w[3]), shift_x(w[2], 2), work)
    partial = partial + [forward(a, pick, *w) for a in second]
    groups = [first[0], second[0], first[1], second[1]]
    partial = [partial[i] for i in (0, 2, 1, 3)]
    weight = jnp.concatenate([p[NX] for p in partial], axis=1)
    pre = [shift_x(jnp.concatenate([p[s] for p in partial], axis=1), -s) for s in range(NX)]
    slot = [p[NX + 1] for p in partial]
    by_half = [jnp.where(a >= 0, a + i % 2 * slots, -1) for i, a in enumerate(slot)]
    z = lax.axis_index("dp") % NZ
    by_half = [by_y_and_z(jnp.concatenate(by_half[i : i + 2], axis=0), z) for i in (0, 2)]

    pre = sum(a.astype(F32) for a in pre)

    gate_pre, up_pre = pre[:hid], pre[hid : 2 * hid]
    delta_hidden = jnp.where(weight > 0.0, pre[2 * hid :] * weight, 0.0)
    sig_gate = jax.nn.sigmoid(gate_pre)
    silu_gate = gate_pre * sig_gate
    hidden = jnp.where(weight > 0.0, silu_gate * up_pre * weight, 0.0)
    delta_up = delta_hidden * silu_gate
    delta_gate = delta_hidden * up_pre * sig_gate * (1.0 + gate_pre * (1.0 - sig_gate))
    delta = jnp.concatenate([delta_gate, delta_up, hidden], axis=0).astype(BF)
    delta = [shift_x(delta, s) for s in range(NX)]
    half = 2 * n
    theirs = local_call(
        theirs_kernel,
        [jax.ShapeDtypeStruct((half, part), BF)],
        (4 * hid * width * half, row_bytes + w_bytes),
    )(by_half[1], *delta, *w)[0]
    theirs = lax.ppermute(theirs, "expert", CORE_SWAP)
    g_all = weight_grads(slot, groups, delta, part)
    cut = part * 5 // 7
    unit = NX * toks
    *left, right = local_call(
        ours_kernel,
        [
            *[jax.ShapeDtypeStruct((NZ * unit, cut), BF)] * NY,
            jax.ShapeDtypeStruct((NZ, NY * unit, part - cut), BF),
        ],
        (4 * hid * width * half, 2 * row_bytes + w_bytes),
    )(by_half[0], *delta, *w, theirs)
    right = exchange(right, Z_GROUPS)
    left, _ = lax.optimization_barrier(([shift_y(left[k], k) for k in range(NY)], g_all))
    near, third = lax.optimization_barrier(((shift_x(g_all[1], -1), shift_x(g_all[3], -3)), g_all[2]))
    left = total(left).reshape(NZ, unit, cut)
    right = total(list(right)).reshape(NY, unit, part - cut)
    left = total(list(exchange(left, Z_GROUPS)))
    right = total([shift_y(right[k], k) for k in range(NY)])
    grad_x = jnp.concatenate([left, right], axis=1)
    third = shift_x(third, -2)
    grad_tokens = from_slices(across_x(grad_x.reshape(NX, toks, part)))

    g_all = (g_all[0], near[0], third, near[1])
    grads = local_call(
        finish_kernel,
        [jax.ShapeDtypeStruct((1, hid, width), F32)] * 3,
        (3 * 3 * hid * width, 8 * 3 * hid * width),
        scalars=1,
    )(x_index, *g_all, keep)
    return (grad_tokens, *grads)


def solution(mesh):
    rows = P(("dp", "expert"), None)
    weights = P("expert", "dp", None)
    return jax.shard_map(
        per_device,
        mesh=mesh,
        in_specs=(rows,) * 4 + (weights,) * 6,
        out_specs=(rows,) + (weights,) * 3,
        check_vma=False,
    )
```

time: 206 us -> 187 us (0.908)
  matrix products: 40.2 us -> 0 us
  Pallas kernels: 13.6 us -> 37.7 us
  starting transfers between devices: 54.9 us -> 70.1 us
  waiting for transfers between devices: 69.7 us -> 57.3 us
  local copies, waits for them, and re-layouts: 13.4 us -> 10.3 us
  other arithmetic: 10.7 us -> 7.87 us
    dot_general x48 -> x0, matrix products: 40.2 us -> none  [the longest x26 20.9 us: mm(): return jnp.dot(a, b, preferred_element_type=F32)]
    all_to_all x1 -> x2, waiting for transfers between devices: 28.3 us -> 0.01 us  [exchange(): return lax.all_to_all(a, 'dp', 0, 0, axis_index_groups=groups, tiled=True)]
    pallas_call x2 -> x9, Pallas kernels: 13.6 us -> 37.7 us  [the longest x7 19.4 us: call(): pl.pallas_call(kernel, out_shape=out_shape, in_specs=[smem] * scalars + [...]
    ppermute x12, waiting for transfers between devices: 18.9 us -> 31.6 us  [shift_x(): lax.ppermute(a, 'expert', [(i, (i // 2 + by) % NX * 2 + i % 2) for i in r...]
    ppermute x3 -> x9, starting transfers between devices: 5.17 us -> 12.5 us  [shift_y(): lax.ppermute(a, 'dp', [(i, (i // NZ + by) % NY * NZ + i % NZ) for i in ra...]
    ppermute x8, waiting for transfers between devices: 18.9 us -> 13.6 us  [shift_z(): lax.ppermute(a, 'dp', [(i, i // NZ * NZ + (i % NZ + by) % NZ) for i in ra...]
    all_to_all x1 -> x2, starting transfers between devices: 6.44 us -> 10.9 us  [exchange(): return lax.all_to_all(a, 'dp', 0, 0, axis_index_groups=groups, tiled=True)]
    all_to_all x2, waiting for transfers between devices: 0.01 us -> 4.45 us  [across_x(): lax.all_to_all(a, 'expert', 0, 0, axis_index_groups=X_GROUPS, tiled=True)]
  transfers between devices with their start and end apart: 28 -> 36, of which waited for: 20 -> 23; matrix products, arithmetic and copies ran while one was open for 20% -> 7% of each run, Pallas kernels for 7% -> 17%
where the time goes in v4:
time: 187 us; the launch traced here: 185 us
  starting transfers between devices  70.1 us (37%)
  waiting for transfers between devices  57.3 us (31%)
  Pallas kernels  37.7 us (20%)
  local copies, waits for them, and re-layouts  10.3 us (6%)
  other arithmetic  7.87 us (4%)
    ppermute x12, waiting for transfers between devices, shift_x(): lax.ppermute(a, 'expert', [(i, (i // 2 + by) % NX * 2 + i % 2) for i in r...  31.6 us
    pallas_call x7, Pallas kernels, call(): pl.pallas_call(kernel, out_shape=out_shape, in_specs=[smem] * scalars + [...  19.4 us
    ppermute x12, starting transfers between devices, shift_x(): lax.ppermute(a, 'expert', [(i, (i // 2 + by) % NX * 2 + i % 2) for i in r...  18.5 us
    ppermute x8, starting transfers between devices, shift_z(): lax.ppermute(a, 'dp', [(i, i // NZ * NZ + (i % NZ + by) % NZ) for i in ra...  16.6 us
    ppermute x8, waiting for transfers between devices, shift_z(): lax.ppermute(a, 'dp', [(i, i // NZ * NZ + (i % NZ + by) % NZ) for i in ra...  13.6 us
    ppermute x9, starting transfers between devices, shift_y(): lax.ppermute(a, 'dp', [(i, (i // NZ + by) % NY * NZ + i % NZ) for i in ra...  12.5 us
    all_to_all x2, starting transfers between devices, across_x(): lax.all_to_all(a, 'expert', 0, 0, axis_index_groups=X_GROUPS, tiled=True)  11.2 us
    all_to_all x2, starting transfers between devices, exchange(): return lax.all_to_all(a, 'dp', 0, 0, axis_index_groups=groups, tiled=True)  10.9 us
  transfers between devices with their start and end apart: 36, of which 23 were waited for; matrix products, arithmetic and copies ran while one was open for 7% of the time, Pallas kernels for 17%

profile of v4, /device:TPU:2, one launch (start us, length us, event | category | flops | bytes accessed | tf_op | source)
XLA Modules:
  0.0 184.6 jit_solution(708598587462353125)
XLA Ops:
  3.9 5.6 %all-to-all-start = ((bf16[4,4,3712]{2,1,0:T(4,128)(2,1)}), bf16[4,4,3712]{2,1,0:T(4,128)(2,1)S(1)}, u32[]{:S(2)}, u32[]{:S(2)}) async-start(bf16[4,4,3712]{2,1,0:T(4,128)(2,1)} %pad_maximum_fusion.5), calls=%async_computation | async-start | bytes 237568 | tf_op jit(solution)/shard_map/all_to_all | solution.py:81
  9.5 4.5 %all-to-all-done = bf16[4,4,3712]{2,1,0:T(4,128)(2,1)S(1)} async-done(((bf16[4,4,3712]{2,1,0:T(4,128)(2,1)}), bf16[4,4,3712]{2,1,0:T(4,128)(2,1)S(1)}, u32[]{:S(2)}, u32[]{:S(2)}) %all-to-all-start) | async-done | bytes 118816 | tf_op jit(solution)/shard_map/all_to_all | solution.py:81
  17.9 8.6 %shard_map.129 = (bf16[192,1792]{1,0:T(8,128)(2,1)}, bf16[192,1792]{1,0:T(8,128)(2,1)}, bf16[192,1792]{1,0:T(8,128)(2,1)}, bf16[192,1792]{1,0:T(8,128)(2,1)}, bf16[4,192,1792]{2,1,0:T(8,128)(2,1)}) custom-call(s32[1]{0:T(128)} %bitcast.4.x_ref, f32[1,64,7168]{2,1,0:T(8,128)} %gm.1, f32[1,64,7168]{2,1,0:T(8,128)} %um.1, f32[1,64,7168]{2,1,0:T(8,128)} %dm.1, ...), custom_call_target="tpu_custom_call" | custom-call | flops 41287680 | bytes 11010048 | tf_op jit(solution)/shard_map/pallas_call | solution.py:147
  26.6 5.9 %collective-permute-start.3 = (bf16[64,3712]{1,0:T(8,128)(2,1)S(1)}, bf16[64,3712]{1,0:T(8,128)(2,1)S(1)}, u32[]{:S(2)}, u32[]{:S(2)}) collective-permute-start(bf16[64,3712]{1,0:T(8,128)(2,1)S(1)} %pad_maximum_fusion), channel_id=1, source_target_pairs={{0,56},{8,0},{16,8},{24,16},{32,24},{40,32},{48,40},{56,48},{64,12... | collective-permute-start | bytes 1425416 | tf_op jit(solution)/shard_map/ppermute | solution.py:37
  35.6 4.8 %collective-permute-done.3 = bf16[64,3712]{1,0:T(8,128)(2,1)S(1)} collective-permute-done((bf16[64,3712]{1,0:T(8,128)(2,1)S(1)}, bf16[64,3712]{1,0:T(8,128)(2,1)S(1)}, u32[]{:S(2)}, u32[]{:S(2)}) %collective-permute-start.3) | collective-permute-done | bytes 475168 | tf_op jit(solution)/shard_map/ppermute | solution.py:37
  40.4 3.7 %collective-permute-start.4 = (bf16[64,3712]{1,0:T(8,128)(2,1)S(1)}, bf16[64,3712]{1,0:T(8,128)(2,1)S(1)}, u32[]{:S(2)}, u32[]{:S(2)}) collective-permute-start(bf16[64,3712]{1,0:T(8,128)(2,1)S(1)} %collective-permute-done.3), channel_id=1, source_target_pairs={{0,56},{8,0},{16,8},{24,16},{32,24},{40,32},{48,40},{56,48},{64,12... | collective-permute-start | bytes 1425416 | tf_op jit(solution)/shard_map/ppermute | solution.py:37
  47.6 4.4 %collective-permute-start.11 = (bf16[192,1792]{1,0:T(8,128)(2,1)S(1)}, bf16[192,1792]{1,0:T(8,128)(2,1)S(1)}, u32[]{:S(2)}, u32[]{:S(2)}) collective-permute-start(bf16[192,1792]{1,0:T(8,128)(2,1)S(1)} %copy-done.13), channel_id=1, source_target_pairs={{0,4},{1,5},{2,6},{3,7},{4,0},{5,1},{6,2},{7,3},{8,12},{9,13},{10,... | collective-permute-start | bytes 2064392 | tf_op jit(solution)/shard_map/ppermute | solution.py:25
  52.0 3.1 %collective-permute-done.6 = bf16[64,3712]{1,0:T(8,128)(2,1)S(1)} collective-permute-done((bf16[64,3712]{1,0:T(8,128)(2,1)S(1)}, bf16[64,3712]{1,0:T(8,128)(2,1)S(1)}, u32[]{:S(2)}, u32[]{:S(2)}) %collective-permute-start.6) | collective-permute-done | bytes 475168 | tf_op jit(solution)/shard_map/ppermute | solution.py:37
  55.1 3.2 %collective-permute-start.9 = (bf16[64,3712]{1,0:T(8,128)(2,1)S(1)}, bf16[64,3712]{1,0:T(8,128)(2,1)S(1)}, u32[]{:S(2)}, u32[]{:S(2)}) collective-permute-start(bf16[64,3712]{1,0:T(8,128)(2,1)S(1)} %collective-permute-done.4), channel_id=1, source_target_pairs={{0,56},{8,0},{16,8},{24,16},{32,24},{40,32},{48,40},{56,48},{64,12... | collective-permute-start | bytes 1425416 | tf_op jit(solution)/shard_map/ppermute | solution.py:37
  60.0 3.8 %collective-permute-done.11.w2 = bf16[192,1792]{1,0:T(8,128)(2,1)S(1)} collective-permute-done((bf16[192,1792]{1,0:T(8,128)(2,1)S(1)}, bf16[192,1792]{1,0:T(8,128)(2,1)S(1)}, u32[]{:S(2)}, u32[]{:S(2)}) %collective-permute-start.11) | collective-permute-done | bytes 688160 | tf_op jit(solution)/shard_map/ppermute | solution.py:25
  66.6 3.7 %collective-permute-start.12 = (bf16[32,3712]{1,0:T(8,128)(2,1)S(1)}, bf16[32,3712]{1,0:T(8,128)(2,1)S(1)}, u32[]{:S(2)}, u32[]{:S(2)}) collective-permute-start(bf16[32,3712]{1,0:T(8,128)(2,1)S(1)} %slice.143), channel_id=1, source_target_pairs={{0,56},{8,0},{16,8},{24,16},{32,24},{40,32},{48,40},{56,48},{64,12... | collective-permute-start | bytes 712712 | tf_op jit(solution)/shard_map/ppermute | solution.py:37
  74.0 3.7 %collective-permute-done.13 = bf16[32,3712]{1,0:T(8,128)(2,1)S(1)} collective-permute-done((bf16[32,3712]{1,0:T(8,128)(2,1)S(1)}, bf16[32,3712]{1,0:T(8,128)(2,1)S(1)}, u32[]{:S(2)}, u32[]{:S(2)}) %collective-permute-start.13) | collective-permute-done | bytes 237600 | tf_op jit(solution)/shard_map/ppermute | solution.py:37
  82.0 2.7 %shard_map.132 = (bf16[192,128]{1,0:T(8,128)(2,1)S(1)}, bf16[192,128]{1,0:T(8,128)(2,1)S(1)}, bf16[192,128]{1,0:T(8,128)(2,1)S(1)}, bf16[192,128]{1,0:T(8,128)(2...) custom-call(bf16[256,3712]{1,0:T(8,128)(2,1)} %collective-permute-done.14.rows.x2.g2, ...), custom_call_target="tpu_custom_call" | custom-call | flops 704643072 | bytes 4653056 | tf_op jit(solution)/shard_map/pallas_call | solution.py:287
  91.5 7.7 %collective-permute-done.16 = bf16[192,512]{1,0:T(8,128)(2,1)S(1)} collective-permute-done((bf16[192,512]{1,0:T(8,128)(2,1)S(1)}, bf16[192,512]{1,0:T(8,128)(2,1)S(1)}, u32[]{:S(2)}, u32[]{:S(2)}) %collective-permute-start.16) | collective-permute-done | bytes 196640 | tf_op jit(solution)/shard_map/ppermute | solution.py:25
  105.6 3.6 %collective-permute-done.19.d1 = bf16[192,512]{1,0:T(8,128)(2,1)S(1)} collective-permute-done((bf16[192,512]{1,0:T(8,128)(2,1)S(1)}, bf16[192,512]{1,0:T(8,128)(2,1)S(1)}, u32[]{:S(2)}, u32[]{:S(2)}) %collective-permute-start.19) | collective-permute-done | bytes 196640 | tf_op jit(solution)/shard_map/ppermute | solution.py:25
  109.2 3.0 %collective-permute-done.20.d2 = bf16[192,512]{1,0:T(8,128)(2,1)S(1)} collective-permute-done((bf16[192,512]{1,0:T(8,128)(2,1)S(1)}, bf16[192,512]{1,0:T(8,128)(2,1)S(1)}, u32[]{:S(2)}, u32[]{:S(2)}) %collective-permute-start.20) | collective-permute-done | bytes 196640 | tf_op jit(solution)/shard_map/ppermute | solution.py:25
  112.2 2.9 %collective-permute-done.21.d3 = bf16[192,512]{1,0:T(8,128)(2,1)S(1)} collective-permute-done((bf16[192,512]{1,0:T(8,128)(2,1)S(1)}, bf16[192,512]{1,0:T(8,128)(2,1)S(1)}, u32[]{:S(2)}, u32[]{:S(2)}) %collective-permute-start.21) | collective-permute-done | bytes 196640 | tf_op jit(solution)/shard_map/ppermute | solution.py:25
  117.2 3.5 %collective-permute-done.22.theirs = bf16[512,1792]{1,0:T(8,128)(2,1)S(1)} collective-permute-done((bf16[512,1792]{1,0:T(8,128)(2,1)S(1)}, bf16[512,1792]{1,0:T(8,128)(2,1)S(1)}, u32[]{:S(2)}, u32[]{:S(2)}) %collective-permute-start.22) | collective-permute-done | bytes 1835040 | tf_op jit(solution)/shard_map/ppermute | solution.py:389
  123.9 4.2 %all-to-all-start.2 = ((bf16[8,64,512]{2,1,0:T(8,128)(2,1)}), bf16[8,64,512]{2,1,0:T(8,128)(2,1)}, u32[]{:S(2)}, u32[]{:S(2)}) async-start(bf16[8,64,512]{2,1,0:T(8,128)(2,1)} %get-tuple-element.140), calls=%async_computation.2 | async-start | bytes 1048576 | tf_op jit(solution)/shard_map/all_to_all | solution.py:77
  132.8 9.7 %shard_map.136 = (bf16[192,1792]{1,0:T(8,128)(2,1)}, bf16[192,1792]{1,0:T(8,128)(2,1)}, bf16[192,1792]{1,0:T(8,128)(2,1)}, bf16[192,1792]{1,0:T(8,128)(2,1)}) custom-call(s32[256,128]{1,0:T(8,128)} %copy-done.7, s32[256,128]{1,0:T(8,128)} %copy-done.8, s32[256,128]{1,0:T(8,128)} %copy-done.9, s32[256,128]{1,0:T(8,128)} %copy-done.10, ...), custom_call_target="tpu_custom_call" | custom-call | flops 2818572288 | bytes 12845056 | tf_op jit(solution)/shard_map/pallas_call | solution.py:234
  149.1 6.7 %all-to-all-start.1 = ((bf16[8,16,1280]{2,1,0:T(8,128)(2,1)}), bf16[8,16,1280]{2,1,0:T(8,128)(2,1)}, u32[]{:S(2)}, u32[]{:S(2)}) async-start(bf16[8,16,1280]{2,1,0:T(8,128)(2,1)} %bitcast.89), calls=%async_computation.1 | async-start | bytes 655360 | tf_op jit(solution)/shard_map/all_to_all | solution.py:77
  155.8 3.9 %collective-permute-done.29.r1 = bf16[192,1792]{1,0:T(8,128)(2,1)} collective-permute-done((bf16[192,1792]{1,0:T(8,128)(2,1)}, bf16[192,1792]{1,0:T(8,128)(2,1)}, u32[]{:S(2)}, u32[]{:S(2)}) %collective-permute-start.29) | collective-permute-done | bytes 688160 | tf_op jit(solution)/shard_map/ppermute | solution.py:25
  172.2 5.7 %all-to-all-start.3 = ((bf16[4,4,1792]{2,1,0:T(4,128)(2,1)}), bf16[4,4,1792]{2,1,0:T(4,128)(2,1)S(1)}, u32[]{:S(2)}, u32[]{:S(2)}) async-start(bf16[4,4,1792]{2,1,0:T(4,128)(2,1)} %reshape.245), calls=%async_computation.3 | async-start | bytes 114688 | tf_op jit(solution)/shard_map/all_to_all | solution.py:81
  179.4 4.6 %shard_map.137 = (f32[1,64,7168]{2,1,0:T(8,128)}, f32[1,64,7168]{2,1,0:T(8,128)}, f32[1,64,7168]{2,1,0:T(8,128)}) custom-call(s32[1]{0:T(128)} %bitcast.4.x_ref, bf16[192,1792]{1,0:T(8,128)(2,1)S(1)} %copy-done.6, bf16[192,1792]{1,0:T(8,128)(2,1)} %collective-permute-done.29.r1, bf16[192,1792]{1,0:T(8,128)(2,1)} %collective-permute-done.31.r2, ...), custom_call_target="tpu_custom_call" | custom-call | flops 4128768 | bytes 11010048 | tf_op jit(solution)/shard_map/pallas_call | solution.py:287
  (169 shorter events, 70.1 us)
Async XLA Ops:
  3.9 10.0 %all-to-all-start = ((bf16[4,4,3712]{2,1,0:T(4,128)(2,1)}), bf16[4,4,3712]{2,1,0:T(4,128)(2,1)S(1)}, u32[]{:S(2)}, u32[]{:S(2)}) async-start(bf16[4,4,3712]{2,1,0:T(4,128)(2,1)} %pad_maximum_fusion.5), calls=%async_computation | async-start | bytes 237568 | tf_op jit(solution)/shard_map/all_to_all | solution.py:81
  13.9 12.6 %collective-permute-start = (bf16[16,3712]{1,0:T(8,128)(2,1)S(1)}, bf16[16,3712]{1,0:T(8,128)(2,1)S(1)}, u32[]{:S(2)}, u32[]{:S(2)}) collective-permute-start(bf16[16,3712]{1,0:T(8,128)(2,1)S(1)} %reshape.240), channel_id=1, source_target_pairs={{0,192},{8,200},{16,208},{24,216},{32,224},{40,232},{48,240},{56,2... | collective-permute-start | bytes 356360 | tf_op jit(solution)/shard_map/ppermute | solution.py:31
  16.3 10.2 %collective-permute-start.1 = (bf16[16,3712]{1,0:T(8,128)(2,1)S(1)}, bf16[16,3712]{1,0:T(8,128)(2,1)S(1)}, u32[]{:S(2)}, u32[]{:S(2)}) collective-permute-start(bf16[16,3712]{1,0:T(8,128)(2,1)S(1)} %reshape.240), channel_id=1, source_target_pairs={{0,128},{8,136},{16,144},{24,152},{32,160},{40,168},{48,176},{56,1... | collective-permute-start | bytes 356360 | tf_op jit(solution)/shard_map/ppermute | solution.py:31
  26.6 13.8 %collective-permute-start.3 = (bf16[64,3712]{1,0:T(8,128)(2,1)S(1)}, bf16[64,3712]{1,0:T(8,128)(2,1)S(1)}, u32[]{:S(2)}, u32[]{:S(2)}) collective-permute-start(bf16[64,3712]{1,0:T(8,128)(2,1)S(1)} %pad_maximum_fusion), channel_id=1, source_target_pairs={{0,56},{8,0},{16,8},{24,16},{32,24},{40,32},{48,40},{56,48},{64,12... | collective-permute-start | bytes 1425416 | tf_op jit(solution)/shard_map/ppermute | solution.py:37
  32.5 11.6 %collective-permute-start.5 = (bf16[64,3712]{1,0:T(8,128)(2,1)S(1)}, bf16[64,3712]{1,0:T(8,128)(2,1)S(1)}, u32[]{:S(2)}, u32[]{:S(2)}) collective-permute-start(bf16[64,3712]{1,0:T(8,128)(2,1)S(1)} %pad_maximum_fusion), channel_id=1, source_target_pairs={{0,8},{8,16},{16,24},{24,32},{32,40},{40,48},{48,56},{56,0},{64,72... | collective-permute-start | bytes 1425416 | tf_op jit(solution)/shard_map/ppermute | solution.py:37
  32.6 14.9 %collective-permute-start.7 = (bf16[192,1792]{1,0:T(8,128)(2,1)}, bf16[192,1792]{1,0:T(8,128)(2,1)S(1)}, u32[]{:S(2)}, u32[]{:S(2)}) collective-permute-start(bf16[192,1792]{1,0:T(8,128)(2,1)} %get-tuple-element.82), channel_id=1, source_target_pairs={{0,2},{1,3},{2,4},{3,5},{4,6},{5,7},{6,0},{7,1},{8,10},{9,11},{10,... | collective-permute-start | bytes 2064392 | tf_op jit(solution)/shard_map/ppermute | solution.py:25
  33.0 14.7 %collective-permute-start.8 = (bf16[192,1792]{1,0:T(8,128)(2,1)}, bf16[192,1792]{1,0:T(8,128)(2,1)S(1)}, u32[]{:S(2)}, u32[]{:S(2)}) collective-permute-start(bf16[192,1792]{1,0:T(8,128)(2,1)} %get-tuple-element.84), channel_id=1, source_target_pairs={{0,6},{1,7},{2,0},{3,1},{4,2},{5,3},{6,4},{7,5},{8,14},{9,15},{10,... | collective-permute-start | bytes 2064392 | tf_op jit(solution)/shard_map/ppermute | solution.py:25
  40.4 11.6 %collective-permute-start.4 = (bf16[64,3712]{1,0:T(8,128)(2,1)S(1)}, bf16[64,3712]{1,0:T(8,128)(2,1)S(1)}, u32[]{:S(2)}, u32[]{:S(2)}) collective-permute-start(bf16[64,3712]{1,0:T(8,128)(2,1)S(1)} %collective-permute-done.3), channel_id=1, source_target_pairs={{0,56},{8,0},{16,8},{24,16},{32,24},{40,32},{48,40},{56,48},{64,12... | collective-permute-start | bytes 1425416 | tf_op jit(solution)/shard_map/ppermute | solution.py:37
  44.1 11.0 %collective-permute-start.6 = (bf16[64,3712]{1,0:T(8,128)(2,1)S(1)}, bf16[64,3712]{1,0:T(8,128)(2,1)S(1)}, u32[]{:S(2)}, u32[]{:S(2)}) collective-permute-start(bf16[64,3712]{1,0:T(8,128)(2,1)S(1)} %collective-permute-done.5), channel_id=1, source_target_pairs={{0,8},{8,16},{16,24},{24,32},{32,40},{40,48},{48,56},{56,0},{64,72... | collective-permute-start | bytes 1425416 | tf_op jit(solution)/shard_map/ppermute | solution.py:37
  47.6 16.2 %collective-permute-start.11 = (bf16[192,1792]{1,0:T(8,128)(2,1)S(1)}, bf16[192,1792]{1,0:T(8,128)(2,1)S(1)}, u32[]{:S(2)}, u32[]{:S(2)}) collective-permute-start(bf16[192,1792]{1,0:T(8,128)(2,1)S(1)} %copy-done.13), channel_id=1, source_target_pairs={{0,4},{1,5},{2,6},{3,7},{4,0},{5,1},{6,2},{7,3},{8,12},{9,13},{10,... | collective-permute-start | bytes 2064392 | tf_op jit(solution)/shard_map/ppermute | solution.py:25
  55.1 10.6 %collective-permute-start.9 = (bf16[64,3712]{1,0:T(8,128)(2,1)S(1)}, bf16[64,3712]{1,0:T(8,128)(2,1)S(1)}, u32[]{:S(2)}, u32[]{:S(2)}) collective-permute-start(bf16[64,3712]{1,0:T(8,128)(2,1)S(1)} %collective-permute-done.4), channel_id=1, source_target_pairs={{0,56},{8,0},{16,8},{24,16},{32,24},{40,32},{48,40},{56,48},{64,12... | collective-permute-start | bytes 1425416 | tf_op jit(solution)/shard_map/ppermute | solution.py:37
  59.2 22.7 %collective-permute-start.14 = (bf16[256,3712]{1,0:T(8,128)(2,1)}, bf16[256,3712]{1,0:T(8,128)(2,1)}, u32[]{:S(2)}, u32[]{:S(2)}) collective-permute-start(bf16[256,3712]{1,0:T(8,128)(2,1)} %constant_dynamic-update-slice_fusion.rows.x0.g0), channel_id=1, source_target_pairs={{0,1},{1,0},{2,3},{3,2},{4,5},{5,4},{6,7},{7,6},{8,9},{9,8},{10,11... | collective-permute-start | bytes 5701640 | tf_op jit(solution)/shard_map/ppermute | solution.py:56
  87.6 11.6 %collective-permute-start.16 = (bf16[192,512]{1,0:T(8,128)(2,1)S(1)}, bf16[192,512]{1,0:T(8,128)(2,1)S(1)}, u32[]{:S(2)}, u32[]{:S(2)}) collective-permute-start(bf16[192,512]{1,0:T(8,128)(2,1)S(1)} %pad_maximum_fusion.1), channel_id=1, source_target_pairs={{0,6},{1,7},{2,0},{3,1},{4,2},{5,3},{6,4},{7,5},{8,14},{9,15},{10,... | collective-permute-start | bytes 589832 | tf_op jit(solution)/shard_map/ppermute | solution.py:25
  89.7 11.4 %collective-permute-start.18 = (bf16[192,512]{1,0:T(8,128)(2,1)S(1)}, bf16[192,512]{1,0:T(8,128)(2,1)S(1)}, u32[]{:S(2)}, u32[]{:S(2)}) collective-permute-start(bf16[192,512]{1,0:T(8,128)(2,1)S(1)} %pad_maximum_fusion.3), channel_id=1, source_target_pairs={{0,2},{1,3},{2,4},{3,5},{4,6},{5,7},{6,0},{7,1},{8,10},{9,11},{10,... | collective-permute-start | bytes 589832 | tf_op jit(solution)/shard_map/ppermute | solution.py:25
  105.1 10.0 %collective-permute-start.21 = (bf16[192,512]{1,0:T(8,128)(2,1)S(1)}, bf16[192,512]{1,0:T(8,128)(2,1)S(1)}, u32[]{:S(2)}, u32[]{:S(2)}) collective-permute-start(bf16[192,512]{1,0:T(8,128)(2,1)S(1)} %pad_maximum_fusion.4.d0), channel_id=1, source_target_pairs={{0,6},{1,7},{2,0},{3,1},{4,2},{5,3},{6,4},{7,5},{8,14},{9,15},{10,... | collective-permute-start | bytes 589832 | tf_op jit(solution)/shard_map/ppermute | solution.py:25
  123.9 25.2 %all-to-all-start.2 = ((bf16[8,64,512]{2,1,0:T(8,128)(2,1)}), bf16[8,64,512]{2,1,0:T(8,128)(2,1)}, u32[]{:S(2)}, u32[]{:S(2)}) async-start(bf16[8,64,512]{2,1,0:T(8,128)(2,1)} %get-tuple-element.140), calls=%async_computation.2 | async-start | bytes 1048576 | tf_op jit(solution)/shard_map/all_to_all | solution.py:77
  128.0 16.5 %collective-permute-start.23 = (bf16[128,1280]{1,0:T(8,128)(2,1)}, bf16[128,1280]{1,0:T(8,128)(2,1)}, u32[]{:S(2)}, u32[]{:S(2)}) collective-permute-start(bf16[128,1280]{1,0:T(8,128)(2,1)} %get-tuple-element.129), channel_id=1, source_target_pairs={{0,64},{8,72},{16,80},{24,88},{32,96},{40,104},{48,112},{56,120},{... | collective-permute-start | bytes 983048 | tf_op jit(solution)/shard_map/ppermute | solution.py:31
  130.0 16.9 %collective-permute-start.24 = (bf16[128,1280]{1,0:T(8,128)(2,1)}, bf16[128,1280]{1,0:T(8,128)(2,1)}, u32[]{:S(2)}, u32[]{:S(2)}) collective-permute-start(bf16[128,1280]{1,0:T(8,128)(2,1)} %get-tuple-element.130), channel_id=1, source_target_pairs={{0,128},{8,136},{16,144},{24,152},{32,160},{40,168},{48,176},{56,1... | collective-permute-start | bytes 983048 | tf_op jit(solution)/shard_map/ppermute | solution.py:31
  131.8 15.2 %collective-permute-start.25 = (bf16[128,1280]{1,0:T(8,128)(2,1)}, bf16[128,1280]{1,0:T(8,128)(2,1)}, u32[]{:S(2)}, u32[]{:S(2)}) collective-permute-start(bf16[128,1280]{1,0:T(8,128)(2,1)} %get-tuple-element.131), channel_id=1, source_target_pairs={{0,192},{8,200},{16,208},{24,216},{32,224},{40,232},{48,240},{56,2... | collective-permute-start | bytes 983048 | tf_op jit(solution)/shard_map/ppermute | solution.py:31
  142.5 17.3 %collective-permute-start.29 = (bf16[192,1792]{1,0:T(8,128)(2,1)}, bf16[192,1792]{1,0:T(8,128)(2,1)}, u32[]{:S(2)}, u32[]{:S(2)}) collective-permute-start(bf16[192,1792]{1,0:T(8,128)(2,1)} %get-tuple-element.133), channel_id=1, source_target_pairs={{0,6},{1,7},{2,0},{3,1},{4,2},{5,3},{6,4},{7,5},{8,14},{9,15},{10,... | collective-permute-start | bytes 2064392 | tf_op jit(solution)/shard_map/ppermute | solution.py:25
  143.4 17.8 %collective-permute-start.30 = (bf16[192,1792]{1,0:T(8,128)(2,1)}, bf16[192,1792]{1,0:T(8,128)(2,1)}, u32[]{:S(2)}, u32[]{:S(2)}) collective-permute-start(bf16[192,1792]{1,0:T(8,128)(2,1)} %get-tuple-element.135), channel_id=1, source_target_pairs={{0,2},{1,3},{2,4},{3,5},{4,6},{5,7},{6,0},{7,1},{8,10},{9,11},{10,... | collective-permute-start | bytes 2064392 | tf_op jit(solution)/shard_map/ppermute | solution.py:25
  149.1 19.8 %all-to-all-start.1 = ((bf16[8,16,1280]{2,1,0:T(8,128)(2,1)}), bf16[8,16,1280]{2,1,0:T(8,128)(2,1)}, u32[]{:S(2)}, u32[]{:S(2)}) async-start(bf16[8,16,1280]{2,1,0:T(8,128)(2,1)} %bitcast.89), calls=%async_computation.1 | async-start | bytes 655360 | tf_op jit(solution)/shard_map/all_to_all | solution.py:77
  161.2 18.1 %collective-permute-start.31 = (bf16[192,1792]{1,0:T(8,128)(2,1)}, bf16[192,1792]{1,0:T(8,128)(2,1)}, u32[]{:S(2)}, u32[]{:S(2)}) collective-permute-start(bf16[192,1792]{1,0:T(8,128)(2,1)} %get-tuple-element.142), channel_id=1, source_target_pairs={{0,4},{1,5},{2,6},{3,7},{4,0},{5,1},{6,2},{7,3},{8,12},{9,13},{10,... | collective-permute-start | bytes 2064392 | tf_op jit(solution)/shard_map/ppermute | solution.py:25
  172.2 11.8 %all-to-all-start.3 = ((bf16[4,4,1792]{2,1,0:T(4,128)(2,1)}), bf16[4,4,1792]{2,1,0:T(4,128)(2,1)S(1)}, u32[]{:S(2)}, u32[]{:S(2)}) async-start(bf16[4,4,1792]{2,1,0:T(4,128)(2,1)} %reshape.245), calls=%async_computation.3 | async-start | bytes 114688 | tf_op jit(solution)/shard_map/all_to_all | solution.py:81
  (26 other events, 280.6 us)

commit v5 on v4

--- a/solution.py
+++ b/solution.py
@@ -9,36 +9,19 @@
 
 NX, NY, NZ = 4, 4, 8
 GROUP = 32
-X_GROUPS = [[0, 2, 4, 6], [1, 3, 5, 7]]
-Z_GROUPS = [[y * NZ + z for z in range(NZ)] for y in range(NY)]
 Z_ORDER = ((0, 1, 7, 2), (6, 3, 5, 4))
-CORE_SWAP = [(i, i ^ 1) for i in range(8)]
+AXES = ("y", "z", "x", "core")
 BF = jnp.bfloat16
 F32 = jnp.float32
 VMEM_LIMIT = 60 * 1024 * 1024
 KERNEL_VMEM = 24 * 1024 * 1024
 
 
-def shift_x(a, by):
-    if by % NX == 0:
+def shift(a, axis, by):
+    size = lax.axis_size(axis)
+    if by % size == 0:
         return a
-    return lax.ppermute(a, "expert", [(i, ((i // 2 + by) % NX) * 2 + i % 2) for i in range(2 * NX)])
-
-
-def shift_y(a, by):
-    if by == 0:
-        return a
-    return lax.ppermute(a, "dp", [(i, ((i // NZ + by) % NY) * NZ + i % NZ) for i in range(NY * NZ)])
-
-
-def shift_z(a, by):
-    if by == 0:
-        return a
-    return lax.ppermute(a, "dp", [(i, (i // NZ) * NZ + (i % NZ + by) % NZ) for i in range(NY * NZ)])
-
-
-def gather_y(a):
-    return jnp.concatenate([a] + [shift_y(a, -k) for k in range(1, NY)], axis=0)
+    return lax.ppermute(a, axis, [(i, (i + by) % size) for i in range(size)])
 
 
 def gather_z(a, early, late, work):
@@ -46,19 +29,19 @@
     for step in range(NZ // 2 - 1):
         if step == 2:
             (after[-1], before[-1]), early = lax.optimization_barrier(((after[-1], before[-1]), early))
-        after.append(shift_z(after[-1], -1))
-        before.append(shift_z(before[-1], 1))
+        after.append(shift(after[-1], "z", -1))
+        before.append(shift(before[-1], "z", 1))
     last, late = lax.optimization_barrier(((after[-1], before[-1]), late))
     cut = a.shape[0] // 2
-    far = (shift_z(last[0][:cut], -1), shift_z(last[1][cut:], 1))
+    far = (shift(last[0][:cut], "z", -1), shift(last[1][cut:], "z", 1))
     first = after[:3] + before[1:2]
     first = jnp.concatenate([first[0], first[1], first[3], first[2]], axis=0)
-    first = (first, lax.ppermute(first, "expert", CORE_SWAP))
+    first = (first, shift(first, "core", 1))
     partial, ws = work(first, early, late)
     far, mine = lax.optimization_barrier((far, partial[0]))
     done = ([mine, partial[1]], ws)
     second = jnp.concatenate([before[2], last[0], last[1], *far], axis=0)
-    return first, done, (second, lax.ppermute(second, "expert", CORE_SWAP))
+    return first, done, (second, shift(second, "core", 1))
 
 
 def by_y_and_z(a, z):
@@ -73,12 +56,8 @@
     return sum(a.astype(F32) for a in terms).astype(BF)
 
 
-def exchange(a, groups):
-    return lax.all_to_all(a, "dp", 0, 0, axis_index_groups=groups, tiled=True)
-
-
-def across_x(a):
-    return lax.all_to_all(a, "expert", 0, 0, axis_index_groups=X_GROUPS, tiled=True)
+def exchange(a, axes):
+    return lax.all_to_all(a, axes, 0, 0, tiled=True)
 
 
 def to_slices(a):
@@ -200,54 +179,63 @@
 
 
 def weight_grad_kernel(
-    s0, s1, s2, s3, x0, x1, x2, x3, g0, g1, g2, g3, d0, d1, d2, d3, o0, o1, o2, o3, d_gu, d_h
+    experts, s0, s1, s2, s3, da, db, r0, r1, r2, r3, oa, ob, x, g, d_gu, d_h, sems
 ):
-    ds, outs = (d0, d1, d2, d3), (o0, o1, o2, o3)
-    gu = 2 * o0.shape[0] // 3
-    slots = d0.shape[1] // 4
-
-    @pl.when(pl.program_id(0) == 0)
-    def _():
-        for i, slot in enumerate((s0, s1, s2, s3)):
-            for s, d in enumerate(ds):
-                spread = nt(
-                    d[:, i * slots : (i + 1) * slots], places(slot[:, s : s + 1], slots).astype(BF)
-                ).astype(BF)
-                at = slice(i * spread.shape[1], (i + 1) * spread.shape[1])
-                d_gu[s * gu : (s + 1) * gu, at] = spread[:gu]
-                d_h[s * gu // 2 : (s + 1) * gu // 2, at] = spread[gu:]
-
-    x = jnp.concatenate([x0[...], x1[...], x2[...], x3[...]], axis=0)
-    g = jnp.concatenate([g0[...], g1[...], g2[...], g3[...]], axis=0)
-    g_gu = mm(d_gu[...], x).astype(BF)
-    g_h = mm(d_h[...], g).astype(BF)
-    for s, out in enumerate(outs):
-        out[:gu] = g_gu[s * gu : (s + 1) * gu]
-        out[gu:] = g_h[s * gu // 2 : (s + 1) * gu // 2]
-
-
-def weight_grads(slots, groups, delta, part):
+    gu = 2 * oa.shape[0] // 3
+    slots = da.shape[1] // 4
+    n, part = r0.shape[0], oa.shape[1]
+    copies = [
+        pltpu.make_async_copy(
+            r.at[:, pl.ds(k * part, part)], dst.at[pl.ds(i * n, n)], sems.at[4 * k + i]
+        )
+        for k, dst in enumerate((x, g))
+        for i, r in enumerate((r0, r1, r2, r3))
+    ]
+    for copy in copies:
+        copy.start()
+    for i, slot in enumerate((s0, s1, s2, s3)):
+        for j, (s, d) in enumerate(zip(experts, (da, db))):
+            spread = nt(
+                d[:, i * slots : (i + 1) * slots], places(slot[:, s : s + 1], slots).astype(BF)
+            ).astype(BF)
+            at = slice(i * n, (i + 1) * n)
+            d_gu[j * gu : (j + 1) * gu, at] = spread[:gu]
+            d_h[j * gu // 2 : (j + 1) * gu // 2, at] = spread[gu:]
+    for copy in copies[:4]:
+        copy.wait()
+    grad = mm(d_gu[...], x[...]).astype(BF)
+    oa[:gu] = grad[:gu]
+    ob[:gu] = grad[gu:]
+    for copy in copies[4:]:
+        copy.wait()
+    grad = mm(d_h[...], g[...]).astype(BF)
+    oa[gu:] = grad[: gu // 2]
+    ob[gu:] = grad[gu // 2 :]
+
+
+def weight_grads(experts, slots, groups, delta, part):
     n, rows = groups[0].shape[0], delta[0].shape[0]
-    wide = 256 if part % 256 == 0 else part
-    first, second = part // wide, 2 * rows // 3
-    whole = lambda a: pl.BlockSpec(a.shape, lambda i: (0, 0))
+    gu = 2 * rows // 3
+    vmem = pl.BlockSpec(memory_space=pltpu.VMEM)
     return pl.pallas_call(
-        weight_grad_kernel,
-        grid=(first,),
-        out_shape=[jax.ShapeDtypeStruct((rows, part), BF)] * NX,
-        in_specs=[whole(a) for a in slots]
-        + [pl.BlockSpec((n, wide), lambda i: (0, i))] * 4
-        + [pl.BlockSpec((n, wide), lambda i: (0, first + i))] * 4
-        + [whole(a) for a in delta],
-        out_specs=[pl.BlockSpec((rows, wide), lambda i: (0, i))] * NX,
-        scratch_shapes=[pltpu.VMEM((NX * second, 4 * n), BF), pltpu.VMEM((NX * second // 2, 4 * n), BF)],
-        compiler_params=pltpu.CompilerParams(vmem_limit_bytes=VMEM_LIMIT),
+        functools.partial(weight_grad_kernel, experts),
+        out_shape=[jax.ShapeDtypeStruct((rows, part), BF)] * 2,
+        in_specs=[vmem] * 6 + [pl.BlockSpec(memory_space=pl.ANY)] * 4,
+        out_specs=[vmem] * 2,
+        scratch_shapes=[
+            pltpu.VMEM((4 * n, part), BF),
+            pltpu.VMEM((4 * n, part), BF),
+            pltpu.VMEM((2 * gu, 4 * n), BF),
+            pltpu.VMEM((gu, 4 * n), BF),
+            pltpu.SemaphoreType.DMA((8,)),
+        ],
+        compiler_params=pltpu.CompilerParams(vmem_limit_bytes=KERNEL_VMEM),
         cost_estimate=pl.CostEstimate(
-            flops=2 * rows * NX * part * 4 * n,
-            bytes_accessed=2 * (8 * n * part + 2 * NX * rows * part),
+            flops=2 * rows * 2 * part * 4 * n,
+            bytes_accessed=2 * (8 * n * part + 2 * 2 * rows * part),
             transcendentals=0,
         ),
-    )(*slots, *groups, *groups, *delta)
+    )(*slots, *[delta[s] for s in experts], *groups)
 
 
 def input_grad(half, slot, ds, ws):
@@ -267,19 +255,16 @@
     out[...] = input_grad(1, slot, (d0, d1, d2, d3), (w0, w1, w2, w3)).astype(BF)
 
 
-def ours_kernel(slot, d0, d1, d2, d3, w0, w1, w2, w3, theirs, l0, l1, l2, l3, right):
-    grad = input_grad(0, slot, (d0, d1, d2, d3), (w0, w1, w2, w3))
-    grad = (grad + theirs[...].astype(F32)).astype(BF)
-    cut = l0.shape[1]
-    unit = grad.shape[0] // (NY * NZ)
-    for y, left in enumerate((l0, l1, l2, l3)):
-        left[...] = grad[y * NZ * unit : (y + 1) * NZ * unit, :cut]
-        for z in range(NZ):
-            row = (y * NZ + z) * unit
-            right[z, y * unit : (y + 1) * unit] = grad[row : row + unit, cut:]
-
-
-def local_call(kernel, out_shape, cost, scalars=0, limit=KERNEL_VMEM):
+def ours_kernel(y_ref, slot, d0, d1, d2, d3, w0, w1, w2, w3, theirs, o0, o1, o2, o3, grad):
+    total_grad = input_grad(0, slot, (d0, d1, d2, d3), (w0, w1, w2, w3)) + theirs[...].astype(F32)
+    grad[...] = total_grad.astype(BF)
+    rows = o0.shape[0]
+    for k, out in enumerate((o0, o1, o2, o3)):
+        start = pl.multiple_of(lax.rem(y_ref[0] + k, NY) * rows, rows)
+        out[...] = grad[pl.ds(start, rows), :]
+
+
+def local_call(kernel, out_shape, cost, scalars=0, scratch=()):
     vmem = pl.BlockSpec(memory_space=pltpu.VMEM)
     smem = pl.BlockSpec(memory_space=pltpu.SMEM)
 
@@ -289,7 +274,8 @@
             out_shape=out_shape,
             in_specs=[smem] * scalars + [vmem] * (len(args) - scalars),
             out_specs=[vmem] * len(out_shape),
-            compiler_params=pltpu.CompilerParams(vmem_limit_bytes=limit),
+            scratch_shapes=list(scratch),
+            compiler_params=pltpu.CompilerParams(vmem_limit_bytes=KERNEL_VMEM),
             cost_estimate=pl.CostEstimate(flops=cost[0], bytes_accessed=cost[1], transcendentals=0),
         )(*args)
 
@@ -308,13 +294,14 @@
     down_master,
     down_scale,
 ):
-    experts = lax.axis_size("expert")
-    expert = lax.axis_index("expert")
+    x, y, z = (lax.axis_index(name) for name in ("x", "y", "z"))
+    experts = NX * lax.axis_size("core")
+    expert = x * lax.axis_size("core") + lax.axis_index("core")
     toks, width = tokens.shape
     hid = gate_master.shape[1]
     part = width // NX
     cap = toks // 2
-    x_index = (expert // 2).reshape(1)
+    x_index = x.reshape(1)
 
     named = expert_ids[:, :, None] == jnp.arange(experts, dtype=jnp.int32)
     factor = jnp.sum(jnp.where(named, gate_values[:, :, None], 0.0), axis=1)
@@ -329,12 +316,13 @@
     payload = jnp.concatenate(
         [to_slices(tokens), to_slices(grad_out), jnp.broadcast_to(cols, (NX,) + cols.shape)], axis=2
     )
-    mine = across_x(payload).reshape(NX * toks, -1)
+    payload = jnp.broadcast_to(payload, (NY,) + payload.shape).reshape(NY * NX, toks, -1)
+    own = exchange(payload, ("y", "x")).reshape(NY * NX * toks, -1)
     *w_mine, keep = dequantize(
         x_index, (gate_master, up_master, down_master), (gate_scale, up_scale, down_scale)
     )
-    own, w_mine = lax.optimization_barrier((gather_y(mine), w_mine))
-    w = [shift_x(a, s) if s != 2 else a for s, a in enumerate(w_mine)]
+    own, w_mine = lax.optimization_barrier((own, w_mine))
+    w = [shift(a, "x", s) if s != 2 else a for s, a in enumerate(w_mine)]
     w = lax.optimization_barrier(w)
     n = NY * NZ * NX * toks // 2
     slots = n // toks * cap
@@ -345,7 +333,7 @@
     pick = (col < cap * NX) & (row == owner + (3 + col % cap) * experts)
     pick |= (col == cap * NX) & (row % experts == expert) & (row < 3 * experts)
     pick = pick.astype(BF)
-    row_bytes = 2 * n * mine.shape[1]
+    row_bytes = 2 * n * own.shape[1]
     w_bytes = 2 * 3 * hid * width
     forward = local_call(
         functools.partial(forward_kernel, toks),
@@ -358,15 +346,14 @@
         ws = (w[0], early[0], late, early[1])
         return [forward(a, pick, *ws) for a in rows], ws
 
-    first, (partial, w), second = gather_z(own, (w[1], w[3]), shift_x(w[2], 2), work)
+    first, (partial, w), second = gather_z(own, (w[1], w[3]), shift(w[2], "x", 2), work)
     partial = partial + [forward(a, pick, *w) for a in second]
     groups = [first[0], second[0], first[1], second[1]]
     partial = [partial[i] for i in (0, 2, 1, 3)]
     weight = jnp.concatenate([p[NX] for p in partial], axis=1)
-    pre = [shift_x(jnp.concatenate([p[s] for p in partial], axis=1), -s) for s in range(NX)]
+    pre = [shift(jnp.concatenate([p[s] for p in partial], axis=1), "x", -s) for s in range(NX)]
     slot = [p[NX + 1] for p in partial]
     by_half = [jnp.where(a >= 0, a + i % 2 * slots, -1) for i, a in enumerate(slot)]
-    z = lax.axis_index("dp") % NZ
     by_half = [by_y_and_z(jnp.concatenate(by_half[i : i + 2], axis=0), z) for i in (0, 2)]
 
     pre = sum(a.astype(F32) for a in pre)
@@ -379,37 +366,35 @@
     delta_up = delta_hidden * silu_gate
     delta_gate = delta_hidden * up_pre * sig_gate * (1.0 + gate_pre * (1.0 - sig_gate))
     delta = jnp.concatenate([delta_gate, delta_up, hidden], axis=0).astype(BF)
-    delta = [shift_x(delta, s) for s in range(NX)]
+    delta = [shift(delta, "x", s) for s in range(NX)]
     half = 2 * n
     theirs = local_call(
         theirs_kernel,
         [jax.ShapeDtypeStruct((half, part), BF)],
         (4 * hid * width * half, row_bytes + w_bytes),
     )(by_half[1], *delta, *w)[0]
-    theirs = lax.ppermute(theirs, "expert", CORE_SWAP)
-    g_all = weight_grads(slot, groups, delta, part)
-    cut = part * 5 // 7
+    theirs = shift(theirs, "core", 1)
+    g_near = weight_grads((1, 3), slot, groups, delta, part)
+    theirs, g_near = lax.optimization_barrier((theirs, g_near))
+    near = (shift(g_near[0], "x", -1), shift(g_near[1], "x", -3))
+    g_own, g_far = weight_grads((0, 2), slot, groups, delta, part)
     unit = NX * toks
-    *left, right = local_call(
+    grad_x = local_call(
         ours_kernel,
-        [
-            *[jax.ShapeDtypeStruct((NZ * unit, cut), BF)] * NY,
-            jax.ShapeDtypeStruct((NZ, NY * unit, part - cut), BF),
-        ],
+        [jax.ShapeDtypeStruct((NZ * unit, part), BF)] * NY,
         (4 * hid * width * half, 2 * row_bytes + w_bytes),
-    )(by_half[0], *delta, *w, theirs)
-    right = exchange(right, Z_GROUPS)
-    left, _ = lax.optimization_barrier(([shift_y(left[k], k) for k in range(NY)], g_all))
-    near, third = lax.optimization_barrier(((shift_x(g_all[1], -1), shift_x(g_all[3], -3)), g_all[2]))
-    left = total(left).reshape(NZ, unit, cut)
-    right = total(list(right)).reshape(NY, unit, part - cut)
-    left = total(list(exchange(left, Z_GROUPS)))
-    right = total([shift_y(right[k], k) for k in range(NY)])
-    grad_x = jnp.concatenate([left, right], axis=1)
-    third = shift_x(third, -2)
-    grad_tokens = from_slices(across_x(grad_x.reshape(NX, toks, part)))
-
-    g_all = (g_all[0], near[0], third, near[1])
+        scalars=1,
+        scratch=[pltpu.VMEM((half, part), BF)],
+    )(y.reshape(1), by_half[0], *delta, *w, theirs)
+    grad_x = [shift(g, "y", k) for k, g in enumerate(grad_x)]
+    near, g_far = lax.optimization_barrier((near, g_far))
+    far = shift(g_far, "x", -2)
+    grad_x = total(grad_x).reshape(NZ * NX, toks, part)
+    grad_x, far = lax.optimization_barrier((grad_x, far))
+    grad_x = exchange(grad_x, ("z", "x"))
+    grad_tokens = from_slices(total(list(grad_x.reshape(NZ, NX, toks, part))))
+
+    g_all = (g_own, near[0], far, near[1])
     grads = local_call(
         finish_kernel,
         [jax.ShapeDtypeStruct((1, hid, width), F32)] * 3,
@@ -420,8 +405,9 @@
 
 
 def solution(mesh):
-    rows = P(("dp", "expert"), None)
-    weights = P("expert", "dp", None)
+    mesh = jax.sharding.Mesh(mesh.devices.reshape(NY, NZ, NX, -1), AXES)
+    rows = P(AXES, None)
+    weights = P(("x", "core"), ("y", "z"), None)
     return jax.shard_map(
         per_device,
         mesh=mesh,

time: 187 us -> 180 us (0.963)
  starting transfers between devices: 70.1 us -> 56.7 us
  local copies, waits for them, and re-layouts: 10.3 us -> 17.2 us
  waiting for transfers between devices: 57.3 us -> 61.5 us
  other arithmetic: 7.87 us -> 4.93 us
    all_to_all x4 -> x2, starting transfers between devices: 22.1 us -> 14.9 us  [exchange(): return lax.all_to_all(a, axes, 0, 0, tiled=True)]
    ppermute x32 -> x26, starting transfers between devices: 48 us -> 41.8 us  [shift(): return lax.ppermute(a, axis, [(i, (i + by) % size) for i in range(size)])]
    all_to_all x4 -> x2, waiting for transfers between devices: 4.46 us -> 8.99 us  [exchange(): return lax.all_to_all(a, axes, 0, 0, tiled=True)]
    unnamed x66 -> x53, local copies, waits for them, and re-layouts: 7.22 us -> 10.6 us
    reshape x2 -> x4, local copies, waits for them, and re-layouts: 0.67 us -> 3.87 us  [the longest x1 2.07 us: per_device(): grad_x = total(grad_x).reshape(NZ * NX, toks, part)]
    convert_element_type x4 -> x2, other arithmetic: 4.18 us -> 2.79 us  [total(): return sum((a.astype(F32) for a in terms)).astype(BF)]
    ppermute x32 -> x26, waiting for transfers between devices: 52.8 us -> 52.5 us  [shift(): return lax.ppermute(a, axis, [(i, (i + by) % size) for i in range(size)])]
    pallas_call x1 -> x2, Pallas kernels: 9.67 us -> 9.88 us  [weight_grads(): pl.pallas_call(functools.partial(weight_grad_kernel, experts), out_shape=...]
  transfers between devices with their start and end apart: 36 -> 28, of which waited for: 23 -> 19; matrix products, arithmetic and copies ran while one was open for 7% -> 6% of each run, Pallas kernels for 17% -> 18%
where the time goes in v5:
time: 180 us; the launch traced here: 178 us
  waiting for transfers between devices  61.5 us (34%)
  starting transfers between devices  56.7 us (32%)
  Pallas kernels  36.9 us (20%)
  local copies, waits for them, and re-layouts  17.2 us (10%)
  other arithmetic  4.93 us (3%)
    ppermute x26, waiting for transfers between devices, shift(): return lax.ppermute(a, axis, [(i, (i + by) % size) for i in range(size)])  52.5 us
    ppermute x26, starting transfers between devices, shift(): return lax.ppermute(a, axis, [(i, (i + by) % size) for i in range(size)])  41.8 us
    pallas_call x7, Pallas kernels, call(): pl.pallas_call(kernel, out_shape=out_shape, in_specs=[smem] * scalars + [...  18.4 us
    all_to_all x2, starting transfers between devices, exchange(): return lax.all_to_all(a, axes, 0, 0, tiled=True)  14.9 us
    unnamed x53, local copies, waits for them, and re-layouts  10.6 us
    pallas_call x2, Pallas kernels, weight_grads(): pl.pallas_call(functools.partial(weight_grad_kernel, experts), out_shape=...  9.88 us
    all_to_all x2, waiting for transfers between devices, exchange(): return lax.all_to_all(a, axes, 0, 0, tiled=True)  8.99 us
    pallas_call x1, Pallas kernels, dequantize(): pl.pallas_call(dequantize_kernel, grid_spec=grid, out_shape=[jax.ShapeDty...  8.56 us
  transfers between devices with their start and end apart: 28, of which 19 were waited for; matrix products, arithmetic and copies ran while one was open for 6% of the time, Pallas kernels for 18%

profile of v5, /device:TPU:2, one launch (start us, length us, event | category | flops | bytes accessed | tf_op | source)
XLA Modules:
  0.0 178.3 jit_solution(14870725979907948501)
XLA Ops:
  5.1 7.5 %all-to-all-start = ((bf16[16,4,3712]{2,1,0:T(4,128)(2,1)}), bf16[16,4,3712]{2,1,0:T(4,128)(2,1)S(1)}, u32[]{:S(2)}, u32[]{:S(2)}) async-start(bf16[16,4,3712]{2,1,0:T(4,128)(2,1)} %bitcast.3), calls=%async_computation | async-start | bytes 950272 | tf_op jit(solution)/shard_map/all_to_all | solution.py:60
  12.5 8.6 %shard_map.129 = (bf16[192,1792]{1,0:T(8,128)(2,1)}, bf16[192,1792]{1,0:T(8,128)(2,1)}, bf16[192,1792]{1,0:T(8,128)(2,1)}, bf16[192,1792]{1,0:T(8,128)(2,1)}, bf16[4,192,1792]{2,1,0:T(8,128)(2,1)}) custom-call(s32[1]{0:T(128)} %bitcast.4.x_ref, f32[1,64,7168]{2,1,0:T(8,128)} %gm.1, f32[1,64,7168]{2,1,0:T(8,128)} %um.1, f32[1,64,7168]{2,1,0:T(8,128)} %dm.1, ...), custom_call_target="tpu_custom_call" | custom-call | flops 41287680 | bytes 11010048 | tf_op jit(solution)/shard_map/pallas_call | solution.py:126
  22.2 5.9 %collective-permute-start = (bf16[64,3712]{1,0:T(8,128)(2,1)S(1)}, bf16[64,3712]{1,0:T(8,128)(2,1)S(1)}, u32[]{:S(2)}, u32[]{:S(2)}) collective-permute-start(bf16[64,3712]{1,0:T(8,128)(2,1)S(1)} %reshape.223), channel_id=1, source_target_pairs={{0,56},{8,0},{16,8},{24,16},{32,24},{40,32},{48,40},{56,48},{1,57}... | collective-permute-start | bytes 1425416 | tf_op jit(solution)/shard_map/ppermute | solution.py:24
  31.2 5.9 %collective-permute-done = bf16[64,3712]{1,0:T(8,128)(2,1)S(1)} collective-permute-done((bf16[64,3712]{1,0:T(8,128)(2,1)S(1)}, bf16[64,3712]{1,0:T(8,128)(2,1)S(1)}, u32[]{:S(2)}, u32[]{:S(2)}) %collective-permute-start) | collective-permute-done | bytes 475168 | tf_op jit(solution)/shard_map/ppermute | solution.py:24
  37.1 3.7 %collective-permute-start.1 = (bf16[64,3712]{1,0:T(8,128)(2,1)S(1)}, bf16[64,3712]{1,0:T(8,128)(2,1)S(1)}, u32[]{:S(2)}, u32[]{:S(2)}) collective-permute-start(bf16[64,3712]{1,0:T(8,128)(2,1)S(1)} %collective-permute-done), channel_id=1, source_target_pairs={{0,56},{8,0},{16,8},{24,16},{32,24},{40,32},{48,40},{56,48},{1,57}... | collective-permute-start | bytes 1425416 | tf_op jit(solution)/shard_map/ppermute | solution.py:24
  45.1 3.6 %collective-permute-start.8 = (bf16[192,1792]{1,0:T(8,128)(2,1)}, bf16[192,1792]{1,0:T(8,128)(2,1)S(1)}, u32[]{:S(2)}, u32[]{:S(2)}) collective-permute-start(bf16[192,1792]{1,0:T(8,128)(2,1)} %get-tuple-element.89), channel_id=1, source_target_pairs={{0,4},{2,6},{4,0},{6,2},{1,5},{3,7},{5,1},{7,3},{8,12},{10,14},{12... | collective-permute-start | bytes 2064392 | tf_op jit(solution)/shard_map/ppermute | solution.py:24
  48.8 3.4 %collective-permute-done.3 = bf16[64,3712]{1,0:T(8,128)(2,1)S(1)} collective-permute-done((bf16[64,3712]{1,0:T(8,128)(2,1)S(1)}, bf16[64,3712]{1,0:T(8,128)(2,1)S(1)}, u32[]{:S(2)}, u32[]{:S(2)}) %collective-permute-start.3) | collective-permute-done | bytes 475168 | tf_op jit(solution)/shard_map/ppermute | solution.py:24
  56.0 6.0 %collective-permute-done.8.w2 = bf16[192,1792]{1,0:T(8,128)(2,1)S(1)} collective-permute-done((bf16[192,1792]{1,0:T(8,128)(2,1)}, bf16[192,1792]{1,0:T(8,128)(2,1)S(1)}, u32[]{:S(2)}, u32[]{:S(2)}) %collective-permute-start.8) | collective-permute-done | bytes 688160 | tf_op jit(solution)/shard_map/ppermute | solution.py:24
  68.0 2.7 %shard_map.130 = (bf16[192,128]{1,0:T(8,128)(2,1)S(1)}, bf16[192,128]{1,0:T(8,128)(2,1)S(1)}, bf16[192,128]{1,0:T(8,128)(2,1)S(1)}, bf16[192,128]{1,0:T(8,128)(2...) custom-call(bf16[256,3712]{1,0:T(8,128)(2,1)} %constant_dynamic-update-slice_fusion.rows.r0, ...), custom_call_target="tpu_custom_call" | custom-call | flops 704643072 | bytes 4653056 | tf_op jit(solution)/shard_map/pallas_call | solution.py:272
  72.7 2.7 %shard_map.131 = (bf16[192,128]{1,0:T(8,128)(2,1)S(1)}, bf16[192,128]{1,0:T(8,128)(2,1)S(1)}, bf16[192,128]{1,0:T(8,128)(2,1)S(1)}, bf16[192,128]{1,0:T(8,128)(2...) custom-call(bf16[256,3712]{1,0:T(8,128)(2,1)} %constant_dynamic-update-slice_fusion.4.rows.r1, ...), custom_call_target="tpu_custom_call" | custom-call | flops 704643072 | bytes 4653056 | tf_op jit(solution)/shard_map/pallas_call | solution.py:272
  75.5 2.7 %shard_map.132 = (bf16[192,128]{1,0:T(8,128)(2,1)S(1)}, bf16[192,128]{1,0:T(8,128)(2,1)S(1)}, bf16[192,128]{1,0:T(8,128)(2,1)S(1)}, bf16[192,128]{1,0:T(8,128)(2...) custom-call(bf16[256,3712]{1,0:T(8,128)(2,1)} %collective-permute-done.11.rows.r2, ...), custom_call_target="tpu_custom_call" | custom-call | flops 704643072 | bytes 4653056 | tf_op jit(solution)/shard_map/pallas_call | solution.py:272
  78.3 2.7 %shard_map.133 = (bf16[192,128]{1,0:T(8,128)(2,1)S(1)}, bf16[192,128]{1,0:T(8,128)(2,1)S(1)}, bf16[192,128]{1,0:T(8,128)(2,1)S(1)}, bf16[192,128]{1,0:T(8,128)(2...) custom-call(bf16[256,3712]{1,0:T(8,128)(2,1)} %collective-permute-done.12.rows.r3, ...), custom_call_target="tpu_custom_call" | custom-call | flops 704643072 | bytes 4653056 | tf_op jit(solution)/shard_map/pallas_call | solution.py:272
  89.1 5.4 %collective-permute-done.14 = bf16[192,512]{1,0:T(8,128)(2,1)S(1)} collective-permute-done((bf16[192,512]{1,0:T(8,128)(2,1)S(1)}, bf16[192,512]{1,0:T(8,128)(2,1)S(1)}, u32[]{:S(2)}, u32[]{:S(2)}) %collective-permute-start.14) | collective-permute-done | bytes 196640 | tf_op jit(solution)/shard_map/ppermute | solution.py:24
  100.0 4.9 %collective-permute-done.17.d2.db = bf16[192,512]{1,0:T(8,128)(2,1)S(1)} collective-permute-done((bf16[192,512]{1,0:T(8,128)(2,1)S(1)}, bf16[192,512]{1,0:T(8,128)(2,1)S(1)}, u32[]{:S(2)}, u32[]{:S(2)}) %collective-permute-start.17) | collective-permute-done | bytes 196640 | tf_op jit(solution)/shard_map/ppermute | solution.py:24
  104.9 3.2 %collective-permute-done.16.d1.da = bf16[192,512]{1,0:T(8,128)(2,1)S(1)} collective-permute-done((bf16[192,512]{1,0:T(8,128)(2,1)S(1)}, bf16[192,512]{1,0:T(8,128)(2,1)S(1)}, u32[]{:S(2)}, u32[]{:S(2)}) %collective-permute-start.16) | collective-permute-done | bytes 196640 | tf_op jit(solution)/shard_map/ppermute | solution.py:24
  110.2 4.5 %shard_map.135 = (bf16[192,1792]{1,0:T(8,128)(2,1)S(1)}, bf16[192,1792]{1,0:T(8,128)(2,1)S(1)}) custom-call(s32[256,128]{1,0:T(8,128)S(1)} %get-tuple-element.102.s0, s32[256,128]{1,0:T(8,128)S(1)} %get-tuple-element.105.s1, s32[256,128]{1,0:T(8,128)S(1)} %get-tuple-element.126.s2, s32[256,128]{1,0:T(8,128)S(1)} %get-tuple-element.127.s3, ...), custom_call_target="tpu_custom_call" | custom-call | flops 1409286144 | bytes 10092544 | tf_op jit(solution)/shard_map/pallas_call | solution.py:220
  114.7 3.0 %collective-permute-start.23 = (bf16[192,1792]{1,0:T(8,128)(2,1)S(1)}, bf16[192,1792]{1,0:T(8,128)(2,1)S(1)}, u32[]{:S(2)}, u32[]{:S(2)}) collective-permute-start(bf16[192,1792]{1,0:T(8,128)(2,1)S(1)} %get-tuple-element.135), channel_id=1, source_target_pairs={{0,6},{2,0},{4,2},{6,4},{1,7},{3,1},{5,3},{7,5},{8,14},{10,8},{12,... | collective-permute-start | bytes 2064392 | tf_op jit(solution)/shard_map/ppermute | solution.py:24
  121.1 2.7 %collective-permute-start.21 = (bf16[128,1792]{1,0:T(8,128)(2,1)S(1)}, bf16[128,1792]{1,0:T(8,128)(2,1)S(1)}, u32[]{:S(2)}, u32[]{:S(2)}) collective-permute-start(bf16[128,1792]{1,0:T(8,128)(2,1)S(1)} %get-tuple-element.133), channel_id=1, source_target_pairs={{0,128},{64,192},{128,0},{192,64},{1,129},{65,193},{129,1},{193,65... | collective-permute-start | bytes 1376264 | tf_op jit(solution)/shard_map/ppermute | solution.py:24
  125.2 5.4 %shard_map.137 = (bf16[192,1792]{1,0:T(8,128)(2,1)S(1)}, bf16[192,1792]{1,0:T(8,128)(2,1)}) custom-call(s32[256,128]{1,0:T(8,128)S(1)} %get-tuple-element.102.s0, s32[256,128]{1,0:T(8,128)S(1)} %get-tuple-element.105.s1, s32[256,128]{1,0:T(8,128)S(1)} %get-tuple-element.126.s2, s32[256,128]{1,0:T(8,128)S(1)} %get-tuple-element.127.s3, ...), custom_call_target="tpu_custom_call" | custom-call | flops 1409286144 | bytes 10092544 | tf_op jit(solution)/shard_map/pallas_call | solution.py:220
  137.9 6.3 %collective-permute-done.21 = bf16[128,1792]{1,0:T(8,128)(2,1)S(1)} collective-permute-done((bf16[128,1792]{1,0:T(8,128)(2,1)S(1)}, bf16[128,1792]{1,0:T(8,128)(2,1)S(1)}, u32[]{:S(2)}, u32[]{:S(2)}) %collective-permute-start.21) | collective-permute-done | bytes 458784 | tf_op jit(solution)/shard_map/ppermute | solution.py:24
  147.3 7.4 %collective-permute-done.25.r2 = bf16[192,1792]{1,0:T(8,128)(2,1)} collective-permute-done((bf16[192,1792]{1,0:T(8,128)(2,1)}, bf16[192,1792]{1,0:T(8,128)(2,1)}, u32[]{:S(2)}, u32[]{:S(2)}) %collective-permute-start.25) | collective-permute-done | bytes 688160 | tf_op jit(solution)/shard_map/ppermute | solution.py:24
  154.7 7.4 %all-to-all-start.1 = ((bf16[32,4,1792]{2,1,0:T(4,128)(2,1)}), bf16[32,4,1792]{2,1,0:T(4,128)(2,1)}, u32[]{:S(2)}, u32[]{:S(2)}) async-start(bf16[32,4,1792]{2,1,0:T(4,128)(2,1)} %reshape.227), calls=%async_computation.1 | async-start | bytes 917504 | tf_op jit(solution)/shard_map/all_to_all | solution.py:60
  164.3 4.3 %shard_map.138 = (f32[1,64,7168]{2,1,0:T(8,128)}, f32[1,64,7168]{2,1,0:T(8,128)}, f32[1,64,7168]{2,1,0:T(8,128)}) custom-call(s32[1]{0:T(128)} %bitcast.4.x_ref, bf16[192,1792]{1,0:T(8,128)(2,1)S(1)} %copy-done.7, bf16[192,1792]{1,0:T(8,128)(2,1)S(1)} %copy-done.3, bf16[192,1792]{1,0:T(8,128)(2,1)} %collective-permute-done.25.r2, ...), custom_call_target="tpu_custom_call" | custom-call | flops 4128768 | bytes 11010048 | tf_op jit(solution)/shard_map/pallas_call | solution.py:272
  168.6 8.0 %all-to-all-done.1 = bf16[32,4,1792]{2,1,0:T(4,128)(2,1)} async-done(((bf16[32,4,1792]{2,1,0:T(4,128)(2,1)}), bf16[32,4,1792]{2,1,0:T(4,128)(2,1)}, u32[]{:S(2)}, u32[]{:S(2)}) %all-to-all-start.1) | async-done | bytes 458784 | tf_op jit(solution)/shard_map/all_to_all | solution.py:60
  (140 shorter events, 59.3 us)
Async XLA Ops:
  5.1 17.1 %all-to-all-start = ((bf16[16,4,3712]{2,1,0:T(4,128)(2,1)}), bf16[16,4,3712]{2,1,0:T(4,128)(2,1)S(1)}, u32[]{:S(2)}, u32[]{:S(2)}) async-start(bf16[16,4,3712]{2,1,0:T(4,128)(2,1)} %bitcast.3), calls=%async_computation | async-start | bytes 950272 | tf_op jit(solution)/shard_map/all_to_all | solution.py:60
  22.2 14.9 %collective-permute-start = (bf16[64,3712]{1,0:T(8,128)(2,1)S(1)}, bf16[64,3712]{1,0:T(8,128)(2,1)S(1)}, u32[]{:S(2)}, u32[]{:S(2)}) collective-permute-start(bf16[64,3712]{1,0:T(8,128)(2,1)S(1)} %reshape.223), channel_id=1, source_target_pairs={{0,56},{8,0},{16,8},{24,16},{32,24},{40,32},{48,40},{56,48},{1,57}... | collective-permute-start | bytes 1425416 | tf_op jit(solution)/shard_map/ppermute | solution.py:24
  28.2 12.6 %collective-permute-start.2 = (bf16[64,3712]{1,0:T(8,128)(2,1)S(1)}, bf16[64,3712]{1,0:T(8,128)(2,1)S(1)}, u32[]{:S(2)}, u32[]{:S(2)}) collective-permute-start(bf16[64,3712]{1,0:T(8,128)(2,1)S(1)} %reshape.223), channel_id=1, source_target_pairs={{0,8},{8,16},{16,24},{24,32},{32,40},{40,48},{48,56},{56,0},{1,9},... | collective-permute-start | bytes 1425416 | tf_op jit(solution)/shard_map/ppermute | solution.py:24
  28.3 16.0 %collective-permute-start.4 = (bf16[192,1792]{1,0:T(8,128)(2,1)}, bf16[192,1792]{1,0:T(8,128)(2,1)S(1)}, u32[]{:S(2)}, u32[]{:S(2)}) collective-permute-start(bf16[192,1792]{1,0:T(8,128)(2,1)} %get-tuple-element.82), channel_id=1, source_target_pairs={{0,2},{2,4},{4,6},{6,0},{1,3},{3,5},{5,7},{7,1},{8,10},{10,12},{12... | collective-permute-start | bytes 2064392 | tf_op jit(solution)/shard_map/ppermute | solution.py:24
  28.8 16.3 %collective-permute-start.5 = (bf16[192,1792]{1,0:T(8,128)(2,1)}, bf16[192,1792]{1,0:T(8,128)(2,1)S(1)}, u32[]{:S(2)}, u32[]{:S(2)}) collective-permute-start(bf16[192,1792]{1,0:T(8,128)(2,1)} %get-tuple-element.84), channel_id=1, source_target_pairs={{0,6},{2,0},{4,2},{6,4},{1,7},{3,1},{5,3},{7,5},{8,14},{10,8},{12,... | collective-permute-start | bytes 2064392 | tf_op jit(solution)/shard_map/ppermute | solution.py:24
  37.1 11.7 %collective-permute-start.1 = (bf16[64,3712]{1,0:T(8,128)(2,1)S(1)}, bf16[64,3712]{1,0:T(8,128)(2,1)S(1)}, u32[]{:S(2)}, u32[]{:S(2)}) collective-permute-start(bf16[64,3712]{1,0:T(8,128)(2,1)S(1)} %collective-permute-done), channel_id=1, source_target_pairs={{0,56},{8,0},{16,8},{24,16},{32,24},{40,32},{48,40},{56,48},{1,57}... | collective-permute-start | bytes 1425416 | tf_op jit(solution)/shard_map/ppermute | solution.py:24
  40.8 11.4 %collective-permute-start.3 = (bf16[64,3712]{1,0:T(8,128)(2,1)S(1)}, bf16[64,3712]{1,0:T(8,128)(2,1)S(1)}, u32[]{:S(2)}, u32[]{:S(2)}) collective-permute-start(bf16[64,3712]{1,0:T(8,128)(2,1)S(1)} %collective-permute-done.2), channel_id=1, source_target_pairs={{0,8},{8,16},{16,24},{24,32},{32,40},{40,48},{48,56},{56,0},{1,9},... | collective-permute-start | bytes 1425416 | tf_op jit(solution)/shard_map/ppermute | solution.py:24
  45.1 16.8 %collective-permute-start.8 = (bf16[192,1792]{1,0:T(8,128)(2,1)}, bf16[192,1792]{1,0:T(8,128)(2,1)S(1)}, u32[]{:S(2)}, u32[]{:S(2)}) collective-permute-start(bf16[192,1792]{1,0:T(8,128)(2,1)} %get-tuple-element.89), channel_id=1, source_target_pairs={{0,4},{2,6},{4,0},{6,2},{1,5},{3,7},{5,1},{7,3},{8,12},{10,14},{12... | collective-permute-start | bytes 2064392 | tf_op jit(solution)/shard_map/ppermute | solution.py:24
  52.2 9.7 %collective-permute-start.6 = (bf16[64,3712]{1,0:T(8,128)(2,1)S(1)}, bf16[64,3712]{1,0:T(8,128)(2,1)S(1)}, u32[]{:S(2)}, u32[]{:S(2)}) collective-permute-start(bf16[64,3712]{1,0:T(8,128)(2,1)S(1)} %collective-permute-done.1), channel_id=1, source_target_pairs={{0,56},{8,0},{16,8},{24,16},{32,24},{40,32},{48,40},{56,48},{1,57}... | collective-permute-start | bytes 1425416 | tf_op jit(solution)/shard_map/ppermute | solution.py:24
  52.5 10.5 %collective-permute-start.7 = (bf16[64,3712]{1,0:T(8,128)(2,1)S(1)}, bf16[64,3712]{1,0:T(8,128)(2,1)S(1)}, u32[]{:S(2)}, u32[]{:S(2)}) collective-permute-start(bf16[64,3712]{1,0:T(8,128)(2,1)S(1)} %collective-permute-done.3), channel_id=1, source_target_pairs={{0,8},{8,16},{16,24},{24,32},{32,40},{40,48},{48,56},{56,0},{1,9},... | collective-permute-start | bytes 1425416 | tf_op jit(solution)/shard_map/ppermute | solution.py:24
  55.1 20.4 %collective-permute-start.11 = (bf16[256,3712]{1,0:T(8,128)(2,1)}, bf16[256,3712]{1,0:T(8,128)(2,1)}, u32[]{:S(2)}, u32[]{:S(2)}) collective-permute-start(bf16[256,3712]{1,0:T(8,128)(2,1)} %constant_dynamic-update-slice_fusion.rows.r0), channel_id=1, source_target_pairs={{0,1},{1,0},{2,3},{3,2},{4,5},{5,4},{6,7},{7,6},{8,9},{9,8},{10,11... | collective-permute-start | bytes 5701640 | tf_op jit(solution)/shard_map/ppermute | solution.py:24
  81.1 8.0 %collective-permute-start.13 = (bf16[192,512]{1,0:T(8,128)(2,1)S(1)}, bf16[192,512]{1,0:T(8,128)(2,1)S(1)}, u32[]{:S(2)}, u32[]{:S(2)}) collective-permute-start(bf16[192,512]{1,0:T(8,128)(2,1)S(1)} %pad_maximum_fusion), channel_id=1, source_target_pairs={{0,6},{2,0},{4,2},{6,4},{1,7},{3,1},{5,3},{7,5},{8,14},{10,8},{12,... | collective-permute-start | bytes 589832 | tf_op jit(solution)/shard_map/ppermute | solution.py:24
  82.7 11.8 %collective-permute-start.14 = (bf16[192,512]{1,0:T(8,128)(2,1)S(1)}, bf16[192,512]{1,0:T(8,128)(2,1)S(1)}, u32[]{:S(2)}, u32[]{:S(2)}) collective-permute-start(bf16[192,512]{1,0:T(8,128)(2,1)S(1)} %pad_maximum_fusion.1), channel_id=1, source_target_pairs={{0,4},{2,6},{4,0},{6,2},{1,5},{3,7},{5,1},{7,3},{8,12},{10,14},{12... | collective-permute-start | bytes 589832 | tf_op jit(solution)/shard_map/ppermute | solution.py:24
  85.1 10.1 %collective-permute-start.15 = (bf16[192,512]{1,0:T(8,128)(2,1)S(1)}, bf16[192,512]{1,0:T(8,128)(2,1)S(1)}, u32[]{:S(2)}, u32[]{:S(2)}) collective-permute-start(bf16[192,512]{1,0:T(8,128)(2,1)S(1)} %pad_maximum_fusion.2), channel_id=1, source_target_pairs={{0,2},{2,4},{4,6},{6,0},{1,3},{3,5},{5,7},{7,1},{8,10},{10,12},{12... | collective-permute-start | bytes 589832 | tf_op jit(solution)/shard_map/ppermute | solution.py:24
  95.5 9.4 %collective-permute-start.17 = (bf16[192,512]{1,0:T(8,128)(2,1)S(1)}, bf16[192,512]{1,0:T(8,128)(2,1)S(1)}, u32[]{:S(2)}, u32[]{:S(2)}) collective-permute-start(bf16[192,512]{1,0:T(8,128)(2,1)S(1)} %pad_maximum_fusion.3.d0.da), channel_id=1, source_target_pairs={{0,4},{2,6},{4,0},{6,2},{1,5},{3,7},{5,1},{7,3},{8,12},{10,14},{12... | collective-permute-start | bytes 589832 | tf_op jit(solution)/shard_map/ppermute | solution.py:24
  97.9 10.2 %collective-permute-start.16 = (bf16[192,512]{1,0:T(8,128)(2,1)S(1)}, bf16[192,512]{1,0:T(8,128)(2,1)S(1)}, u32[]{:S(2)}, u32[]{:S(2)}) collective-permute-start(bf16[192,512]{1,0:T(8,128)(2,1)S(1)} %pad_maximum_fusion.3.d0.da), channel_id=1, source_target_pairs={{0,2},{2,4},{4,6},{6,0},{1,3},{3,5},{5,7},{7,1},{8,10},{10,12},{12... | collective-permute-start | bytes 589832 | tf_op jit(solution)/shard_map/ppermute | solution.py:24
  99.9 8.2 %collective-permute-start.18 = (bf16[192,512]{1,0:T(8,128)(2,1)S(1)}, bf16[192,512]{1,0:T(8,128)(2,1)S(1)}, u32[]{:S(2)}, u32[]{:S(2)}) collective-permute-start(bf16[192,512]{1,0:T(8,128)(2,1)S(1)} %pad_maximum_fusion.3.d0.da), channel_id=1, source_target_pairs={{0,6},{2,0},{4,2},{6,4},{1,7},{3,1},{5,3},{7,5},{8,14},{10,8},{12,... | collective-permute-start | bytes 589832 | tf_op jit(solution)/shard_map/ppermute | solution.py:24
  114.7 18.3 %collective-permute-start.23 = (bf16[192,1792]{1,0:T(8,128)(2,1)S(1)}, bf16[192,1792]{1,0:T(8,128)(2,1)S(1)}, u32[]{:S(2)}, u32[]{:S(2)}) collective-permute-start(bf16[192,1792]{1,0:T(8,128)(2,1)S(1)} %get-tuple-element.135), channel_id=1, source_target_pairs={{0,6},{2,0},{4,2},{6,4},{1,7},{3,1},{5,3},{7,5},{8,14},{10,8},{12,... | collective-permute-start | bytes 2064392 | tf_op jit(solution)/shard_map/ppermute | solution.py:24
  117.7 17.5 %collective-permute-start.24 = (bf16[192,1792]{1,0:T(8,128)(2,1)S(1)}, bf16[192,1792]{1,0:T(8,128)(2,1)S(1)}, u32[]{:S(2)}, u32[]{:S(2)}) collective-permute-start(bf16[192,1792]{1,0:T(8,128)(2,1)S(1)} %get-tuple-element.136), channel_id=1, source_target_pairs={{0,2},{2,4},{4,6},{6,0},{1,3},{3,5},{5,7},{7,1},{8,10},{10,12},{12... | collective-permute-start | bytes 2064392 | tf_op jit(solution)/shard_map/ppermute | solution.py:24
  119.6 18.4 %collective-permute-start.20 = (bf16[128,1792]{1,0:T(8,128)(2,1)S(1)}, bf16[128,1792]{1,0:T(8,128)(2,1)S(1)}, u32[]{:S(2)}, u32[]{:S(2)}) collective-permute-start(bf16[128,1792]{1,0:T(8,128)(2,1)S(1)} %get-tuple-element.132), channel_id=1, source_target_pairs={{0,64},{64,128},{128,192},{192,0},{1,65},{65,129},{129,193},{193,1... | collective-permute-start | bytes 1376264 | tf_op jit(solution)/shard_map/ppermute | solution.py:24
  121.1 23.1 %collective-permute-start.21 = (bf16[128,1792]{1,0:T(8,128)(2,1)S(1)}, bf16[128,1792]{1,0:T(8,128)(2,1)S(1)}, u32[]{:S(2)}, u32[]{:S(2)}) collective-permute-start(bf16[128,1792]{1,0:T(8,128)(2,1)S(1)} %get-tuple-element.133), channel_id=1, source_target_pairs={{0,128},{64,192},{128,0},{192,64},{1,129},{65,193},{129,1},{193,65... | collective-permute-start | bytes 1376264 | tf_op jit(solution)/shard_map/ppermute | solution.py:24
  123.8 20.4 %collective-permute-start.22 = (bf16[128,1792]{1,0:T(8,128)(2,1)S(1)}, bf16[128,1792]{1,0:T(8,128)(2,1)S(1)}, u32[]{:S(2)}, u32[]{:S(2)}) collective-permute-start(bf16[128,1792]{1,0:T(8,128)(2,1)S(1)} %get-tuple-element.134), channel_id=1, source_target_pairs={{0,192},{64,0},{128,64},{192,128},{1,193},{65,1},{129,65},{193,129... | collective-permute-start | bytes 1376264 | tf_op jit(solution)/shard_map/ppermute | solution.py:24
  136.1 18.5 %collective-permute-start.25 = (bf16[192,1792]{1,0:T(8,128)(2,1)}, bf16[192,1792]{1,0:T(8,128)(2,1)}, u32[]{:S(2)}, u32[]{:S(2)}) collective-permute-start(bf16[192,1792]{1,0:T(8,128)(2,1)} %get-tuple-element.138), channel_id=1, source_target_pairs={{0,4},{2,6},{4,0},{6,2},{1,5},{3,7},{5,1},{7,3},{8,12},{10,14},{12... | collective-permute-start | bytes 2064392 | tf_op jit(solution)/shard_map/ppermute | solution.py:24
  154.7 21.9 %all-to-all-start.1 = ((bf16[32,4,1792]{2,1,0:T(4,128)(2,1)}), bf16[32,4,1792]{2,1,0:T(4,128)(2,1)}, u32[]{:S(2)}, u32[]{:S(2)}) async-start(bf16[32,4,1792]{2,1,0:T(4,128)(2,1)} %reshape.227), calls=%async_computation.1 | async-start | bytes 917504 | tf_op jit(solution)/shard_map/all_to_all | solution.py:60
  (12 other events, 77.9 us)

commit v6 on v5

--- a/solution.py
+++ b/solution.py
@@ -40,8 +40,8 @@
     partial, ws = work(first, early, late)
     far, mine = lax.optimization_barrier((far, partial[0]))
     done = ([mine, partial[1]], ws)
-    second = jnp.concatenate([before[2], last[0], last[1], *far], axis=0)
-    return first, done, (second, shift(second, "core", 1))
+    second = (jnp.concatenate([before[2], last[0], last[1]], axis=0), *far)
+    return first, done, (second, tuple(shift(piece, "core", 1) for piece in second))
 
 
 def by_y_and_z(a, z):
@@ -158,8 +158,12 @@
     return jnp.where(column == slot, 1.0, 0.0)
 
 
-def forward_kernel(toks, rows, pick, w0, w1, w2, w3, p0, p1, p2, p3, weight, slot):
+def forward_kernel(toks, pick, w0, w1, w2, w3, *refs):
+    pieces, (p0, p1, p2, p3, weight, slot) = refs[:-6], refs[-6:]
     ws, outs = (w0, w1, w2, w3), (p0, p1, p2, p3)
+    rows = pieces[0]
+    if len(pieces) > 1:
+        rows = jnp.concatenate([piece[...] for piece in pieces], axis=0)
     part, n, slots = w0.shape[1], rows.shape[0], weight.shape[1]
     gu = 2 * w0.shape[0] // 3
     found = mm(rows[:, 2 * part :], pick[...])
@@ -179,18 +183,23 @@
 
 
 def weight_grad_kernel(
-    experts, s0, s1, s2, s3, da, db, r0, r1, r2, r3, oa, ob, x, g, d_gu, d_h, sems
+    experts, s0, s1, s2, s3, da, db, *refs
 ):
+    pieces, (oa, ob, x, g, d_gu, d_h, sems) = refs[:-7], refs[-7:]
     gu = 2 * oa.shape[0] // 3
     slots = da.shape[1] // 4
-    n, part = r0.shape[0], oa.shape[1]
-    copies = [
-        pltpu.make_async_copy(
-            r.at[:, pl.ds(k * part, part)], dst.at[pl.ds(i * n, n)], sems.at[4 * k + i]
-        )
-        for k, dst in enumerate((x, g))
-        for i, r in enumerate((r0, r1, r2, r3))
-    ]
+    n, part = s0.shape[0], oa.shape[1]
+    copies = []
+    for k, dst in enumerate((x, g)):
+        start = 0
+        for r in pieces:
+            at = pl.ds(start, r.shape[0])
+            copies.append(
+                pltpu.make_async_copy(
+                    r.at[:, pl.ds(k * part, part)], dst.at[at], sems.at[len(copies)]
+                )
+            )
+            start += r.shape[0]
     for copy in copies:
         copy.start()
     for i, slot in enumerate((s0, s1, s2, s3)):
@@ -201,12 +210,12 @@
             at = slice(i * n, (i + 1) * n)
             d_gu[j * gu : (j + 1) * gu, at] = spread[:gu]
             d_h[j * gu // 2 : (j + 1) * gu // 2, at] = spread[gu:]
-    for copy in copies[:4]:
+    for copy in copies[: len(pieces)]:
         copy.wait()
     grad = mm(d_gu[...], x[...]).astype(BF)
     oa[:gu] = grad[:gu]
     ob[:gu] = grad[gu:]
-    for copy in copies[4:]:
+    for copy in copies[len(pieces) :]:
         copy.wait()
     grad = mm(d_h[...], g[...]).astype(BF)
     oa[gu:] = grad[: gu // 2]
@@ -214,20 +223,21 @@
 
 
 def weight_grads(experts, slots, groups, delta, part):
-    n, rows = groups[0].shape[0], delta[0].shape[0]
+    n, rows = slots[0].shape[0], delta[0].shape[0]
+    pieces = [piece for group in groups for piece in group]
     gu = 2 * rows // 3
     vmem = pl.BlockSpec(memory_space=pltpu.VMEM)
     return pl.pallas_call(
         functools.partial(weight_grad_kernel, experts),
         out_shape=[jax.ShapeDtypeStruct((rows, part), BF)] * 2,
-        in_specs=[vmem] * 6 + [pl.BlockSpec(memory_space=pl.ANY)] * 4,
+        in_specs=[vmem] * 6 + [pl.BlockSpec(memory_space=pl.ANY)] * len(pieces),
         out_specs=[vmem] * 2,
         scratch_shapes=[
             pltpu.VMEM((4 * n, part), BF),
             pltpu.VMEM((4 * n, part), BF),
             pltpu.VMEM((2 * gu, 4 * n), BF),
             pltpu.VMEM((gu, 4 * n), BF),
-            pltpu.SemaphoreType.DMA((8,)),
+            pltpu.SemaphoreType.DMA((2 * len(pieces),)),
         ],
         compiler_params=pltpu.CompilerParams(vmem_limit_bytes=KERNEL_VMEM),
         cost_estimate=pl.CostEstimate(
@@ -235,7 +245,7 @@
             bytes_accessed=2 * (8 * n * part + 2 * 2 * rows * part),
             transcendentals=0,
         ),
-    )(*slots, *[delta[s] for s in experts], *groups)
+    )(*slots, *[delta[s] for s in experts], *pieces)
 
 
 def input_grad(half, slot, ds, ws):
@@ -344,11 +354,11 @@
 
     def work(rows, early, late):
         ws = (w[0], early[0], late, early[1])
-        return [forward(a, pick, *ws) for a in rows], ws
+        return [forward(pick, *ws, a) for a in rows], ws
 
     first, (partial, w), second = gather_z(own, (w[1], w[3]), shift(w[2], "x", 2), work)
-    partial = partial + [forward(a, pick, *w) for a in second]
-    groups = [first[0], second[0], first[1], second[1]]
+    partial = partial + [forward(pick, *w, *a) for a in second]
+    groups = [(first[0],), second[0], (first[1],), second[1]]
     partial = [partial[i] for i in (0, 2, 1, 3)]
     weight = jnp.concatenate([p[NX] for p in partial], axis=1)
     pre = [shift(jnp.concatenate([p[s] for p in partial], axis=1), "x", -s) for s in range(NX)]

time: 180 us -> 173 us (0.961)
  waiting for transfers between devices: 61.5 us -> 72.3 us
  Pallas kernels: 36.9 us -> 28.7 us
  local copies, waits for them, and re-layouts: 17.2 us -> 9.21 us
    ppermute x26 -> x28, waiting for transfers between devices: 52.5 us -> 63.2 us  [shift(): return lax.ppermute(a, axis, [(i, (i + by) % size) for i in range(size)])]
    unnamed x53 -> x49, local copies, waits for them, and re-layouts: 10.6 us -> 4.24 us
    pallas_call x7, Pallas kernels: 18.4 us -> 12.3 us  [call(): pl.pallas_call(kernel, out_shape=out_shape, in_specs=[smem] * scalars + [...]
    pallas_call x2, Pallas kernels: 9.88 us -> 7.76 us  [weight_grads(): pl.pallas_call(functools.partial(weight_grad_kernel, experts), out_shape=...]
    ppermute x26 -> x28, starting transfers between devices: 41.8 us -> 41.4 us  [shift(): return lax.ppermute(a, axis, [(i, (i + by) % size) for i in range(size)])]
  transfers between devices with their start and end apart: 28 -> 30, of which waited for: 19 -> 20; matrix products, arithmetic and copies ran while one was open for 6% -> 2% of each run, Pallas kernels for 18% -> 15%
where the time goes in v6:
time: 173 us; the launch traced here: 172 us
  waiting for transfers between devices  72.3 us (42%)
  starting transfers between devices  55.4 us (32%)
  Pallas kernels  28.7 us (17%)
  local copies, waits for them, and re-layouts  9.21 us (5%)
  other arithmetic  4.91 us (3%)
    ppermute x28, waiting for transfers between devices, shift(): return lax.ppermute(a, axis, [(i, (i + by) % size) for i in range(size)])  63.2 us
    ppermute x28, starting transfers between devices, shift(): return lax.ppermute(a, axis, [(i, (i + by) % size) for i in range(size)])  41.4 us
    all_to_all x2, starting transfers between devices, exchange(): return lax.all_to_all(a, axes, 0, 0, tiled=True)  14 us
    pallas_call x7, Pallas kernels, call(): pl.pallas_call(kernel, out_shape=out_shape, in_specs=[smem] * scalars + [...  12.3 us
    all_to_all x2, waiting for transfers between devices, exchange(): return lax.all_to_all(a, axes, 0, 0, tiled=True)  9.04 us
    pallas_call x1, Pallas kernels, dequantize(): pl.pallas_call(dequantize_kernel, grid_spec=grid, out_shape=[jax.ShapeDty...  8.56 us
    pallas_call x2, Pallas kernels, weight_grads(): pl.pallas_call(functools.partial(weight_grad_kernel, experts), out_shape=...  7.76 us
    unnamed x49, local copies, waits for them, and re-layouts  4.24 us
  transfers between devices with their start and end apart: 30, of which 20 were waited for; matrix products, arithmetic and copies ran while one was open for 2% of the time, Pallas kernels for 15%

profile of v6, /device:TPU:2, one launch (start us, length us, event | category | flops | bytes accessed | tf_op | source)
XLA Modules:
  0.0 171.7 jit_solution(10905993131894408434)
XLA Ops:
  5.1 7.5 %all-to-all-start = ((bf16[16,4,3712]{2,1,0:T(4,128)(2,1)}), bf16[16,4,3712]{2,1,0:T(4,128)(2,1)S(1)}, u32[]{:S(2)}, u32[]{:S(2)}) async-start(bf16[16,4,3712]{2,1,0:T(4,128)(2,1)} %bitcast.3), calls=%async_computation | async-start | bytes 950272 | tf_op jit(solution)/shard_map/all_to_all | solution.py:60
  12.5 8.6 %shard_map.129 = (bf16[192,1792]{1,0:T(8,128)(2,1)}, bf16[192,1792]{1,0:T(8,128)(2,1)}, bf16[192,1792]{1,0:T(8,128)(2,1)}, bf16[192,1792]{1,0:T(8,128)(2,1)}, bf16[4,192,1792]{2,1,0:T(8,128)(2,1)}) custom-call(s32[1]{0:T(128)} %bitcast.4.x_ref, f32[1,64,7168]{2,1,0:T(8,128)} %gm.1, f32[1,64,7168]{2,1,0:T(8,128)} %um.1, f32[1,64,7168]{2,1,0:T(8,128)} %dm.1, ...), custom_call_target="tpu_custom_call" | custom-call | flops 41287680 | bytes 11010048 | tf_op jit(solution)/shard_map/pallas_call | solution.py:126
  22.3 5.9 %collective-permute-start = (bf16[64,3712]{1,0:T(8,128)(2,1)S(1)}, bf16[64,3712]{1,0:T(8,128)(2,1)S(1)}, u32[]{:S(2)}, u32[]{:S(2)}) collective-permute-start(bf16[64,3712]{1,0:T(8,128)(2,1)S(1)} %reshape.223), channel_id=1, source_target_pairs={{0,56},{8,0},{16,8},{24,16},{32,24},{40,32},{48,40},{56,48},{1,57}... | collective-permute-start | bytes 1425416 | tf_op jit(solution)/shard_map/ppermute | solution.py:24
  30.3 6.9 %collective-permute-done = bf16[64,3712]{1,0:T(8,128)(2,1)S(1)} collective-permute-done((bf16[64,3712]{1,0:T(8,128)(2,1)S(1)}, bf16[64,3712]{1,0:T(8,128)(2,1)S(1)}, u32[]{:S(2)}, u32[]{:S(2)}) %collective-permute-start) | collective-permute-done | bytes 475168 | tf_op jit(solution)/shard_map/ppermute | solution.py:24
  37.1 3.7 %collective-permute-start.1 = (bf16[64,3712]{1,0:T(8,128)(2,1)S(1)}, bf16[64,3712]{1,0:T(8,128)(2,1)S(1)}, u32[]{:S(2)}, u32[]{:S(2)}) collective-permute-start(bf16[64,3712]{1,0:T(8,128)(2,1)S(1)} %collective-permute-done), channel_id=1, source_target_pairs={{0,56},{8,0},{16,8},{24,16},{32,24},{40,32},{48,40},{56,48},{1,57}... | collective-permute-start | bytes 1425416 | tf_op jit(solution)/shard_map/ppermute | solution.py:24
  40.9 3.2 %collective-permute-done.4.w1 = bf16[192,1792]{1,0:T(8,128)(2,1)S(1)} collective-permute-done((bf16[192,1792]{1,0:T(8,128)(2,1)}, bf16[192,1792]{1,0:T(8,128)(2,1)S(1)}, u32[]{:S(2)}, u32[]{:S(2)}) %collective-permute-start.4) | collective-permute-done | bytes 688160 | tf_op jit(solution)/shard_map/ppermute | solution.py:24
  44.9 3.7 %collective-permute-start.8 = (bf16[192,1792]{1,0:T(8,128)(2,1)S(1)}, bf16[192,1792]{1,0:T(8,128)(2,1)S(1)}, u32[]{:S(2)}, u32[]{:S(2)}) collective-permute-start(bf16[192,1792]{1,0:T(8,128)(2,1)S(1)} %copy-done.6), channel_id=1, source_target_pairs={{0,4},{2,6},{4,0},{6,2},{1,5},{3,7},{5,1},{7,3},{8,12},{10,14},{12... | collective-permute-start | bytes 2064392 | tf_op jit(solution)/shard_map/ppermute | solution.py:24
  48.8 3.4 %collective-permute-done.3 = bf16[64,3712]{1,0:T(8,128)(2,1)S(1)} collective-permute-done((bf16[64,3712]{1,0:T(8,128)(2,1)S(1)}, bf16[64,3712]{1,0:T(8,128)(2,1)S(1)}, u32[]{:S(2)}, u32[]{:S(2)}) %collective-permute-start.3) | collective-permute-done | bytes 475168 | tf_op jit(solution)/shard_map/ppermute | solution.py:24
  54.5 7.0 %collective-permute-done.8.w2 = bf16[192,1792]{1,0:T(8,128)(2,1)S(1)} collective-permute-done((bf16[192,1792]{1,0:T(8,128)(2,1)S(1)}, bf16[192,1792]{1,0:T(8,128)(2,1)S(1)}, u32[]{:S(2)}, u32[]{:S(2)}) %collective-permute-start.8) | collective-permute-done | bytes 688160 | tf_op jit(solution)/shard_map/ppermute | solution.py:24
  63.7 3.0 %collective-permute-start.9 = (bf16[32,3712]{1,0:T(8,128)(2,1)S(1)}, bf16[32,3712]{1,0:T(8,128)(2,1)S(1)}, u32[]{:S(2)}, u32[]{:S(2)}) collective-permute-start(bf16[32,3712]{1,0:T(8,128)(2,1)S(1)} %slice.135), channel_id=1, source_target_pairs={{0,56},{8,0},{16,8},{24,16},{32,24},{40,32},{48,40},{56,48},{1,57}... | collective-permute-start | bytes 712712 | tf_op jit(solution)/shard_map/ppermute | solution.py:24
  68.0 4.8 %collective-permute-done.10.refs_2_.refs_3_ = bf16[32,3712]{1,0:T(8,128)(2,1)S(1)} collective-permute-done((bf16[32,3712]{1,0:T(8,128)(2,1)S(1)}, bf16[32,3712]{1,0:T(8,128)(2,1)S(1)}, u32[]{:S(2)}, u32[]{:S(2)}) %collective-permute-start.10) | collective-permute-done | bytes 237600 | tf_op jit(solution)/shard_map/ppermute | solution.py:24
  84.5 5.4 %collective-permute-done.16 = bf16[192,512]{1,0:T(8,128)(2,1)S(1)} collective-permute-done((bf16[192,512]{1,0:T(8,128)(2,1)S(1)}, bf16[192,512]{1,0:T(8,128)(2,1)S(1)}, u32[]{:S(2)}, u32[]{:S(2)}) %collective-permute-start.16) | collective-permute-done | bytes 196640 | tf_op jit(solution)/shard_map/ppermute | solution.py:24
  95.4 4.4 %collective-permute-done.19.d2.db = bf16[192,512]{1,0:T(8,128)(2,1)S(1)} collective-permute-done((bf16[192,512]{1,0:T(8,128)(2,1)S(1)}, bf16[192,512]{1,0:T(8,128)(2,1)S(1)}, u32[]{:S(2)}, u32[]{:S(2)}) %collective-permute-start.19) | collective-permute-done | bytes 196640 | tf_op jit(solution)/shard_map/ppermute | solution.py:24
  99.8 3.8 %collective-permute-done.18.d1.da = bf16[192,512]{1,0:T(8,128)(2,1)S(1)} collective-permute-done((bf16[192,512]{1,0:T(8,128)(2,1)S(1)}, bf16[192,512]{1,0:T(8,128)(2,1)S(1)}, u32[]{:S(2)}, u32[]{:S(2)}) %collective-permute-start.18) | collective-permute-done | bytes 196640 | tf_op jit(solution)/shard_map/ppermute | solution.py:24
  105.6 3.5 %shard_map.135 = (bf16[192,1792]{1,0:T(8,128)(2,1)S(1)}, bf16[192,1792]{1,0:T(8,128)(2,1)S(1)}) custom-call(s32[256,128]{1,0:T(8,128)S(1)} %get-tuple-element.102.s0, s32[256,128]{1,0:T(8,128)S(1)} %get-tuple-element.105.s1, s32[256,128]{1,0:T(8,128)S(1)} %get-tuple-element.126.s2, s32[256,128]{1,0:T(8,128)S(1)} %get-tuple-element.127.s3, ...), custom_call_target="tpu_custom_call" | custom-call | flops 1409286144 | bytes 10092544 | tf_op jit(solution)/shard_map/pallas_call | solution.py:230
  109.2 2.9 %collective-permute-start.25 = (bf16[192,1792]{1,0:T(8,128)(2,1)S(1)}, bf16[192,1792]{1,0:T(8,128)(2,1)S(1)}, u32[]{:S(2)}, u32[]{:S(2)}) collective-permute-start(bf16[192,1792]{1,0:T(8,128)(2,1)S(1)} %get-tuple-element.135), channel_id=1, source_target_pairs={{0,6},{2,0},{4,2},{6,4},{1,7},{3,1},{5,3},{7,5},{8,14},{10,8},{12,... | collective-permute-start | bytes 2064392 | tf_op jit(solution)/shard_map/ppermute | solution.py:24
  115.5 2.7 %collective-permute-start.23 = (bf16[128,1792]{1,0:T(8,128)(2,1)S(1)}, bf16[128,1792]{1,0:T(8,128)(2,1)S(1)}, u32[]{:S(2)}, u32[]{:S(2)}) collective-permute-start(bf16[128,1792]{1,0:T(8,128)(2,1)S(1)} %get-tuple-element.133), channel_id=1, source_target_pairs={{0,128},{64,192},{128,0},{192,64},{1,129},{65,193},{129,1},{193,65... | collective-permute-start | bytes 1376264 | tf_op jit(solution)/shard_map/ppermute | solution.py:24
  119.6 4.3 %shard_map.137 = (bf16[192,1792]{1,0:T(8,128)(2,1)S(1)}, bf16[192,1792]{1,0:T(8,128)(2,1)}) custom-call(s32[256,128]{1,0:T(8,128)S(1)} %get-tuple-element.102.s0, s32[256,128]{1,0:T(8,128)S(1)} %get-tuple-element.105.s1, s32[256,128]{1,0:T(8,128)S(1)} %get-tuple-element.126.s2, s32[256,128]{1,0:T(8,128)S(1)} %get-tuple-element.127.s3, ...), custom_call_target="tpu_custom_call" | custom-call | flops 1409286144 | bytes 10092544 | tf_op jit(solution)/shard_map/pallas_call | solution.py:230
  124.8 2.7 %collective-permute-done.25.r1 = bf16[192,1792]{1,0:T(8,128)(2,1)S(1)} collective-permute-done((bf16[192,1792]{1,0:T(8,128)(2,1)S(1)}, bf16[192,1792]{1,0:T(8,128)(2,1)S(1)}, u32[]{:S(2)}, u32[]{:S(2)}) %collective-permute-start.25) | collective-permute-done | bytes 688160 | tf_op jit(solution)/shard_map/ppermute | solution.py:24
  131.4 7.2 %collective-permute-done.23 = bf16[128,1792]{1,0:T(8,128)(2,1)S(1)} collective-permute-done((bf16[128,1792]{1,0:T(8,128)(2,1)S(1)}, bf16[128,1792]{1,0:T(8,128)(2,1)S(1)}, u32[]{:S(2)}, u32[]{:S(2)}) %collective-permute-start.23) | collective-permute-done | bytes 458784 | tf_op jit(solution)/shard_map/ppermute | solution.py:24
  141.5 7.5 %collective-permute-done.27.r2 = bf16[192,1792]{1,0:T(8,128)(2,1)} collective-permute-done((bf16[192,1792]{1,0:T(8,128)(2,1)}, bf16[192,1792]{1,0:T(8,128)(2,1)}, u32[]{:S(2)}, u32[]{:S(2)}) %collective-permute-start.27) | collective-permute-done | bytes 688160 | tf_op jit(solution)/shard_map/ppermute | solution.py:24
  149.0 6.5 %all-to-all-start.1 = ((bf16[32,4,1792]{2,1,0:T(4,128)(2,1)}), bf16[32,4,1792]{2,1,0:T(4,128)(2,1)}, u32[]{:S(2)}, u32[]{:S(2)}) async-start(bf16[32,4,1792]{2,1,0:T(4,128)(2,1)} %reshape.227), calls=%async_computation.1 | async-start | bytes 917504 | tf_op jit(solution)/shard_map/all_to_all | solution.py:60
  157.8 4.2 %shard_map.138 = (f32[1,64,7168]{2,1,0:T(8,128)}, f32[1,64,7168]{2,1,0:T(8,128)}, f32[1,64,7168]{2,1,0:T(8,128)}) custom-call(s32[1]{0:T(128)} %bitcast.4.x_ref, bf16[192,1792]{1,0:T(8,128)(2,1)S(1)} %copy-done.5, bf16[192,1792]{1,0:T(8,128)(2,1)S(1)} %collective-permute-done.25.r1, bf16[192,1792]{1,0:T(8,128)(2,1)} %collective-permute-done.27.r2, ...), custom_call_target="tpu_custom_call" | custom-call | flops 4128768 | bytes 11010048 | tf_op jit(solution)/shard_map/pallas_call | solution.py:282
  162.0 8.0 %all-to-all-done.1 = bf16[32,4,1792]{2,1,0:T(4,128)(2,1)} async-done(((bf16[32,4,1792]{2,1,0:T(4,128)(2,1)}), bf16[32,4,1792]{2,1,0:T(4,128)(2,1)}, u32[]{:S(2)}, u32[]{:S(2)}) %all-to-all-start.1) | async-done | bytes 458784 | tf_op jit(solution)/shard_map/all_to_all | solution.py:60
  (140 shorter events, 49.8 us)
Async XLA Ops:
  5.1 17.1 %all-to-all-start = ((bf16[16,4,3712]{2,1,0:T(4,128)(2,1)}), bf16[16,4,3712]{2,1,0:T(4,128)(2,1)S(1)}, u32[]{:S(2)}, u32[]{:S(2)}) async-start(bf16[16,4,3712]{2,1,0:T(4,128)(2,1)} %bitcast.3), calls=%async_computation | async-start | bytes 950272 | tf_op jit(solution)/shard_map/all_to_all | solution.py:60
  22.3 14.9 %collective-permute-start = (bf16[64,3712]{1,0:T(8,128)(2,1)S(1)}, bf16[64,3712]{1,0:T(8,128)(2,1)S(1)}, u32[]{:S(2)}, u32[]{:S(2)}) collective-permute-start(bf16[64,3712]{1,0:T(8,128)(2,1)S(1)} %reshape.223), channel_id=1, source_target_pairs={{0,56},{8,0},{16,8},{24,16},{32,24},{40,32},{48,40},{56,48},{1,57}... | collective-permute-start | bytes 1425416 | tf_op jit(solution)/shard_map/ppermute | solution.py:24
  28.2 12.6 %collective-permute-start.2 = (bf16[64,3712]{1,0:T(8,128)(2,1)S(1)}, bf16[64,3712]{1,0:T(8,128)(2,1)S(1)}, u32[]{:S(2)}, u32[]{:S(2)}) collective-permute-start(bf16[64,3712]{1,0:T(8,128)(2,1)S(1)} %reshape.223), channel_id=1, source_target_pairs={{0,8},{8,16},{16,24},{24,32},{32,40},{40,48},{48,56},{56,0},{1,9},... | collective-permute-start | bytes 1425416 | tf_op jit(solution)/shard_map/ppermute | solution.py:24
  28.2 15.9 %collective-permute-start.4 = (bf16[192,1792]{1,0:T(8,128)(2,1)}, bf16[192,1792]{1,0:T(8,128)(2,1)S(1)}, u32[]{:S(2)}, u32[]{:S(2)}) collective-permute-start(bf16[192,1792]{1,0:T(8,128)(2,1)} %get-tuple-element.82), channel_id=1, source_target_pairs={{0,2},{2,4},{4,6},{6,0},{1,3},{3,5},{5,7},{7,1},{8,10},{10,12},{12... | collective-permute-start | bytes 2064392 | tf_op jit(solution)/shard_map/ppermute | solution.py:24
  28.6 16.3 %collective-permute-start.5 = (bf16[192,1792]{1,0:T(8,128)(2,1)}, bf16[192,1792]{1,0:T(8,128)(2,1)S(1)}, u32[]{:S(2)}, u32[]{:S(2)}) collective-permute-start(bf16[192,1792]{1,0:T(8,128)(2,1)} %get-tuple-element.84), channel_id=1, source_target_pairs={{0,6},{2,0},{4,2},{6,4},{1,7},{3,1},{5,3},{7,5},{8,14},{10,8},{12,... | collective-permute-start | bytes 2064392 | tf_op jit(solution)/shard_map/ppermute | solution.py:24
  37.1 11.7 %collective-permute-start.1 = (bf16[64,3712]{1,0:T(8,128)(2,1)S(1)}, bf16[64,3712]{1,0:T(8,128)(2,1)S(1)}, u32[]{:S(2)}, u32[]{:S(2)}) collective-permute-start(bf16[64,3712]{1,0:T(8,128)(2,1)S(1)} %collective-permute-done), channel_id=1, source_target_pairs={{0,56},{8,0},{16,8},{24,16},{32,24},{40,32},{48,40},{56,48},{1,57}... | collective-permute-start | bytes 1425416 | tf_op jit(solution)/shard_map/ppermute | solution.py:24
  40.8 11.4 %collective-permute-start.3 = (bf16[64,3712]{1,0:T(8,128)(2,1)S(1)}, bf16[64,3712]{1,0:T(8,128)(2,1)S(1)}, u32[]{:S(2)}, u32[]{:S(2)}) collective-permute-start(bf16[64,3712]{1,0:T(8,128)(2,1)S(1)} %collective-permute-done.2), channel_id=1, source_target_pairs={{0,8},{8,16},{16,24},{24,32},{32,40},{40,48},{48,56},{56,0},{1,9},... | collective-permute-start | bytes 1425416 | tf_op jit(solution)/shard_map/ppermute | solution.py:24
  44.9 16.6 %collective-permute-start.8 = (bf16[192,1792]{1,0:T(8,128)(2,1)S(1)}, bf16[192,1792]{1,0:T(8,128)(2,1)S(1)}, u32[]{:S(2)}, u32[]{:S(2)}) collective-permute-start(bf16[192,1792]{1,0:T(8,128)(2,1)S(1)} %copy-done.6), channel_id=1, source_target_pairs={{0,4},{2,6},{4,0},{6,2},{1,5},{3,7},{5,1},{7,3},{8,12},{10,14},{12... | collective-permute-start | bytes 2064392 | tf_op jit(solution)/shard_map/ppermute | solution.py:24
  52.3 9.3 %collective-permute-start.6 = (bf16[64,3712]{1,0:T(8,128)(2,1)S(1)}, bf16[64,3712]{1,0:T(8,128)(2,1)S(1)}, u32[]{:S(2)}, u32[]{:S(2)}) collective-permute-start(bf16[64,3712]{1,0:T(8,128)(2,1)S(1)} %collective-permute-done.1), channel_id=1, source_target_pairs={{0,56},{8,0},{16,8},{24,16},{32,24},{40,32},{48,40},{56,48},{1,57}... | collective-permute-start | bytes 1425416 | tf_op jit(solution)/shard_map/ppermute | solution.py:24
  52.5 10.5 %collective-permute-start.7 = (bf16[64,3712]{1,0:T(8,128)(2,1)S(1)}, bf16[64,3712]{1,0:T(8,128)(2,1)S(1)}, u32[]{:S(2)}, u32[]{:S(2)}) collective-permute-start(bf16[64,3712]{1,0:T(8,128)(2,1)S(1)} %collective-permute-done.3), channel_id=1, source_target_pairs={{0,8},{8,16},{16,24},{24,32},{32,40},{40,48},{48,56},{56,0},{1,9},... | collective-permute-start | bytes 1425416 | tf_op jit(solution)/shard_map/ppermute | solution.py:24
  54.3 20.3 %collective-permute-start.11 = (bf16[256,3712]{1,0:T(8,128)(2,1)S(1)}, bf16[256,3712]{1,0:T(8,128)(2,1)S(1)}, u32[]{:S(2)}, u32[]{:S(2)}) collective-permute-start(bf16[256,3712]{1,0:T(8,128)(2,1)S(1)} %constant_dynamic-update-slice_fusion.refs_0_), channel_id=1, source_target_pairs={{0,1},{1,0},{2,3},{3,2},{4,5},{5,4},{6,7},{7,6},{8,9},{9,8},{10,11... | collective-permute-start | bytes 5701640 | tf_op jit(solution)/shard_map/ppermute | solution.py:24
  63.1 12.7 %collective-permute-start.12 = (bf16[192,3712]{1,0:T(8,128)(2,1)S(1)}, bf16[192,3712]{1,0:T(8,128)(2,1)S(1)}, u32[]{:S(2)}, u32[]{:S(2)}) collective-permute-start(bf16[192,3712]{1,0:T(8,128)(2,1)S(1)} %constant_dynamic-update-slice_fusion.4.refs_0_.refs_1_), channel_id=1, source_target_pairs={{0,1},{1,0},{2,3},{3,2},{4,5},{5,4},{6,7},{7,6},{8,9},{9,8},{10,11... | collective-permute-start | bytes 4276232 | tf_op jit(solution)/shard_map/ppermute | solution.py:24
  63.3 9.5 %collective-permute-start.10 = (bf16[32,3712]{1,0:T(8,128)(2,1)S(1)}, bf16[32,3712]{1,0:T(8,128)(2,1)S(1)}, u32[]{:S(2)}, u32[]{:S(2)}) collective-permute-start(bf16[32,3712]{1,0:T(8,128)(2,1)S(1)} %slice.136), channel_id=1, source_target_pairs={{0,8},{8,16},{16,24},{24,32},{32,40},{40,48},{48,56},{56,0},{1,9},... | collective-permute-start | bytes 712712 | tf_op jit(solution)/shard_map/ppermute | solution.py:24
  63.7 9.1 %collective-permute-start.9 = (bf16[32,3712]{1,0:T(8,128)(2,1)S(1)}, bf16[32,3712]{1,0:T(8,128)(2,1)S(1)}, u32[]{:S(2)}, u32[]{:S(2)}) collective-permute-start(bf16[32,3712]{1,0:T(8,128)(2,1)S(1)} %slice.135), channel_id=1, source_target_pairs={{0,56},{8,0},{16,8},{24,16},{32,24},{40,32},{48,40},{56,48},{1,57}... | collective-permute-start | bytes 712712 | tf_op jit(solution)/shard_map/ppermute | solution.py:24
  78.6 11.3 %collective-permute-start.16 = (bf16[192,512]{1,0:T(8,128)(2,1)S(1)}, bf16[192,512]{1,0:T(8,128)(2,1)S(1)}, u32[]{:S(2)}, u32[]{:S(2)}) collective-permute-start(bf16[192,512]{1,0:T(8,128)(2,1)S(1)} %pad_maximum_fusion.1), channel_id=1, source_target_pairs={{0,4},{2,6},{4,0},{6,2},{1,5},{3,7},{5,1},{7,3},{8,12},{10,14},{12... | collective-permute-start | bytes 589832 | tf_op jit(solution)/shard_map/ppermute | solution.py:24
  81.1 9.6 %collective-permute-start.17 = (bf16[192,512]{1,0:T(8,128)(2,1)S(1)}, bf16[192,512]{1,0:T(8,128)(2,1)S(1)}, u32[]{:S(2)}, u32[]{:S(2)}) collective-permute-start(bf16[192,512]{1,0:T(8,128)(2,1)S(1)} %pad_maximum_fusion.2), channel_id=1, source_target_pairs={{0,2},{2,4},{4,6},{6,0},{1,3},{3,5},{5,7},{7,1},{8,10},{10,12},{12... | collective-permute-start | bytes 589832 | tf_op jit(solution)/shard_map/ppermute | solution.py:24
  93.4 10.2 %collective-permute-start.18 = (bf16[192,512]{1,0:T(8,128)(2,1)S(1)}, bf16[192,512]{1,0:T(8,128)(2,1)S(1)}, u32[]{:S(2)}, u32[]{:S(2)}) collective-permute-start(bf16[192,512]{1,0:T(8,128)(2,1)S(1)} %pad_maximum_fusion.3.d0.da), channel_id=1, source_target_pairs={{0,2},{2,4},{4,6},{6,0},{1,3},{3,5},{5,7},{7,1},{8,10},{10,12},{12... | collective-permute-start | bytes 589832 | tf_op jit(solution)/shard_map/ppermute | solution.py:24
  109.2 18.2 %collective-permute-start.25 = (bf16[192,1792]{1,0:T(8,128)(2,1)S(1)}, bf16[192,1792]{1,0:T(8,128)(2,1)S(1)}, u32[]{:S(2)}, u32[]{:S(2)}) collective-permute-start(bf16[192,1792]{1,0:T(8,128)(2,1)S(1)} %get-tuple-element.135), channel_id=1, source_target_pairs={{0,6},{2,0},{4,2},{6,4},{1,7},{3,1},{5,3},{7,5},{8,14},{10,8},{12,... | collective-permute-start | bytes 2064392 | tf_op jit(solution)/shard_map/ppermute | solution.py:24
  112.1 17.5 %collective-permute-start.26 = (bf16[192,1792]{1,0:T(8,128)(2,1)S(1)}, bf16[192,1792]{1,0:T(8,128)(2,1)S(1)}, u32[]{:S(2)}, u32[]{:S(2)}) collective-permute-start(bf16[192,1792]{1,0:T(8,128)(2,1)S(1)} %get-tuple-element.136), channel_id=1, source_target_pairs={{0,2},{2,4},{4,6},{6,0},{1,3},{3,5},{5,7},{7,1},{8,10},{10,12},{12... | collective-permute-start | bytes 2064392 | tf_op jit(solution)/shard_map/ppermute | solution.py:24
  113.9 17.5 %collective-permute-start.22 = (bf16[128,1792]{1,0:T(8,128)(2,1)S(1)}, bf16[128,1792]{1,0:T(8,128)(2,1)S(1)}, u32[]{:S(2)}, u32[]{:S(2)}) collective-permute-start(bf16[128,1792]{1,0:T(8,128)(2,1)S(1)} %get-tuple-element.132), channel_id=1, source_target_pairs={{0,64},{64,128},{128,192},{192,0},{1,65},{65,129},{129,193},{193,1... | collective-permute-start | bytes 1376264 | tf_op jit(solution)/shard_map/ppermute | solution.py:24
  115.5 23.1 %collective-permute-start.23 = (bf16[128,1792]{1,0:T(8,128)(2,1)S(1)}, bf16[128,1792]{1,0:T(8,128)(2,1)S(1)}, u32[]{:S(2)}, u32[]{:S(2)}) collective-permute-start(bf16[128,1792]{1,0:T(8,128)(2,1)S(1)} %get-tuple-element.133), channel_id=1, source_target_pairs={{0,128},{64,192},{128,0},{192,64},{1,129},{65,193},{129,1},{193,65... | collective-permute-start | bytes 1376264 | tf_op jit(solution)/shard_map/ppermute | solution.py:24
  118.2 20.4 %collective-permute-start.24 = (bf16[128,1792]{1,0:T(8,128)(2,1)S(1)}, bf16[128,1792]{1,0:T(8,128)(2,1)S(1)}, u32[]{:S(2)}, u32[]{:S(2)}) collective-permute-start(bf16[128,1792]{1,0:T(8,128)(2,1)S(1)} %get-tuple-element.134), channel_id=1, source_target_pairs={{0,192},{64,0},{128,64},{192,128},{1,193},{65,1},{129,65},{193,129... | collective-permute-start | bytes 1376264 | tf_op jit(solution)/shard_map/ppermute | solution.py:24
  130.5 18.5 %collective-permute-start.27 = (bf16[192,1792]{1,0:T(8,128)(2,1)}, bf16[192,1792]{1,0:T(8,128)(2,1)}, u32[]{:S(2)}, u32[]{:S(2)}) collective-permute-start(bf16[192,1792]{1,0:T(8,128)(2,1)} %get-tuple-element.138), channel_id=1, source_target_pairs={{0,4},{2,6},{4,0},{6,2},{1,5},{3,7},{5,1},{7,3},{8,12},{10,14},{12... | collective-permute-start | bytes 2064392 | tf_op jit(solution)/shard_map/ppermute | solution.py:24
  149.0 21.0 %all-to-all-start.1 = ((bf16[32,4,1792]{2,1,0:T(4,128)(2,1)}), bf16[32,4,1792]{2,1,0:T(4,128)(2,1)}, u32[]{:S(2)}, u32[]{:S(2)}) async-start(bf16[32,4,1792]{2,1,0:T(4,128)(2,1)} %reshape.227), calls=%async_computation.1 | async-start | bytes 917504 | tf_op jit(solution)/shard_map/all_to_all | solution.py:60
  (13 other events, 91.7 us)
